TPU v7x, 32 devices: a whole 2x2x4 slice. The times are simulated.
32 devices in a mesh: dp: 8 (over y, x, core), tensor: 4 (over z).
Axes of the slice: x: 2, y: 2, z: 4, core: 2. Of those that a mesh axis runs over, the one named last changes fastest.
Arguments:
- inputs: float32 [2, 8, 2048, 512], P(None, 'dp', 'tensor'), may hold values from -6 to 6
- memory: float32 [2, 8, 256, 512], P(None, 'dp', 'tensor'), may hold values from -6 to 6
- lengths: int32 [2, 8, 13], P(None, 'dp'), may hold values from 32 to 1664, as said below
- parent: int32 [2, 8, 13], P(None, 'dp'), may hold values from 0 to 4, as said below
- self_qkv: float32 [3, 512, 512], P(None, 'dp', 'tensor'), may hold values from -0.25 to 0.25
- self_out: float32 [512, 512], P('tensor', 'dp'), may hold values from -1 to 1
- cross_q: float32 [512, 512], P('dp', 'tensor'), may hold values from -0.25 to 0.25
- cross_kv: float32 [2, 512, 512], P(None, 'dp', 'tensor'), may hold values from -0.25 to 0.25
- cross_out: float32 [512, 512], P('tensor', 'dp'), may hold values from -1 to 1
- ff_in: float32 [512, 2048], P('dp', 'tensor'), may hold values from -0.25 to 0.25
- ff_bias_in: float32 [2048], P('tensor'), may hold values from -3 to 3
- ff_out: float32 [2048, 512], P('tensor', 'dp'), may hold values from -0.125 to 0.125
- ff_bias_out: float32 [512], replicated, may hold values from -3 to 3
- cotangent: float32 [2, 8, 2048, 512], P(None, 'dp', 'tensor'), may hold values from -6 to 6
Outputs:
- output: float32 [2, 8, 2048, 512], P(None, 'dp', 'tensor')
- grad_inputs: float32 [2, 8, 2048, 512], P(None, 'dp', 'tensor')
- grad_memory: float32 [2, 8, 256, 512], P(None, 'dp', 'tensor')
- grad_self_qkv: float32 [3, 512, 512], P(None, 'dp', 'tensor')
- grad_self_out: float32 [512, 512], P('tensor', 'dp')
- grad_cross_q: float32 [512, 512], P('dp', 'tensor')
- grad_cross_kv: float32 [2, 512, 512], P(None, 'dp', 'tensor')
- grad_cross_out: float32 [512, 512], P('tensor', 'dp')
- grad_ff_in: float32 [512, 2048], P('dp', 'tensor')
- grad_ff_bias_in: float32 [2048], P('tensor')
- grad_ff_out: float32 [2048, 512], P('tensor', 'dp')
- grad_ff_bias_out: float32 [512], replicated
Inputs may be any that keep to these rules, and one draw needn't show every extreme that they name: Each tree's 13 lengths sum to 2048; entry 0 is the trunk; entries 1 to 12 lie between 32 and 128, and one of them equals 32 in every tree; in some tree all of entries 1 to 12 equal 32. `parent`: entry 0 (the trunk) and entries 1 to 4 (the branches) are 0; entries 5 to 12 (the leaves) each name a branch, 1 to 4, and every branch is named by some leaf.
All inputs are finite; a program needn't handle non-finite values.
Results may differ from a plain program's by a relative error of at most 0.0003.
Values sent between devices are 32-bit elements; how exact they have to be, the bound alone decides.
No kernel may reach another device: no remote copies, remote signals or barrier semaphores. Data moves between devices by JAX's collectives and lax.ppermute only.
A program may use at most 384 MiB of HBM per device.

v0:
```python
import jax
import jax.numpy as jnp
from jax import lax
from jax.sharding import PartitionSpec as P

HEAD = 64


HIGH = lax.Precision.HIGHEST
NEG = -1e30
ROOT_HALF = 0.7071067811865476
NORMAL_PEAK = 0.3989422804014327


def product(left, right):
    return jnp.dot(left, right, precision=HIGH)


def inner_prod(left, right):
    return jnp.einsum("rk,rn->kn", left, right, precision=HIGH)


def outer_prod(left, right):
    return jnp.einsum("rk,nk->rn", left, right, precision=HIGH)


def smooth_grad(values):
    return 0.5 * (1.0 + lax.erf(values * ROOT_HALF)) + values * NORMAL_PEAK * jnp.exp(
        -0.5 * values * values
    )


def widen_rows(rows):
    return lax.all_gather(rows, "tensor", axis=0, tiled=True)


def narrow(terms):
    return lax.psum_scatter(terms, "tensor", scatter_dimension=0, tiled=True)


def tree_paths(tree_lengths, tree_parent, row_count):
    ends = jnp.cumsum(tree_lengths)
    places = jnp.arange(row_count, dtype=jnp.int32)
    segment = jnp.sum((places[:, None] >= ends[None, :-1]).astype(jnp.int32), axis=1)
    labels = jnp.arange(tree_lengths.shape[0], dtype=jnp.int32)
    first_up = jnp.sum(
        jnp.where(segment[:, None] == labels[None, :], tree_parent[None, :], 0), axis=1
    )
    second_up = jnp.sum(
        jnp.where(first_up[:, None] == labels[None, :], tree_parent[None, :], 0), axis=1
    )
    return (segment, first_up, second_up)


def allowed(path_info, row_start, block_rows, last_key):
    segment, first_up, second_up = path_info
    row_seg = lax.dynamic_slice_in_dim(segment, row_start, block_rows)
    row_first = lax.dynamic_slice_in_dim(first_up, row_start, block_rows)
    row_second = lax.dynamic_slice_in_dim(second_up, row_start, block_rows)
    key_seg = segment[:last_key]
    row_place = row_start + jnp.arange(block_rows, dtype=jnp.int32)
    key_place = jnp.arange(last_key, dtype=jnp.int32)
    same_seg = (row_seg[:, None] == key_seg[None, :]) & (row_place[:, None] >= key_place[None, :])
    ancestor = (row_seg[:, None] > 0) & (
        (key_seg[None, :] == row_first[:, None]) | (key_seg[None, :] == row_second[:, None])
    )
    return same_seg | ancestor


def block_scores(queries, keys, path_info, first_row, block_rows, last_key, col_start, row_offset):
    scores = outer_prod(
        queries[first_row : first_row + block_rows, col_start : col_start + HEAD],
        keys[:last_key, col_start : col_start + HEAD],
    ) * HEAD ** (-0.5)
    if path_info is not None:
        scores = jnp.where(
            allowed(path_info, row_offset + first_row, block_rows, last_key), scores, NEG
        )
    return scores


def key_limit(keys, path_info, first_row, block_rows):
    if path_info is not None:
        return first_row + block_rows
    return keys.shape[0]


def attend(queries, keys, values, path_info, row_offset):
    row_count = queries.shape[0]
    block_rows = min(512, row_count)
    local_heads = queries.shape[1] // HEAD
    out_blocks, sum_blocks = ([], [])
    for first_row in range(0, row_count, block_rows):
        last_key = key_limit(keys, path_info, first_row, block_rows)
        head_outs, head_sums = ([], [])
        for head_idx in range(local_heads):
            col_start = head_idx * HEAD
            scores = block_scores(
                queries, keys, path_info, first_row, block_rows, last_key, col_start, row_offset
            )
            row_max = jnp.max(scores, axis=1, keepdims=True)
            weights_exp = jnp.exp(scores - row_max)
            row_total = jnp.sum(weights_exp, axis=1, keepdims=True)
            head_outs.append(
                product(weights_exp, values[:last_key, col_start : col_start + HEAD]) / row_total
            )
            head_sums.append(row_max + jnp.log(row_total))
        out_blocks.append(jnp.concatenate(head_outs, axis=1))
        sum_blocks.append(jnp.concatenate(head_sums, axis=1))
    return (jnp.concatenate(out_blocks, axis=0), jnp.concatenate(sum_blocks, axis=0))


def attend_back(queries, keys, values, outputs, log_sums, grad_out, path_info, row_offset):
    row_count = queries.shape[0]
    block_rows = min(512, row_count)
    local_heads = queries.shape[1] // HEAD
    scale = HEAD ** (-0.5)
    grad_keys = jnp.zeros_like(keys)
    grad_values = jnp.zeros_like(values)
    query_blocks = []
    for first_row in range(0, row_count, block_rows):
        last_key = key_limit(keys, path_info, first_row, block_rows)
        row_end = first_row + block_rows
        query_parts, key_parts, value_parts = ([], [], [])
        for head_idx in range(local_heads):
            col_start = head_idx * HEAD
            col_end = col_start + HEAD
            scores = block_scores(
                queries, keys, path_info, first_row, block_rows, last_key, col_start, row_offset
            )
            probs = jnp.exp(scores - log_sums[first_row:row_end, head_idx : head_idx + 1])
            grad_head = grad_out[first_row:row_end, col_start:col_end]
            delta = jnp.sum(
                grad_head * outputs[first_row:row_end, col_start:col_end], axis=1, keepdims=True
            )
            grad_scores = (
                probs
                * (outer_prod(grad_head, values[:last_key, col_start:col_end]) - delta)
                * scale
            )
            query_parts.append(product(grad_scores, keys[:last_key, col_start:col_end]))
            key_parts.append(inner_prod(grad_scores, queries[first_row:row_end, col_start:col_end]))
            value_parts.append(inner_prod(probs, grad_head))
        query_blocks.append(jnp.concatenate(query_parts, axis=1))
        grad_keys = grad_keys.at[:last_key].add(jnp.concatenate(key_parts, axis=1))
        grad_values = grad_values.at[:last_key].add(jnp.concatenate(value_parts, axis=1))
    return (jnp.concatenate(query_blocks, axis=0), grad_keys, grad_values)


def head_step(tokens, memory_rows, grad_rows, path_info, full, bias_in, bias_out):
    qkv_w, attn_w, cross_qw, cross_kvw, cross_ow, in_w, out_w = full
    token_all = widen_rows(tokens)
    queries = product(token_all, qkv_w[0])
    keys_self = product(token_all, qkv_w[1])
    values_self = product(token_all, qkv_w[2])
    attn, attn_sums = attend(queries, keys_self, values_self, path_info, 0)
    hidden_one = tokens + narrow(product(attn, attn_w))
    hidden_all, memory_all = (
        lax.all_gather(hidden_one, "tensor", axis=0, tiled=True),
        lax.all_gather(memory_rows, "tensor", axis=0, tiled=True),
    )
    cross_queries = product(hidden_all, cross_qw)
    cross_keys = product(memory_all, cross_kvw[0])
    cross_values = product(memory_all, cross_kvw[1])
    context, context_sums = attend(cross_queries, cross_keys, cross_values, None, 0)
    hidden_two = hidden_one + narrow(product(context, cross_ow))
    hidden_wide = widen_rows(hidden_two)
    pre_act = product(hidden_wide, in_w) + bias_in
    acted = jax.nn.gelu(pre_act, approximate=False)
    output_rows = hidden_two + narrow(product(acted, out_w)) + bias_out
    grad_wide = widen_rows(grad_rows)
    grad_pre = outer_prod(grad_wide, out_w) * smooth_grad(pre_act)
    grad_in_w = inner_prod(hidden_wide, grad_pre)
    grad_out_w = inner_prod(acted, grad_wide)
    grad_bias_in = jnp.sum(grad_pre, axis=0)
    grad_two = grad_rows + narrow(outer_prod(grad_pre, in_w))
    grad_two_all = widen_rows(grad_two)
    grad_context = outer_prod(grad_two_all, cross_ow)
    grad_cross_out = inner_prod(context, grad_two_all)
    grad_cross_queries, grad_cross_keys, grad_cross_values = attend_back(
        cross_queries, cross_keys, cross_values, context, context_sums, grad_context, None, 0
    )
    grad_cross_q = inner_prod(hidden_all, grad_cross_queries)
    grad_cross_kv = jnp.stack(
        [inner_prod(memory_all, grad_cross_keys), inner_prod(memory_all, grad_cross_values)]
    )
    hidden_part = outer_prod(grad_cross_queries, cross_qw)
    memory_part = outer_prod(grad_cross_keys, cross_kvw[0]) + outer_prod(
        grad_cross_values, cross_kvw[1]
    )
    hidden_sum, grad_memory = (
        lax.psum_scatter(hidden_part, "tensor", scatter_dimension=0, tiled=True),
        lax.psum_scatter(memory_part, "tensor", scatter_dimension=0, tiled=True),
    )
    grad_one = grad_two + hidden_sum
    grad_one_all = widen_rows(grad_one)
    grad_attn = outer_prod(grad_one_all, attn_w)
    grad_attn_w = inner_prod(attn, grad_one_all)
    grad_queries, grad_keys, grad_values = attend_back(
        queries, keys_self, values_self, attn, attn_sums, grad_attn, path_info, 0
    )
    grad_qkv = jnp.stack(
        [
            inner_prod(token_all, grad_queries),
            inner_prod(token_all, grad_keys),
            inner_prod(token_all, grad_values),
        ]
    )
    token_part = (
        outer_prod(grad_queries, qkv_w[0])
        + outer_prod(grad_keys, qkv_w[1])
        + outer_prod(grad_values, qkv_w[2])
    )
    grad_tokens = grad_one + narrow(token_part)
    grads = (
        grad_qkv,
        grad_attn_w,
        grad_cross_q,
        grad_cross_kv,
        grad_cross_out,
        grad_in_w,
        grad_out_w,
    )
    return (output_rows, grad_tokens, grad_memory, grads, grad_bias_in, jnp.sum(grad_rows, axis=0))


def on_device(
    inputs,
    memory,
    lengths,
    parent,
    self_qkv,
    self_out,
    cross_q,
    cross_kv,
    cross_out,
    ff_in,
    ff_bias_in,
    ff_out,
    ff_bias_out,
    cotangent,
):
    row_count = inputs.shape[2] * lax.axis_size("tensor")
    results, grad_inputs, grad_memories = ([], [], [])
    totals = None
    bias_in_total = jnp.zeros_like(ff_bias_in)
    bias_out_total = jnp.zeros_like(ff_bias_out)
    for micro_idx in range(inputs.shape[0]):
        full = (
            lax.all_gather(self_qkv, "dp", axis=1, tiled=True),
            lax.all_gather(self_out, "dp", axis=1, tiled=True),
            lax.all_gather(cross_q, "dp", axis=0, tiled=True),
            lax.all_gather(cross_kv, "dp", axis=1, tiled=True),
            lax.all_gather(cross_out, "dp", axis=1, tiled=True),
            lax.all_gather(ff_in, "dp", axis=0, tiled=True),
            lax.all_gather(ff_out, "dp", axis=1, tiled=True),
        )
        path_info = tree_paths(lengths[micro_idx, 0], parent[micro_idx, 0], row_count)
        output_rows, grad_tokens, grad_memory, grads, grad_bias_in, grad_bias_out = head_step(
            inputs[micro_idx, 0],
            memory[micro_idx, 0],
            cotangent[micro_idx, 0],
            path_info,
            full,
            ff_bias_in,
            ff_bias_out,
        )
        totals = grads if totals is None else jax.tree.map(jnp.add, totals, grads)
        bias_in_total = bias_in_total + grad_bias_in
        bias_out_total = bias_out_total + grad_bias_out
        results.append(output_rows)
        grad_inputs.append(grad_tokens)
        grad_memories.append(grad_memory)
    totals = (
        lax.psum_scatter(totals[0], "dp", scatter_dimension=1, tiled=True),
        lax.psum_scatter(totals[1], "dp", scatter_dimension=1, tiled=True),
        lax.psum_scatter(totals[2], "dp", scatter_dimension=0, tiled=True),
        lax.psum_scatter(totals[3], "dp", scatter_dimension=1, tiled=True),
        lax.psum_scatter(totals[4], "dp", scatter_dimension=1, tiled=True),
        lax.psum_scatter(totals[5], "dp", scatter_dimension=0, tiled=True),
        lax.psum_scatter(totals[6], "dp", scatter_dimension=1, tiled=True),
    )
    bias_in_grad = lax.psum(bias_in_total, "dp")
    bias_out_grad = lax.psum(bias_out_total, ("dp", "tensor"))
    return (
        jnp.stack(results)[:, None],
        jnp.stack(grad_inputs)[:, None],
        jnp.stack(grad_memories)[:, None],
        totals[0],
        totals[1],
        totals[2],
        totals[3],
        totals[4],
        totals[5],
        bias_in_grad,
        totals[6],
        bias_out_grad,
    )


def solution(mesh):
    placed = (
        P(None, "dp", "tensor", None),
        P(None, "dp", "tensor", None),
        P(None, "dp", None),
        P(None, "dp", None),
        P(None, "dp", "tensor"),
        P("tensor", "dp"),
        P("dp", "tensor"),
        P(None, "dp", "tensor"),
        P("tensor", "dp"),
        P("dp", "tensor"),
        P("tensor"),
        P("tensor", "dp"),
        P(),
        P(None, "dp", "tensor", None),
    )
    return jax.shard_map(
        on_device,
        mesh=mesh,
        in_specs=placed,
        out_specs=(
            P(None, "dp", "tensor", None),
            P(None, "dp", "tensor", None),
            P(None, "dp", "tensor", None),
            P(None, "dp", "tensor"),
            P("tensor", "dp"),
            P("dp", "tensor"),
            P(None, "dp", "tensor"),
            P("tensor", "dp"),
            P("dp", "tensor"),
            P("tensor"),
            P("tensor", "dp"),
            P(),
        ),
        check_vma=False,
    )
```

profile of v0, /device:TPU:0, one launch (start us, length us, event | category | flops | bytes accessed | tf_op | source)
XLA Modules:
  0.0 2201.3 jit_solution(11520739869136421906)
XLA Ops:
  34.2 60.6 %all-gather.43.cloned.1.call-done = f32[1,1,2048,512]{3,2,1,0:T(8,128)} async-done(((f32[1,1,512,512]{3,2,1,0:T(8,128)}), f32[1,1,2048,512]{3,2,1,0:T(8,128)}) %all-gather.43.cloned.1.call-update) | async-done | bytes 4194320 | tf_op jit(solution)/shard_map/all_gather | solution.py:34
  253.3 79.5 %reduce-scatter.20.cloned.1.call-done = f32[512,512]{1,0:T(8,128)} async-done(((f32[2048,512]{1,0:T(8,128)}), f32[512,512]{1,0:T(8,128)}) %reduce-scatter.20.cloned.1.call-update) | async-done | bytes 1048592 | tf_op jit(solution)/shard_map/reduce_scatter | solution.py:38
  346.3 23.6 %all-gather.3 = f32[1,1,256,512]{3,2,1,0:T(8,128)S(1)} all-gather(f32[1,1,64,512]{3,2,1,0:T(8,128)S(1)} %get-tuple-element.637), channel_id=5, replica_groups=mesh['dp'=8,'tensor'=4] {'tensor'}, dimensions={2}, use_global_device_ids=true | all-gather | bytes 655360 | tf_op jit(solution)/shard_map/all_gather | solution.py:160
  390.2 35.8 %all-gather.29.cloned.1.call-done = f32[2048,512]{1,0:T(8,128)} async-done(((f32[512,512]{1,0:T(8,128)}), f32[2048,512]{1,0:T(8,128)}) %all-gather.29.cloned.1.call-update) | async-done | bytes 4194320 | tf_op jit(solution)/shard_map/all_gather | solution.py:159
  458.3 22.0 all-gather.1
  482.1 33.0 %all-gather.21.cloned.1.call-done = f32[2048,512]{1,0:T(8,128)} async-done(((f32[512,512]{1,0:T(8,128)}), f32[2048,512]{1,0:T(8,128)}) %all-gather.21.cloned.1.call-update) | async-done | bytes 4194320 | tf_op jit(solution)/shard_map/all_gather | solution.py:159
  548.3 44.5 %reduce-scatter.28.cloned.1.call-done = f32[512,512]{1,0:T(8,128)} async-done(((f32[2048,512]{1,0:T(8,128)}), f32[512,512]{1,0:T(8,128)}) %reduce-scatter.28.cloned.1.call-update) | async-done | bytes 1048592 | tf_op jit(solution)/shard_map/reduce_scatter | solution.py:38
  595.3 125.1 %reduce-scatter.22.cloned.1.call-done = f32[512,512]{1,0:T(8,128)} async-done(((f32[2048,512]{1,0:T(8,128)}), f32[512,512]{1,0:T(8,128)}) %reduce-scatter.22.cloned.1.call-update) | async-done | bytes 1048592 | tf_op jit(solution)/shard_map/reduce_scatter | solution.py:38
  750.3 71.7 %all-gather.23.cloned.1.call-done = f32[2048,512]{1,0:T(8,128)} async-done(((f32[512,512]{1,0:T(8,128)}), f32[2048,512]{1,0:T(8,128)}) %all-gather.23.cloned.1.call-update) | async-done | bytes 4194320 | tf_op jit(solution)/shard_map/all_gather | solution.py:34
  821.9 27.5 %fusion.1 = (f32[2048,512]{1,0:T(8,128)}, f32[2048,512]{1,0:T(8,128)}, f32[2048,512]{1,0:T(8,128)}) fusion(f32[512]{0:T(512)S(1)} %copy-done.481, f32[2048,512]{1,0:T(8,128)} %fusion.739, f32[2048,512]{1,0:T(8,128)} %all-gather.23.cloned.1.call-done, f32[512,512]{1,0:T(8,128)S(1)} %copy-done.71), kind=kOutput, calls=%fused_computation.5 | convolution fusion | flops 6578765824 | bytes 22022144 | tf_op jit(solution)/shard_map/dot_general | solution.py:16
  849.4 78.5 %all-gather.45.cloned.1.call-done = f32[1,1,2048,512]{3,2,1,0:T(8,128)} async-done(((f32[1,1,512,512]{3,2,1,0:T(8,128)}), f32[1,1,2048,512]{3,2,1,0:T(8,128)}) %all-gather.45.cloned.1.call-update) | async-done | bytes 4194320 | tf_op jit(solution)/shard_map/all_gather | solution.py:34
  949.8 58.9 %all-gather.47.cloned.1.call-done = f32[1,1,2048,512]{3,2,1,0:T(8,128)} async-done(((f32[1,1,512,512]{3,2,1,0:T(8,128)}), f32[1,1,2048,512]{3,2,1,0:T(8,128)}) %all-gather.47.cloned.1.call-update) | async-done | bytes 4194320 | tf_op jit(solution)/shard_map/all_gather | solution.py:34
  1030.4 55.7 %reduce-scatter.32.cloned.1.call-done = f32[512,512]{1,0:T(8,128)} async-done(((f32[2048,512]{1,0:T(8,128)}), f32[512,512]{1,0:T(8,128)}) %reduce-scatter.32.cloned.1.call-update) | async-done | bytes 1048592 | tf_op jit(solution)/shard_map/reduce_scatter | solution.py:38
  1086.2 79.5 %reduce-scatter.38.cloned.1.call-done = f32[512,512]{1,0:T(8,128)} async-done(((f32[2048,512]{1,0:T(8,128)}), f32[512,512]{1,0:T(8,128)}) %reduce-scatter.38.cloned.1.call-update) | async-done | bytes 1048592 | tf_op jit(solution)/shard_map/reduce_scatter | solution.py:38
  1179.6 70.5 %all-gather.37.cloned.1.call-done = f32[2048,512]{1,0:T(8,128)} async-done(((f32[512,512]{1,0:T(8,128)}), f32[2048,512]{1,0:T(8,128)}) %all-gather.37.cloned.1.call-update) | async-done | bytes 4194320 | tf_op jit(solution)/shard_map/all_gather | solution.py:34
  1281.2 49.7 %all-gather.33.cloned.1.call-done = f32[2048,512]{1,0:T(8,128)} async-done(((f32[512,512]{1,0:T(8,128)}), f32[2048,512]{1,0:T(8,128)}) %all-gather.33.cloned.1.call-update) | async-done | bytes 4194320 | tf_op jit(solution)/shard_map/all_gather | solution.py:34
  1358.4 50.0 %reduce-scatter.40.cloned.1.call-done = f32[512,512]{1,0:T(8,128)} async-done(((f32[2048,512]{1,0:T(8,128)}), f32[512,512]{1,0:T(8,128)}) %reduce-scatter.40.cloned.1.call-update) | async-done | bytes 1048592 | tf_op jit(solution)/shard_map/reduce_scatter | solution.py:192
  1411.2 124.7 %reduce-scatter.34.cloned.1.call-done = f32[512,512]{1,0:T(8,128)} async-done(((f32[2048,512]{1,0:T(8,128)}), f32[512,512]{1,0:T(8,128)}) %reduce-scatter.34.cloned.1.call-update) | async-done | bytes 1048592 | tf_op jit(solution)/shard_map/reduce_scatter | solution.py:192
  1895.7 43.6 %psum.15 = f32[512]{0:T(512)} all-reduce(f32[512]{0:T(512)S(1)} %add.834), channel_id=1, replica_groups=mesh['dp'=8,'tensor'=4] {'dp','tensor'}, use_global_device_ids=true, to_apply=%region_130.131 | all-reduce | flops 512 | bytes 4096 | tf_op jit(solution)/shard_map/psum | solution.py:284
  2014.3 26.9 %reduce-scatter.54.cloned.1.call-done = f32[64,512]{1,0:T(8,128)} async-done(((f32[512,512]{1,0:T(8,128)}), f32[64,512]{1,0:T(8,128)}) %reduce-scatter.54.cloned.1.call-update) | async-done | bytes 131088 | tf_op jit(solution)/shard_map/reduce_scatter | solution.py:280
  2041.2 40.0 %reduce-scatter.56.cloned.1.call-done = f32[512,64]{0,1:T(8,128)} async-done(((f32[512,512]{0,1:T(8,128)}), f32[512,64]{0,1:T(8,128)}) %reduce-scatter.56.cloned.1.call-update) | async-done | bytes 131088 | tf_op jit(solution)/shard_map/reduce_scatter | solution.py:281
  2081.2 37.5 %reduce-scatter.52.cloned.1.call-done = f32[128,64]{0,1:T(8,128)} async-done(((f32[128,512]{0,1:T(8,128)}), f32[128,64]{0,1:T(8,128)}) %reduce-scatter.52.cloned.1.call-update) | async-done | bytes 32784 | tf_op jit(solution)/shard_map/reduce_scatter | solution.py:279
  2118.7 37.1 %reduce-scatter.50.cloned.1.call-done = f32[64,128]{1,0:T(8,128)} async-done(((f32[512,128]{1,0:T(8,128)}), f32[64,128]{1,0:T(8,128)}) %reduce-scatter.50.cloned.1.call-update) | async-done | bytes 32784 | tf_op jit(solution)/shard_map/reduce_scatter | solution.py:277
  2155.7 37.5 %reduce-scatter.48.cloned.1.call-done = f32[128,64]{0,1:T(8,128)} async-done(((f32[128,512]{0,1:T(8,128)}), f32[128,64]{0,1:T(8,128)}) %reduce-scatter.48.cloned.1.call-update) | async-done | bytes 32784 | tf_op jit(solution)/shard_map/reduce_scatter | solution.py:276
  (1437 shorter events, 863.7 us)
Async XLA Ops:
  11.9 241.4 %reduce-scatter.26.cloned.1.call-start = ((), (), s32[]{:S(2)}) async-start(), calls=%async_computation.26 | async-start | bytes 5242880 | tf_op jit(solution)/shard_map/reduce_scatter | solution.py:38
  369.9 222.8 %reduce-scatter.28.cloned.1.call-start = ((), (), s32[]{:S(2)}) async-start(), calls=%async_computation.28 | async-start | bytes 5242880 | tf_op jit(solution)/shard_map/reduce_scatter | solution.py:38
  458.2 262.1 %reduce-scatter.22.cloned.1.call-start = ((), (), s32[]{:S(2)}) async-start(), calls=%async_computation.21 | async-start | bytes 5242880 | tf_op jit(solution)/shard_map/reduce_scatter | solution.py:38
  548.3 191.9 %all-gather.31.cloned.1.call-start = ((), (), s32[]{:S(2)}) async-start(), calls=%async_computation.29 | async-start | bytes 5242880 | tf_op jit(solution)/shard_map/all_gather | solution.py:34
  595.2 226.7 %all-gather.23.cloned.1.call-start = ((), (), s32[]{:S(2)}) async-start(), calls=%async_computation.22 | async-start | bytes 5242880 | tf_op jit(solution)/shard_map/all_gather | solution.py:34
  723.6 204.4 %all-gather.45.cloned.1.call-start = ((), (), s32[]{:S(2)}) async-start(), calls=%async_computation.50 | async-start | bytes 5242880 | tf_op jit(solution)/shard_map/all_gather | solution.py:34
  727.4 281.3 %all-gather.47.cloned.1.call-start = ((), (), s32[]{:S(2)}) async-start(), calls=%async_computation.51 | async-start | bytes 5242880 | tf_op jit(solution)/shard_map/all_gather | solution.py:34
  728.1 358.0 %reduce-scatter.32.cloned.1.call-start = ((), (), s32[]{:S(2)}) async-start(), calls=%async_computation.31 | async-start | bytes 5242880 | tf_op jit(solution)/shard_map/reduce_scatter | solution.py:38
  949.8 215.9 %reduce-scatter.38.cloned.1.call-start = ((), (), s32[]{:S(2)}) async-start(), calls=%async_computation.36 | async-start | bytes 5242880 | tf_op jit(solution)/shard_map/reduce_scatter | solution.py:38
  1030.4 219.8 %all-gather.37.cloned.1.call-start = ((), (), s32[]{:S(2)}) async-start(), calls=%async_computation.37 | async-start | bytes 5242880 | tf_op jit(solution)/shard_map/all_gather | solution.py:34
  1170.5 238.0 %reduce-scatter.40.cloned.1.call-start = ((), (), s32[]{:S(2)}) async-start(), calls=%async_computation.38 | async-start | bytes 5242880 | tf_op jit(solution)/shard_map/reduce_scatter | solution.py:192
  1276.4 259.6 %reduce-scatter.34.cloned.1.call-start = ((), (), s32[]{:S(2)}) async-start(), calls=%async_computation.33 | async-start | bytes 5242880 | tf_op jit(solution)/shard_map/reduce_scatter | solution.py:192
  1358.3 260.0 %all-gather.39.cloned.1.call-start = ((), (), s32[]{:S(2)}) async-start(), calls=%async_computation.39 | async-start | bytes 5242880 | tf_op jit(solution)/shard_map/all_gather | solution.py:34
  1411.2 307.6 %all-gather.35.cloned.1.call-start = ((), (), s32[]{:S(2)}) async-start(), calls=%async_computation.34 | async-start | bytes 5242880 | tf_op jit(solution)/shard_map/all_gather | solution.py:34
  1538.7 414.2 %reduce-scatter.24.cloned.1.call-start = ((), (), s32[]{:S(2)}) async-start(), calls=%async_computation.25 | async-start | bytes 5242880 | tf_op jit(solution)/shard_map/reduce_scatter | solution.py:38
  1549.2 403.8 %reduce-scatter.30.cloned.1.call-start = ((), (), s32[]{:S(2)}) async-start(), calls=%async_computation.30 | async-start | bytes 5242880 | tf_op jit(solution)/shard_map/reduce_scatter | solution.py:38
  1569.3 419.0 %reduce-scatter.44.cloned.1.call-start = ((), (), s32[]{:S(2)}) async-start(), calls=%async_computation.41 | async-start | bytes 655360 | tf_op jit(solution)/shard_map/reduce_scatter | solution.py:193
  1610.6 377.8 %reduce-scatter.46.cloned.1.call-start = ((), (), s32[]{:S(2)}) async-start(), calls=%async_computation.42 | async-start | bytes 655360 | tf_op jit(solution)/shard_map/reduce_scatter | solution.py:193
  1618.3 388.5 %all-reduce.9.cloned.1.call-start = ((), (), s32[]{:S(2)}) async-start(), calls=%async_computation.52 | async-start | bytes 3145728
  1858.2 183.0 %reduce-scatter.54.cloned.1.call-start = ((), (), s32[]{:S(2)}) async-start(), calls=%async_computation.46 | async-start | bytes 1179648 | tf_op jit(solution)/shard_map/reduce_scatter | solution.py:280
  1876.0 205.1 %reduce-scatter.56.cloned.1.call-start = ((), (), s32[]{:S(2)}) async-start(), calls=%async_computation.47 | async-start | bytes 1179648 | tf_op jit(solution)/shard_map/reduce_scatter | solution.py:281
  1894.3 224.4 %reduce-scatter.52.cloned.1.call-start = ((), (), s32[]{:S(2)}) async-start(), calls=%async_computation.45 | async-start | bytes 294912 | tf_op jit(solution)/shard_map/reduce_scatter | solution.py:279
  1971.7 184.1 %reduce-scatter.50.cloned.1.call-start = ((), (), s32[]{:S(2)}) async-start(), calls=%async_computation.44 | async-start | bytes 294912 | tf_op jit(solution)/shard_map/reduce_scatter | solution.py:277
  1988.3 205.0 %reduce-scatter.48.cloned.1.call-start = ((), (), s32[]{:S(2)}) async-start(), calls=%async_computation.43 | async-start | bytes 294912 | tf_op jit(solution)/shard_map/reduce_scatter | solution.py:276
  (493 other events, 8955.1 us)
Sparse Core Ops, SparseCore 0:
  11.3 83.4 all-gather.42
  96.3 79.2 all-gather.40
  178.0 75.2 reduce-scatter.25
  255.6 77.2 reduce-scatter.19
  336.4 89.5 all-gather.28
  427.4 87.6 all-gather.20
  517.4 75.3 reduce-scatter.27
  595.2 125.1 reduce-scatter.21
  1411.3 144.3 all-gather.38
  1557.2 80.5 all-gather.34
  1640.0 75.2 reduce-scatter.23
  1717.6 77.2 reduce-scatter.29
  1797.2 22.1 reduce-scatter.43
  1821.5 19.9 reduce-scatter.45
  1844.5 76.6 reduce-scatter.35
  1923.4 77.2 reduce-scatter.41
  2004.6 36.4 reduce-scatter.53
  2045.1 35.9 reduce-scatter.55
  2085.0 33.5 reduce-scatter.51
  2122.1 33.5 reduce-scatter.49
  2159.6 33.5 reduce-scatter.47
Sparse Core Ops, SparseCore 1:
  550.0 21.9 all-gather.24
  595.3 144.8 all-gather.30
  741.6 80.2 all-gather.22
  823.9 21.8 all-gather.26
  847.3 80.6 all-gather.44
  929.5 79.1 all-gather.46
  1010.9 75.3 reduce-scatter.31
  1088.4 77.2 reduce-scatter.37
  1169.1 81.0 all-gather.36
  1251.8 79.1 all-gather.32
  1333.1 75.3 reduce-scatter.39
  1410.9 125.0 reduce-scatter.33
  1834.3 57.8 all-reduce.8
where the time goes:
time: 2210 us; the launch traced here: 2200 us
  waiting for transfers between devices  1220 us (55%)
  matrix products  706 us (32%)
  blocking collectives  152 us (7%)
  other arithmetic  76.2 us (3%)
  local copies, waits for them, and re-layouts  24.2 us (1%)
  between operations  24.2 us (1%)
    all_gather x10, waiting for transfers between devices, widen_rows(): return lax.all_gather(rows, 'tensor', axis=0, tiled=True)  406 us
    reduce_scatter x10, waiting for transfers between devices, narrow(): return lax.psum_scatter(terms, 'tensor', scatter_dimension=0, tiled=True)  385 us
    dot_general x84, matrix products, outer_prod(): return jnp.einsum('rk,nk->rn', left, right, precision=HIGH)  250 us
    dot_general x84, matrix products, product(): return jnp.dot(left, right, precision=HIGH)  242 us
    dot_general x84, matrix products, inner_prod(): return jnp.einsum('rk,rn->kn', left, right, precision=HIGH)  215 us
    reduce_scatter x2, waiting for transfers between devices, head_step(): lax.psum_scatter(hidden_part, 'tensor', scatter_dimension=0, tiled=True)  175 us
    all_gather x2, waiting for transfers between devices, head_step(): lax.all_gather(hidden_one, 'tensor', axis=0, tiled=True)  68.8 us
    all_gather x2, blocking collectives, head_step(): lax.all_gather(memory_rows, 'tensor', axis=0, tiled=True)  45.6 us
  transfers between devices with their start and end apart: 34, of which 23 were waited for; matrix products, arithmetic and copies ran while one was open for 36% of the time, Pallas kernels for 0%

commit v1 on v0

v1 whole, which is shorter than its diff:
```python
import functools

import jax
import jax.numpy as jnp
from jax import lax
from jax.experimental import pallas as pl
from jax.experimental.pallas import tpu as pltpu
from jax.sharding import PartitionSpec as P

HEAD = 64
LOG2E = 1.4426950408889634
LN2 = 0.6931471805599453
BF = jnp.bfloat16
F32 = jnp.float32
NT = (((1,), (1,)), ((), ()))
NN = (((1,), (0,)), ((), ()))


def dot(a, b, dims=NN):
    return lax.dot_general(a, b, dims, preferred_element_type=F32)


def split(x):
    hi = x.astype(BF).astype(F32)
    return hi, x - hi


def attn_fwd_kernel(q_ref, k_ref, v_ref, qa_ref, ka_ref, o_ref, l_ref, qs, ks, vt, *, causal, qb, kb, rq, rk):
    lane = lax.broadcasted_iota(jnp.int32, (256, 128), 1)
    left = lane < HEAD

    def sel(a, b):
        return jnp.where(left, a, b)

    def build_q(i, _):
        r = pl.ds(pl.multiple_of(i * 256, 256), 256)
        x = q_ref[r, :] * (HEAD ** -0.5 * LOG2E)
        hi, lo = split(x)
        hir, lor = pltpu.roll(hi, HEAD, 1), pltpu.roll(lo, HEAD, 1)
        aux = qa_ref[r, :].astype(F32) if causal else jnp.zeros((256, 128), F32)
        qs[0, r, 0:128] = sel(hi, hir).astype(BF)
        qs[0, r, 128:256] = sel(lo, aux).astype(BF)
        qs[1, r, 0:128] = sel(hir, hi).astype(BF)
        qs[1, r, 128:256] = sel(lor, aux).astype(BF)
        return 0

    def build_k(i, _):
        r = pl.ds(pl.multiple_of(i * 256, 256), 256)
        hi, lo = split(k_ref[r, :])
        hir, lor = pltpu.roll(hi, HEAD, 1), pltpu.roll(lo, HEAD, 1)
        aux = ka_ref[r, :].astype(F32) if causal else jnp.zeros((256, 128), F32)
        ks[0, r, 0:128] = sel(hi, lor).astype(BF)
        ks[0, r, 128:256] = sel(hi, aux).astype(BF)
        ks[1, r, 0:128] = sel(hir, lo).astype(BF)
        ks[1, r, 128:256] = sel(hir, aux).astype(BF)
        hi, lo = split(v_ref[r, :])
        hir, lor = pltpu.roll(hi, HEAD, 1), pltpu.roll(lo, HEAD, 1)
        vt[0, :, r] = sel(hi, lor).T.astype(BF)
        vt[1, :, r] = sel(hir, lo).T.astype(BF)
        return 0

    lax.fori_loop(0, rq // 256, build_q, 0)
    lax.fori_loop(0, rk // 256, build_k, 0)

    def one_q(i, _):
        rows = pl.ds(pl.multiple_of(i * qb, qb), qb)
        qh = [qs[h, rows, :] for h in range(2)]

        def step(carry, first_key, diag):
            keys = pl.ds(pl.multiple_of(first_key, kb), kb)
            out = []
            for h in range(2):
                m, s, acc = carry[h]
                st = dot(ks[h, keys, :], qh[h], NT)
                if diag:
                    kk = lax.broadcasted_iota(jnp.int32, (kb, qb), 0)
                    qq = lax.broadcasted_iota(jnp.int32, (kb, qb), 1)
                    st = jnp.where(kk <= qq, st, -1e30)
                mn = jnp.maximum(m, jnp.max(st, axis=0, keepdims=True))
                p = jnp.exp2(st - mn)
                al = jnp.exp2(m - mn)
                s = s * al + jnp.sum(p, axis=0, keepdims=True)
                ph = p.astype(BF)
                plo = (p - ph.astype(F32)).astype(BF)
                acc = acc * al + dot(vt[h, :, keys], ph) + dot(vt[h, :, keys], plo)
                out.append((mn, s, acc))
            return tuple(out)

        init = (jnp.full((1, qb), -1e30, F32), jnp.zeros((1, qb), F32), jnp.zeros((128, qb), F32))
        carry = (init, init)
        if causal:
            carry = lax.fori_loop(0, i * (qb // kb), lambda j, c: step(c, j * kb, False), carry)
            assert qb == kb
            carry = step(carry, i * qb, True)
        else:
            for j in range(rk // kb):
                carry = step(carry, j * kb, False)
        outs = []
        for h in range(2):
            m, s, acc = carry[h]
            outs.append((acc[0:HEAD] + acc[HEAD:]) / s)
            l_ref[0, h:h + 1, rows] = m + jnp.log2(s)
        o_ref[rows, :] = jnp.concatenate(outs, axis=0).T
        return 0

    lax.fori_loop(0, rq // qb, one_q, 0)


def attn_fwd(q, k, v, qaux, kaux, causal, qb=256, kb=256):
    rq, w = q.shape
    rk = k.shape[0]
    pairs = w // 128
    ra = qaux.shape[0]
    qspec = pl.BlockSpec((rq, 128), lambda p: (0, p))
    kspec = pl.BlockSpec((rk, 128), lambda p: (0, p))
    return pl.pallas_call(
        functools.partial(attn_fwd_kernel, causal=causal, qb=qb, kb=kb, rq=rq, rk=rk),
        grid=(pairs,),
        in_specs=[qspec, kspec, kspec,
                  pl.BlockSpec((ra, 128), lambda p: (0, 0)), pl.BlockSpec((ra, 128), lambda p: (0, 0))],
        out_specs=[qspec, pl.BlockSpec((1, 2, rq), lambda p: (p, 0, 0))],
        out_shape=[jax.ShapeDtypeStruct((rq, w), F32), jax.ShapeDtypeStruct((pairs, 2, rq), F32)],
        scratch_shapes=[pltpu.VMEM((2, rq, 256), BF), pltpu.VMEM((2, rk, 256), BF), pltpu.VMEM((2, 128, rk), BF)],
        compiler_params=pltpu.CompilerParams(vmem_limit_bytes=48 << 20),
        cost_estimate=pl.CostEstimate(flops=int(2e9) * pairs, bytes_accessed=rq * w * 16, transcendentals=0),
        name="attn_fwd",
    )(q, k, v, qaux, kaux)


def attn_bwd_kernel(q_ref, k_ref, v_ref, do_ref, l_ref, d_ref, qa_ref, ka_ref, dq_ref, dk_ref, dv_ref,
                    qs, ks, kt, vs, dos, dka, dva, *, causal, qb, kb, rq, rk):
    lane = lax.broadcasted_iota(jnp.int32, (256, 128), 1)
    left = lane < HEAD

    def sel(a, b):
        return jnp.where(left, a, b)

    def build_q(i, _):
        r = pl.ds(pl.multiple_of(i * 256, 256), 256)
        hi, lo = split(q_ref[r, :] * (HEAD ** -0.5 * LOG2E))
        hir, lor = pltpu.roll(hi, HEAD, 1), pltpu.roll(lo, HEAD, 1)
        aux = qa_ref[r, :].astype(F32) if causal else jnp.zeros((256, 128), F32)
        qs[0, r, 0:128] = sel(hi, lor).astype(BF)
        qs[0, r, 128:256] = sel(hi, aux).astype(BF)
        qs[1, r, 0:128] = sel(hir, lo).astype(BF)
        qs[1, r, 128:256] = sel(hir, aux).astype(BF)
        hi, lo = split(do_ref[r, :])
        hir, lor = pltpu.roll(hi, HEAD, 1), pltpu.roll(lo, HEAD, 1)
        zero = jnp.zeros((256, 128), F32)
        dos[0, r, 0:128] = sel(hi, lor).astype(BF)
        dos[0, r, 128:256] = sel(hi, zero).astype(BF)
        dos[1, r, 0:128] = sel(hir, lo).astype(BF)
        dos[1, r, 128:256] = sel(hir, zero).astype(BF)
        return 0

    def build_k(i, _):
        r = pl.ds(pl.multiple_of(i * 256, 256), 256)
        hi, lo = split(k_ref[r, :])
        hir, lor = pltpu.roll(hi, HEAD, 1), pltpu.roll(lo, HEAD, 1)
        aux = ka_ref[r, :].astype(F32) if causal else jnp.zeros((256, 128), F32)
        ks[0, r, 0:128] = sel(hi, hir).astype(BF)
        ks[0, r, 128:256] = sel(lo, aux).astype(BF)
        ks[1, r, 0:128] = sel(hir, hi).astype(BF)
        ks[1, r, 128:256] = sel(lor, aux).astype(BF)
        kt[0, :, r] = sel(hi, lor).T.astype(BF)
        kt[1, :, r] = sel(hir, lo).T.astype(BF)
        hi, lo = split(v_ref[r, :])
        hir, lor = pltpu.roll(hi, HEAD, 1), pltpu.roll(lo, HEAD, 1)
        zero = jnp.zeros((256, 128), F32)
        vs[0, r, 0:128] = sel(hi, hir).astype(BF)
        vs[0, r, 128:256] = sel(lo, zero).astype(BF)
        vs[1, r, 0:128] = sel(hir, hi).astype(BF)
        vs[1, r, 128:256] = sel(lor, zero).astype(BF)
        dka[0, r, :] = zero
        dka[1, r, :] = zero
        dva[0, r, :] = zero
        dva[1, r, :] = zero
        return 0

    lax.fori_loop(0, rq // 256, build_q, 0)
    lax.fori_loop(0, rk // 256, build_k, 0)

    def one_q(i, _):
        rows = pl.ds(pl.multiple_of(i * qb, qb), qb)

        def step(carry, first_key, diag):
            keys = pl.ds(pl.multiple_of(first_key, kb), kb)
            out = []
            for h in range(2):
                acc = carry[h]
                qh = qs[h, rows, :]
                dh = dos[h, rows, :]
                st = dot(ks[h, keys, :], qh, NT)
                if diag:
                    kk = lax.broadcasted_iota(jnp.int32, (kb, qb), 0)
                    qq = lax.broadcasted_iota(jnp.int32, (kb, qb), 1)
                    st = jnp.where(kk <= qq, st, -1e30)
                p = jnp.exp2(st - l_ref[0, h:h + 1, rows])
                ph = p.astype(BF)
                plo = (p - ph.astype(F32)).astype(BF)
                dhl = dh[:, 0:128]
                dva[h, keys, :] += dot(ph, dhl) + dot(plo, dhl)
                dp = dot(vs[h, keys, :], dh, NT)
                ds = p * (dp - d_ref[0, h:h + 1, rows])
                dsh = ds.astype(BF)
                dsl = (ds - dsh.astype(F32)).astype(BF)
                qhl = qh[:, 0:128]
                dka[h, keys, :] += dot(dsh, qhl) + dot(dsl, qhl)
                kth = kt[h, :, keys]
                acc = acc + dot(kth, dsh) + dot(kth, dsl)
                out.append(acc)
            return tuple(out)

        init = jnp.zeros((128, qb), F32)
        carry = (init, init)
        if causal:
            carry = lax.fori_loop(0, i * (qb // kb), lambda j, c: step(c, j * kb, False), carry)
            carry = step(carry, i * qb, True)
        else:
            for j in range(rk // kb):
                carry = step(carry, j * kb, False)
        outs = [(a[0:HEAD] + a[HEAD:]) * (HEAD ** -0.5) for a in carry]
        dq_ref[rows, :] = jnp.concatenate(outs, axis=0).T
        return 0

    lax.fori_loop(0, rq // qb, one_q, 0)

    def finish(i, _):
        r = pl.ds(pl.multiple_of(i * 256, 256), 256)
        a, b = dka[0, r, :], dka[1, r, :]
        dk_ref[r, :] = sel(a + pltpu.roll(a, HEAD, 1), b + pltpu.roll(b, HEAD, 1)) * LN2
        a, b = dva[0, r, :], dva[1, r, :]
        dv_ref[r, :] = sel(a + pltpu.roll(a, HEAD, 1), b + pltpu.roll(b, HEAD, 1))
        return 0

    lax.fori_loop(0, rk // 256, finish, 0)


def attn_bwd(q, k, v, do, lse, delta, qaux, kaux, causal, qb=256, kb=256):
    rq, w = q.shape
    rk = k.shape[0]
    pairs = w // 128
    ra = qaux.shape[0]
    qspec = pl.BlockSpec((rq, 128), lambda p: (0, p))
    kspec = pl.BlockSpec((rk, 128), lambda p: (0, p))
    lspec = pl.BlockSpec((1, 2, rq), lambda p: (p, 0, 0))
    aspec = pl.BlockSpec((ra, 128), lambda p: (0, 0))
    return pl.pallas_call(
        functools.partial(attn_bwd_kernel, causal=causal, qb=qb, kb=kb, rq=rq, rk=rk),
        grid=(pairs,),
        in_specs=[qspec, kspec, kspec, qspec, lspec, lspec, aspec, aspec],
        out_specs=[qspec, kspec, kspec],
        out_shape=[jax.ShapeDtypeStruct((rq, w), F32), jax.ShapeDtypeStruct((rk, w), F32), jax.ShapeDtypeStruct((rk, w), F32)],
        scratch_shapes=[pltpu.VMEM((2, rq, 256), BF), pltpu.VMEM((2, rk, 256), BF), pltpu.VMEM((2, 128, rk), BF),
                        pltpu.VMEM((2, rk, 256), BF), pltpu.VMEM((2, rq, 256), BF),
                        pltpu.VMEM((2, rk, 128), F32), pltpu.VMEM((2, rk, 128), F32)],
        compiler_params=pltpu.CompilerParams(vmem_limit_bytes=56 << 20),
        cost_estimate=pl.CostEstimate(flops=int(5e9) * pairs, bytes_accessed=rq * w * 32, transcendentals=0),
        name="attn_bwd",
    )(q, k, v, do, lse, delta, qaux, kaux)


def tree_aux(lengths, parent, n):
    segs = lengths.shape[0]
    ends = jnp.cumsum(lengths)
    places = jnp.arange(n, dtype=jnp.int32)
    seg = jnp.sum((places[:, None] >= ends[None, :-1]).astype(jnp.int32), axis=1)
    labels = jnp.arange(segs, dtype=jnp.int32)
    onehot = seg[:, None] == labels[None, :]
    up1 = jnp.sum(jnp.where(onehot, parent[None, :], 0), axis=1)
    up2 = jnp.sum(jnp.where(up1[:, None] == labels[None, :], parent[None, :], 0), axis=1)
    lab = jnp.arange(128, dtype=jnp.int32)[None, :] - HEAD
    inside = (lab >= 0) & (lab < segs)
    sg = seg[:, None]
    kaux = jnp.where(inside & (lab == sg), 1.0, 0.0).astype(BF)
    ok = (lab == sg) | ((sg > 0) & ((lab == up1[:, None]) | (lab == up2[:, None])))
    qaux = jnp.where(inside & ~ok, -1e30, 0.0).astype(BF)
    return qaux, kaux


HIGH = lax.Precision.HIGH
TN = (((0,), (0,)), ((), ()))
ROOT_HALF = 0.7071067811865476
NORMAL_PEAK = 0.3989422804014327
BOTH = ("dp", "tensor")


def mm(a, b, dims=NN):
    return lax.dot_general(a, b, dims, precision=HIGH, preferred_element_type=F32)


def flip_bit(size, bit):
    return [(i, i ^ (1 << bit)) for i in range(size)]


def item_routes(dp, tensor):
    routes = []
    for turn in range(2):
        pairs = []
        for c in range(dp // 2):
            for t in range(2):
                for z in range(tensor):
                    b = (z + turn) % 2
                    pairs.append(((2 * c + t) * tensor + z, (2 * c + z // 2) * tensor + 2 * b + t))
        routes.append(pairs)
    return routes


def scatter_items(x, routes, z):
    first = lax.ppermute(lax.dynamic_index_in_dim(x, z % 2, 0, keepdims=False), BOTH, routes[0])
    second = lax.ppermute(lax.dynamic_index_in_dim(x, 1 - z % 2, 0, keepdims=False), BOTH, routes[1])
    even = z // 2 == 0
    return jnp.where(even, jnp.concatenate([first, second]), jnp.concatenate([second, first]))


def return_items(rows, routes, z):
    half = rows.shape[0] // 2
    b = z // 2
    back = [[(d, s) for s, d in r] for r in routes]
    first = lax.ppermute(lax.dynamic_slice_in_dim(rows, b * half, half), BOTH, back[0])
    second = lax.ppermute(lax.dynamic_slice_in_dim(rows, (1 - b) * half, half), BOTH, back[1])
    even = z % 2 == 0
    return jnp.where(even, jnp.stack([first, second]), jnp.stack([second, first]))


def swap(x, dp):
    return lax.ppermute(x, "dp", flip_bit(dp, 0))


def both_cores(mine, other, k):
    return jnp.where(k == 0, jnp.concatenate([mine, other]), jnp.concatenate([other, mine]))


def flip_where(x, axis, flag):
    return jnp.where(flag, lax.rev(x, (axis,)), x)


def gather_weights(x, dp, tensor, d, z):
    bits = dp.bit_length() - 1
    parts = [x] + [
        lax.ppermute(x, "tensor", [(i, (i + s) % tensor) for i in range(tensor)]) for s in range(1, tensor)
    ]
    around = jnp.stack(parts)
    order = (z - jnp.arange(tensor)) % tensor
    rows = x.shape[0]
    halves = []
    for part, seq in ((0, list(range(1, bits))), (1, list(range(bits - 1, 0, -1)))):
        cur = around[None, :, part * rows // 2:(part + 1) * rows // 2]
        rel = [0]
        for bit in seq + [0]:
            cur = jnp.concatenate([cur, lax.ppermute(cur, "dp", flip_bit(dp, bit))])
            rel = rel + [r ^ (1 << bit) for r in rel]
        place = jnp.argsort(jnp.array(rel))
        halves.append((cur, place))
    return halves, order


def place_kernel(ta_ref, tb_ref, ts_ref, a_ref, b_ref, *outs, widths):
    half = a_ref.shape[2]
    start = 0
    for o, w in zip(outs, widths):
        o[0:half, :] = a_ref[0, 0, :, start:start + w]
        o[half:, :] = b_ref[0, 0, :, start:start + w]
        start += w


def full_weights(x, widths, dp, tensor, d, z):
    rows = x.shape[0]
    if rows % 16:
        g = lax.all_gather(x, BOTH, axis=0).reshape(dp, tensor, rows, x.shape[1])
        outs, start = [], 0
        for w in widths:
            outs.append(g[:, :, :, start:start + w].transpose(0, 2, 1, 3).reshape(dp * rows, tensor * w))
            start += w
        return outs
    ((a, pa), (b, pb)), _ = gather_weights(x, dp, tensor, d, z)
    who = jnp.arange(dp)
    ta, tb = pa[who ^ d].astype(jnp.int32), pb[who ^ d].astype(jnp.int32)
    ts = ((z - jnp.arange(tensor)) % tensor).astype(jnp.int32)
    total = x.shape[1]
    return pl.pallas_call(
        functools.partial(place_kernel, widths=widths),
        grid_spec=pltpu.PrefetchScalarGridSpec(
            num_scalar_prefetch=3,
            grid=(dp, tensor),
            in_specs=[
                pl.BlockSpec((1, 1, rows // 2, total), lambda i, j, ta, tb, ts: (ta[i], ts[j], 0, 0)),
                pl.BlockSpec((1, 1, rows // 2, total), lambda i, j, ta, tb, ts: (tb[i], ts[j], 0, 0)),
            ],
            out_specs=[pl.BlockSpec((rows, w), lambda i, j, ta, tb, ts: (i, j)) for w in widths],
        ),
        out_shape=[jax.ShapeDtypeStruct((dp * rows, tensor * w), F32) for w in widths],
        cost_estimate=pl.CostEstimate(flops=0, bytes_accessed=8 * dp * tensor * rows * total, transcendentals=0),
        name="place_weights",
    )(ta, tb, ts, a, b)


def pick(x, axis, index):
    return lax.dynamic_index_in_dim(x, index, axis, keepdims=False)


def pack_grads(mats, dp, tensor):
    parts = []
    for m in mats:
        r, w = m.shape[0] // dp, m.shape[1] // tensor
        parts.append(m.reshape(dp, r, tensor, w).transpose(0, 2, 1, 3))
    return jnp.concatenate(parts, axis=3)


def sum_columns(part, dp, tensor, d, z):
    bits = dp.bit_length() - 1
    rows, width = part.shape[2:]
    halves = []
    for which, seq in ((0, list(range(1, bits))), (1, list(range(bits - 1, 0, -1)))):
        cur = part[:, :, which * rows // 2:(which + 1) * rows // 2]
        left = sorted(range(1, bits), reverse=True)
        cur = cur.reshape((2,) * len(left) + cur.shape[1:])
        for bit in seq:
            axis = left.index(bit)
            mine = (d >> bit) & 1
            sent = lax.ppermute(pick(cur, axis, 1 - mine), "dp", flip_bit(dp, bit))
            cur = pick(cur, axis, mine) + sent
            left.remove(bit)
        halves.append(cur)
    cur = jnp.concatenate(halves, axis=1)
    total = pick(cur, 0, z)
    for s in range(1, tensor):
        total = total + lax.ppermute(
            pick(cur, 0, (z + s) % tensor), "tensor", [(i, (i + s) % tensor) for i in range(tensor)]
        )
    return total


def reduce_grads(mats, dp, tensor, d, z):
    part = pack_grads(mats, dp, tensor)
    if part.shape[2] % 16:
        flat = part.reshape((dp * tensor,) + part.shape[2:])
        return lax.psum_scatter(flat, BOTH, scatter_dimension=0, tiled=False)
    part = part.reshape((dp // 2, 2) + part.shape[1:])
    mine = pick(part, 1, d % 2) + swap(pick(part, 1, 1 - d % 2), dp)
    return sum_columns(mine, dp, tensor, d, z)


def reduce_head_grads(mats, dp, tensor, d, z):
    part = pack_grads(mats, dp, tensor // 2)
    k = d % 2
    if part.shape[2] % 16:
        none = jnp.zeros_like(part)
        full = jnp.where(k == 0, jnp.concatenate([part, none], 1), jnp.concatenate([none, part], 1))
        flat = full.reshape((dp * tensor,) + part.shape[2:])
        return lax.psum_scatter(flat, BOTH, scatter_dimension=0, tiled=False)
    part = part.reshape((dp // 2, 2) + part.shape[1:])
    mine, other = pick(part, 1, k), swap(pick(part, 1, 1 - k), dp)
    joined = jnp.where(k == 0, jnp.concatenate([mine, other], 1), jnp.concatenate([other, mine], 1))
    return sum_columns(joined, dp, tensor, d, z)


def on_device(
    inputs, memory, lengths, parent, self_qkv, self_out, cross_q, cross_kv, cross_out,
    ff_in, ff_bias_in, ff_out, ff_bias_out, cotangent,
):
    dp, tensor = lax.axis_size("dp"), lax.axis_size("tensor")
    d, z = lax.axis_index("dp"), lax.axis_index("tensor")
    k = d % 2
    routes = item_routes(dp, tensor)
    rows = inputs.shape[2] * 2
    width = inputs.shape[3]
    heads_wide = width // 2
    hw = self_qkv.shape[2]

    x = scatter_items(inputs[:, 0], routes, z)
    x_all = both_cores(x, swap(x, dp), k)
    qkv_w = full_weights(
        jnp.concatenate([self_qkv[0], self_qkv[1], self_qkv[2]], axis=1), [hw] * 3, dp, tensor, d, z
    )
    own_w = [lax.dynamic_slice_in_dim(w, k * heads_wide, heads_wide, 1) for w in qkv_w]
    out_t, cq, ck, cv, cross_out_t = full_weights(
        jnp.concatenate([self_out.T, cross_q, cross_kv[0], cross_kv[1], cross_out.T], axis=1),
        [hw] * 5, dp, tensor, d, z,
    )
    mem = scatter_items(memory[:, 0], routes, z)
    mem_all = both_cores(mem, swap(mem, dp), k)
    w_in, w_out_t = full_weights(jnp.concatenate([ff_in, ff_out.T], axis=1), [ff_in.shape[1]] * 2, dp, tensor, d, z)
    bias_in = lax.all_gather(ff_bias_in, "tensor", axis=0, tiled=True)
    g = scatter_items(cotangent[:, 0], routes, z)

    other_len, other_par = swap(lengths, dp), swap(parent, dp)
    tree = z % 2
    my_len = jnp.where(tree == k, lengths[:, 0], other_len[:, 0])[z // 2]
    my_par = jnp.where(tree == k, parent[:, 0], other_par[:, 0])[z // 2]
    qaux, kaux = tree_aux(my_len, my_par, 2 * rows)

    q, key, val = (mm(x_all, w) for w in own_w)
    attn, lse = attn_fwd(q, key, val, qaux, kaux, True)
    mine = lax.dynamic_slice_in_dim(attn, k * rows, rows)
    other = swap(lax.dynamic_slice_in_dim(attn, (1 - k) * rows, rows), dp)
    attn_rows = jnp.where(k == 0, jnp.concatenate([mine, other], 1), jnp.concatenate([other, mine], 1))

    h1 = x + mm(attn_rows, out_t, NT)
    q2 = mm(h1, cq)
    k2, v2 = mm(mem_all, ck), mm(mem_all, cv)
    ctx, lse2 = attn_fwd(q2, k2, v2, qaux, kaux, False)
    h2 = h1 + mm(ctx, cross_out_t, NT)
    u = mm(h2, w_in) + bias_in
    cdf = 0.5 * (1.0 + lax.erf(u * ROOT_HALF))
    act = u * cdf
    output = h2 + mm(act, w_out_t, NT) + ff_bias_out
    du = mm(g, w_out_t) * (cdf + u * NORMAL_PEAK * jnp.exp(-0.5 * u * u))
    grad_out_t = mm(g, act, TN)
    grad_in = mm(h2, du, TN)
    grad_bias = jnp.concatenate([jnp.sum(du, axis=0), jnp.sum(g, axis=0)])
    dh2 = g + mm(du, w_in, NT)
    dctx = mm(dh2, cross_out_t)
    grad_cross_out_t = mm(dh2, ctx, TN)
    heads = width // HEAD
    pick_heads = (jnp.arange(width)[None, :] // HEAD == jnp.arange(heads)[:, None]).astype(F32)

    def deltas(a, b):
        prod = a * b
        n = prod.shape[1] // HEAD
        return lax.dot_general(
            pick_heads[:n, :prod.shape[1]], prod, NT, precision=lax.Precision.HIGHEST
        ).reshape(n // 2, 2, prod.shape[0])

    dq2, dk2, dv2 = attn_bwd(q2, k2, v2, dctx, lse2, deltas(dctx, ctx), qaux, kaux, False)
    grad_cross_q = mm(h1, dq2, TN)
    grad_ck, grad_cv = mm(mem_all, dk2, TN), mm(mem_all, dv2, TN)
    mem_part = mm(dk2, ck, NT) + mm(dv2, cv, NT)
    mem_rows = mem_part.shape[0] // 2
    grad_mem = lax.dynamic_slice_in_dim(mem_part, k * mem_rows, mem_rows) + swap(
        lax.dynamic_slice_in_dim(mem_part, (1 - k) * mem_rows, mem_rows), dp
    )
    dh1 = dh2 + mm(dq2, cq, NT)
    dattn_rows = mm(dh1, out_t)
    grad_self_out_t = mm(dh1, attn_rows, TN)
    mine = lax.dynamic_slice_in_dim(dattn_rows, k * heads_wide, heads_wide, 1)
    other = swap(lax.dynamic_slice_in_dim(dattn_rows, (1 - k) * heads_wide, heads_wide, 1), dp)
    dattn = both_cores(mine, other, k)
    dq, dk, dv = attn_bwd(q, key, val, dattn, lse, deltas(dattn, attn), qaux, kaux, True)
    part = mm(dq, own_w[0], NT) + mm(dk, own_w[1], NT) + mm(dv, own_w[2], NT)
    dx = (
        dh1
        + lax.dynamic_slice_in_dim(part, k * rows, rows)
        + swap(lax.dynamic_slice_in_dim(part, (1 - k) * rows, rows), dp)
    )
    grad_qkv = [mm(x_all, t, TN) for t in (dq, dk, dv)]

    ff = reduce_grads([grad_in, grad_out_t], dp, tensor, d, z)
    mid = reduce_grads([grad_self_out_t, grad_cross_q, grad_ck, grad_cv, grad_cross_out_t], dp, tensor, d, z)
    att = reduce_head_grads(grad_qkv, dp, tensor, d, z)
    grad_bias = lax.psum(grad_bias, BOTH)
    fw = ff_in.shape[1]
    out_rows = return_items(output, routes, z)
    grad_x = return_items(dx, routes, z)
    grad_m = return_items(grad_mem, routes, z)
    return (
        out_rows[:, None],
        grad_x[:, None],
        grad_m[:, None],
        jnp.stack([att[:, i * hw:(i + 1) * hw] for i in range(3)]),
        mid[:, 0:hw].T,
        mid[:, hw:2 * hw],
        jnp.stack([mid[:, 2 * hw:3 * hw], mid[:, 3 * hw:4 * hw]]),
        mid[:, 4 * hw:5 * hw].T,
        ff[:, :fw],
        lax.dynamic_slice_in_dim(grad_bias, z * fw, fw),
        ff[:, fw:].T,
        grad_bias[tensor * fw:],
    )


def solution(mesh):
    rows4 = P(None, "dp", "tensor", None)
    col3, row2, col2 = P(None, "dp", "tensor"), P("tensor", "dp"), P("dp", "tensor")
    idx = P(None, "dp", None)
    return jax.shard_map(
        on_device,
        mesh=mesh,
        in_specs=(rows4, rows4, idx, idx, col3, row2, col2, col3, row2, col2, P("tensor"), row2, P(), rows4),
        out_specs=(rows4, rows4, rows4, col3, row2, col2, col3, row2, col2, P("tensor"), row2, P()),
        check_vma=False,
    )
```

time: 2210 us -> 904 us (0.41)
  waiting for transfers between devices: 1220 us -> 162 us
  matrix products: 706 us -> 147 us
  Pallas kernels: 0 us -> 248 us
  starting transfers between devices: 2.74 us -> 141 us
  blocking collectives: 152 us -> 53.8 us
  local copies, waits for them, and re-layouts: 24.2 us -> 75.8 us
    reduce_scatter x19 -> x0, waiting for transfers between devices: 739 us -> none  [the longest x10 385 us: narrow(): return lax.psum_scatter(terms, 'tensor', scatter_dimension=0, tiled=True)]
    dot_general x252 -> x32, matrix products: 706 us -> 147 us  [the longest x30 145 us: mm(): lax.dot_general(a, b, dims, precision=HIGH, preferred_element_type=F32)]
    all_gather x14 -> x0, waiting for transfers between devices: 474 us -> none  [the longest x10 406 us: widen_rows(): return lax.all_gather(rows, 'tensor', axis=0, tiled=True)]
    pallas_call x0 -> x7, Pallas kernels: none -> 248 us  [the longest x2 123 us: attn_bwd(): pl.pallas_call(functools.partial(attn_bwd_kernel, causal=causal, qb=qb, k...]
    ppermute x0 -> x71, waiting for transfers between devices: none -> 162 us  [the longest x3 53.8 us: return_items(): lax.ppermute(lax.dynamic_slice_in_dim(rows, (1 - b) * half, half), BOTH,...]
    ppermute x0 -> x71, starting transfers between devices: none -> 141 us  [the longest x18 65.4 us: gather_weights(): cur = jnp.concatenate([cur, lax.ppermute(cur, 'dp', flip_bit(dp, bit))])]
    all_gather x7 -> x1, blocking collectives: 94.3 us -> 11.9 us  [on_device(): bias_in = lax.all_gather(ff_bias_in, 'tensor', axis=0, tiled=True)]
    concatenate x4 -> x21, other arithmetic: 0.39 us -> 38.2 us  [the longest x18 27.4 us: gather_weights(): cur = jnp.concatenate([cur, lax.ppermute(cur, 'dp', flip_bit(dp, bit))])]
  transfers between devices with their start and end apart: 34 -> 71, of which waited for: 23 -> 20; matrix products, arithmetic and copies ran while one was open for 36% -> 19% of each run, Pallas kernels for 0% -> 23%
where the time goes in v1:
time: 904 us; the launch traced here: 894 us
  Pallas kernels  248 us (27%)
  waiting for transfers between devices  162 us (18%)
  matrix products  147 us (16%)
  starting transfers between devices  141 us (16%)
  local copies, waits for them, and re-layouts  75.8 us (8%)
  other arithmetic  64.5 us (7%)
  blocking collectives  53.8 us (6%)
    dot_general x30, matrix products, mm(): lax.dot_general(a, b, dims, precision=HIGH, preferred_element_type=F32)  145 us
    pallas_call x2, Pallas kernels, attn_bwd(): pl.pallas_call(functools.partial(attn_bwd_kernel, causal=causal, qb=qb, k...  123 us
    pallas_call x2, Pallas kernels, attn_fwd(): pl.pallas_call(functools.partial(attn_fwd_kernel, causal=causal, qb=qb, k...  66.9 us
    ppermute x18, starting transfers between devices, gather_weights(): cur = jnp.concatenate([cur, lax.ppermute(cur, 'dp', flip_bit(dp, bit))])  65.4 us
    pallas_call x3, Pallas kernels, full_weights(): pl.pallas_call(functools.partial(place_kernel, widths=widths), grid_spec=...  57.8 us
    ppermute x3, waiting for transfers between devices, return_items(): lax.ppermute(lax.dynamic_slice_in_dim(rows, (1 - b) * half, half), BOTH,...  53.8 us
    ppermute x12, waiting for transfers between devices, sum_columns(): sent = lax.ppermute(pick(cur, axis, 1 - mine), 'dp', flip_bit(dp, bit))  51.3 us
    psum x1, blocking collectives, on_device(): grad_bias = lax.psum(grad_bias, BOTH)  42 us
  transfers between devices with their start and end apart: 71, of which 20 were waited for; matrix products, arithmetic and copies ran while one was open for 19% of the time, Pallas kernels for 23%

profile of v1, /device:TPU:0, one launch (start us, length us, event | category | flops | bytes accessed | tf_op | source)
XLA Modules:
  0.0 894.1 jit_solution(16680405916979345269)
XLA Ops:
  19.2 11.9 %all-gather = f32[4,1,512]{2,1,0:T(1,128)S(1)} all-gather(f32[1,1,512]{2,1,0:T(1,128)S(1)} %bitcast.297), channel_id=1, replica_groups=mesh['dp'=8,'tensor'=4] {'tensor'}, dimensions={0}, use_global_device_ids=true | all-gather | bytes 10240 | tf_op jit(solution)/shard_map/all_gather | solution.py:484
  44.9 14.3 %collective-permute-done.16 = f32[64,640]{1,0:T(8,128)S(1)} collective-permute-done((f32[64,640]{1,0:T(8,128)S(1)}, f32[64,640]{1,0:T(8,128)S(1)}, u32[]{:S(2)}, u32[]{:S(2)}) %collective-permute-start.16) | collective-permute-done | bytes 163872 | tf_op jit(solution)/shard_map/ppermute | solution.py:341
  76.8 10.9 %collective-permute-done.6 = f32[1,4,32,384]{3,2,1,0:T(8,128)S(1)} collective-permute-done((f32[1,4,32,384]{3,2,1,0:T(8,128)S(1)}, f32[1,4,32,384]{3,2,1,0:T(8,128)S(1)}, u32[]{:S(2)}, u32[]{:S(2)}) %collective-permute-start.6) | collective-permute-done | bytes 196640 | tf_op jit(solution)/shard_map/ppermute | solution.py:351
  96.8 11.3 %collective-permute-done.7 = f32[2,4,32,384]{3,2,1,0:T(8,128)S(1)} collective-permute-done((f32[2,4,32,384]{3,2,1,0:T(8,128)S(1)}, f32[2,4,32,384]{3,2,1,0:T(8,128)S(1)}, u32[]{:S(2)}, u32[]{:S(2)}) %collective-permute-start.7) | collective-permute-done | bytes 393248 | tf_op jit(solution)/shard_map/ppermute | solution.py:351
  111.8 9.9 %collective-permute-start.11 = (f32[4,4,32,384]{3,2,1,0:T(8,128)S(1)}, f32[4,4,32,384]{3,2,1,0:T(8,128)S(1)}, u32[]{:S(2)}, u32[]{:S(2)}) collective-permute-start(f32[4,4,32,384]{3,2,1,0:T(8,128)S(1)} %pad_maximum_fusion.16), channel_id=1, source_target_pairs={{0,4},{4,0},{8,12},{12,8},{16,20},{20,16},{24,28},{28,24},{1,5},{5... | collective-permute-start | bytes 2359304 | tf_op jit(solution)/shard_map/ppermute | solution.py:351
  127.4 37.2 %collective-permute-start.8 = (f32[4,4,32,384]{3,2,1,0:T(8,128)S(1)}, f32[4,4,32,384]{3,2,1,0:T(8,128)S(1)}, u32[]{:S(2)}, u32[]{:S(2)}) collective-permute-start(f32[4,4,32,384]{3,2,1,0:T(8,128)S(1)} %pad_maximum_fusion.15), channel_id=1, source_target_pairs={{0,4},{4,0},{8,12},{12,8},{16,20},{20,16},{24,28},{28,24},{1,5},{5... | collective-permute-start | bytes 2359304 | tf_op jit(solution)/shard_map/ppermute | solution.py:351
  175.3 17.5 %place_weights.3 = (f32[512,512]{1,0:T(8,128)}, f32[512,512]{1,0:T(8,128)}, f32[512,512]{1,0:T(8,128)}) custom-call(s32[8]{0:T(128)} %gather_fusion, s32[8]{0:T(128)} %gather_fusion.1, s32[4]{0:T(128)} %and_select_fusion.ts_ref, f32[8,4,32,384]{3,2,1,0:T(8,128)} %pad_maximum_fusion.7.a_ref, f32[8,4,32,384]{3,2,1,0:T(8,128)} %pad_maximum_fusion.8.b_ref), custom_call_target="tpu_custom_call" | custom-call | bytes 6291456 | tf_op jit(solution)/shard_map/place_weights/pallas_call | solution.py:381
  217.7 52.3 %attn_fwd.2 = (f32[2048,256]{1,0:T(8,128)S(1)}, f32[2,2,2048]{2,1,0:T(2,128)S(1)}) custom-call(f32[2048,256]{1,0:T(8,128)S(1)} %fusion.26.q_ref, f32[2048,256]{1,0:T(8,128)} %fusion.22.k_ref, f32[2048,256]{1,0:T(8,128)} %fusion.18.v_ref, bf16[2048,128]{1,0:T(8,128)(2,1)S(1)} %get-tuple-element.127.qa_ref, bf16[2048,128]{1,0:T(8,128)(2,1)S(1)} %get-tuple-element.126.ka_ref), custom_call_target="tpu_custom_call" | custom-call | flops 4000000000 | bytes 8388608 | tf_op jit(solution)/shard_map/attn_fwd/pallas_call | solution.py:116
  273.5 19.3 %place_weights.4 = (f32[512,512]{1,0:T(8,128)}, f32[512,512]{1,0:T(8,128)}, f32[512,512]{1,0:T(8,128)}, f32[512,512]{1,0:T(8,128)}, f32[512,512]{1,0:T(8,128)}) custom-call(s32[8]{0:T(128)} %gather_fusion, s32[8]{0:T(128)} %gather_fusion.1, s32[4]{0:T(128)} %and_select_fusion.ts_ref, f32[8,4,32,640]{3,2,1,0:T(8,128)} %pad_maximum_fusion.3.a_ref, ...), custom_call_target="tpu_custom_call" | custom-call | bytes 10485760 | tf_op jit(solution)/shard_map/place_weights/pallas_call | solution.py:381
  306.0 21.0 %place_weights.5 = (f32[512,2048]{1,0:T(8,128)}, f32[512,2048]{1,0:T(8,128)}) custom-call(s32[8]{0:T(128)} %gather_fusion, s32[8]{0:T(128)} %gather_fusion.1, s32[4]{0:T(128)} %and_select_fusion.ts_ref, f32[8,4,32,1024]{3,2,1,0:T(8,128)} %pad_maximum_fusion.1.a_ref, f32[8,4,32,1024]{3,2,1,0:T(8,128)} %pad_maximum_fusion.2.b_ref), custom_call_target="tpu_custom_call" | custom-call | bytes 16777216 | tf_op jit(solution)/shard_map/place_weights/pallas_call | solution.py:381
  335.4 14.6 %attn_fwd.3 = (f32[1024,512]{1,0:T(8,128)S(1)}, f32[4,2,1024]{2,1,0:T(2,128)S(1)}) custom-call(f32[1024,512]{1,0:T(8,128)} %fusion.92.q_ref, f32[256,512]{1,0:T(8,128)S(1)} %fusion.82.k_ref, f32[256,512]{1,0:T(8,128)S(1)} %fusion.81.v_ref, bf16[2048,128]{1,0:T(8,128)(2,1)S(1)} %copy-done.5, bf16[2048,128]{1,0:T(8,128)(2,1)S(1)} %copy-done.3), custom_call_target="tpu_custom_call" | custom-call | flops 8000000000 | bytes 8388608 | tf_op jit(solution)/shard_map/attn_fwd/pallas_call | solution.py:116
  352.3 9.0 %fusion.93 = f32[1024,2048]{1,0:T(8,128)} fusion(f32[1024,512]{1,0:T(8,128)S(1)} %convolution_add_fusion.1, f32[512,2048]{1,0:T(8,128)S(1)} %copy-done.19), kind=kOutput, calls=%fused_computation.281 | convolution fusion | flops 6442450944 | bytes 14680064 | tf_op jit(solution)/shard_map/dot_general | solution.py:289
  361.3 13.6 %fusion.91 = (f32[2048]{0:T(1024)S(1)}, f32[1024,2048]{1,0:T(8,128)S(1)}) fusion(f32[1024,2048]{1,0:T(8,128)} %fusion.93, f32[2048]{0:T(1024)S(1)} %bitcast.294, f32[512,2048]{1,0:T(8,128)S(1)} %copy-done.94, f32[512,512]{1,0:T(8,128)S(1)} %copy-done.49, f32[512,512]{1,0:T(8,128)S(1)} %copy-done.46, pred[]{:T(512)S(6)} %eq.143), kind=kOutput, calls=%fused_computation.279 | convolution fusion | flops 6467090432 | bytes 23085056 | tf_op jit(solution)/shard_map/dot_general | solution.py:289
  388.2 26.2 %attn_bwd.2 = (f32[1024,512]{1,0:T(8,128)}, f32[256,512]{1,0:T(8,128)}, f32[256,512]{1,0:T(8,128)}) custom-call(f32[1024,512]{1,0:T(8,128)} %fusion.92.q_ref, f32[256,512]{1,0:T(8,128)} %copy-done, f32[256,512]{1,0:T(8,128)} %copy-done.1, f32[1024,512]{1,0:T(8,128)} %copy-done.23, f32[4,2,1024]{2,1,0:T(2,128)} %copy-done.8, f32[4,2,1024]{2,1,0:T(2,128)} %reshape.367.d_ref, ...), custom_call_target="tpu_custom_call" | custom-call | flops 20000000000 | bytes 16777216 | tf_op jit(solution)/shard_map/attn_bwd/pallas_call | solution.py:248
  422.4 10.9 %fusion.99 = f32[512,2048]{1,0:T(8,128)} fusion(f32[1024,512]{1,0:T(8,128)S(1)} %copy-done.15, f32[1024,2048]{1,0:T(8,128)} %copy-done.9), kind=kOutput, calls=%fused_computation.287 | convolution fusion | flops 6442450944 | bytes 14680064 | tf_op jit(solution)/shard_map/dot_general | solution.py:289
  433.4 9.1 %add_add_fusion.2 = f32[1024,512]{1,0:T(8,128)} fusion(f32[1024,512]{1,0:T(8,128)S(1)} %copy-done.15, f32[512,2048]{1,0:T(8,128)S(1)} %copy-done.95, f32[1024,2048]{1,0:T(8,128)S(1)} %bitcast.261, f32[2048]{0:T(1024)S(1)} %bitcast.295, f32[512]{0:T(512)S(1)} %copy-done.96), kind=kOutput, calls=%fused_computation.37 | convolution fusion | flops 6453985280 | bytes 16787456 | tf_op jit(solution)/shard_map/dot_general | solution.py:289
  442.5 9.7 %fusion.5 = f32[512,2048]{1,0:T(8,128)} fusion(f32[1024,2048]{1,0:T(8,128)S(1)} %bitcast.261, f32[2048]{0:T(1024)S(1)} %bitcast.296, f32[512,512]{1,0:T(8,128)S(1)} %copy-done.50, f32[512,512]{1,0:T(8,128)S(1)} %copy-done.47, pred[]{:T(512)S(6)} %eq.143), kind=kOutput, calls=%fused_computation.17 | convolution fusion | flops 6454509568 | bytes 14688257 | tf_op jit(solution)/shard_map/dot_general | solution.py:289
  497.0 9.8 %pad_maximum_fusion = f32[8,4,64,1024]{3,1,2,0:T(4,128)} fusion(f32[8,4,64,512]{3,1,2,0:T(4,128)} %bitcast.258, f32[8,4,64,512]{3,1,2,0:T(4,128)} %bitcast.259), kind=kLoop, calls=%fused_computation.7 | loop fusion | flops 2097152 | bytes 16777216 | tf_op jit(solution)/shard_map/concatenate | solution.py:407
  531.2 42.0 %psum.7 = f32[2560]{0:T(1024)S(1)} all-reduce(f32[2560]{0:T(1024)S(1)} %pad_maximum_fusion.27), channel_id=1, replica_groups=mesh['dp'=8,'tensor'=4] {'dp','tensor'}, use_global_device_ids=true, to_apply=%region_12.13 | all-reduce | flops 2560 | bytes 20480 | tf_op jit(solution)/shard_map/psum | solution.py:551
  579.9 97.2 %attn_bwd.3 = (f32[2048,256]{1,0:T(8,128)}, f32[2048,256]{1,0:T(8,128)}, f32[2048,256]{1,0:T(8,128)}) custom-call(f32[2048,256]{1,0:T(8,128)} %copy-done.6, f32[2048,256]{1,0:T(8,128)} %fusion.22.k_ref, f32[2048,256]{1,0:T(8,128)} %fusion.18.v_ref, f32[2048,256]{1,0:T(8,128)} %copy-done.22, f32[2,2,2048]{2,1,0:T(2,128)} %copy-done.7, ...), custom_call_target="tpu_custom_call" | custom-call | flops 10000000000 | bytes 16777216 | tf_op jit(solution)/shard_map/attn_bwd/pallas_call | solution.py:248
  739.9 11.3 %collective-permute-start.52 = (f32[64,384]{1,0:T(8,128)S(1)}, f32[64,384]{1,0:T(8,128)S(1)}, u32[]{:S(2)}, u32[]{:S(2)}) collective-permute-start(f32[64,384]{1,0:T(8,128)S(1)} %get-tuple-element.98), channel_id=1, source_target_pairs={{0,1},{1,2},{2,3},{3,0},{4,5},{5,6},{6,7},{7,4},{8,9},{9,10},{10,1... | collective-permute-start | bytes 294920 | tf_op jit(solution)/shard_map/ppermute | solution.py:428
  751.9 24.5 %collective-permute-done.37 = f32[512,512]{1,0:T(8,128)S(1)} collective-permute-done((f32[512,512]{1,0:T(8,128)S(1)}, f32[512,512]{1,0:T(8,128)S(1)}, u32[]{:S(2)}, u32[]{:S(2)}) %collective-permute-start.37) | collective-permute-done | bytes 1048608 | tf_op jit(solution)/shard_map/ppermute | solution.py:321
  809.9 22.2 %collective-permute-done.57 = f32[4,32,640]{2,1,0:T(8,128)S(1)} collective-permute-done((f32[4,32,640]{2,1,0:T(8,128)S(1)}, f32[4,32,640]{2,1,0:T(8,128)S(1)}, u32[]{:S(2)}, u32[]{:S(2)}) %collective-permute-start.57) | collective-permute-done | bytes 327712 | tf_op jit(solution)/shard_map/ppermute | solution.py:421
  865.9 24.4 %collective-permute-done.43 = f32[512,512]{1,0:T(8,128)S(1)} collective-permute-done((f32[512,512]{1,0:T(8,128)S(1)}, f32[512,512]{1,0:T(8,128)S(1)}, u32[]{:S(2)}, u32[]{:S(2)}) %collective-permute-start.43) | collective-permute-done | bytes 1048608 | tf_op jit(solution)/shard_map/ppermute | solution.py:321
  (496 shorter events, 361.5 us)
Async XLA Ops:
  2.3 35.0 %collective-permute-start.4 = (f32[64,384]{1,0:T(8,128)}, f32[64,384]{1,0:T(8,128)}, u32[]{:S(2)}, u32[]{:S(2)}) collective-permute-start(f32[64,384]{1,0:T(8,128)} %get-tuple-element.120), channel_id=1, source_target_pairs={{0,2},{1,3},{2,0},{3,1},{4,6},{5,7},{6,4},{7,5},{8,10},{9,11},{10,... | collective-permute-start | bytes 294920 | tf_op jit(solution)/shard_map/ppermute | solution.py:341
  70.7 41.0 %collective-permute-start = (f32[512,512]{1,0:T(8,128)S(1)}, f32[512,512]{1,0:T(8,128)S(1)}, u32[]{:S(2)}, u32[]{:S(2)}) collective-permute-start(f32[512,512]{1,0:T(8,128)S(1)} %copy-done.75), channel_id=1, source_target_pairs={{0,0},{1,2},{2,4},{3,6},{4,1},{5,3},{6,5},{7,7},{8,8},{9,10},{10,1... | collective-permute-start | bytes 3145736 | tf_op jit(solution)/shard_map/ppermute | solution.py:310
  87.7 34.0 %collective-permute-start.1 = (f32[512,512]{1,0:T(8,128)S(1)}, f32[512,512]{1,0:T(8,128)S(1)}, u32[]{:S(2)}, u32[]{:S(2)}) collective-permute-start(f32[512,512]{1,0:T(8,128)S(1)} %copy-done.74), channel_id=1, source_target_pairs={{0,2},{1,0},{2,6},{3,4},{4,3},{5,1},{6,7},{7,5},{8,10},{9,8},{10,1... | collective-permute-start | bytes 3145736 | tf_op jit(solution)/shard_map/ppermute | solution.py:311
  111.6 53.1 %collective-permute-start.39 = (f32[512,512]{1,0:T(8,128)S(1)}, f32[512,512]{1,0:T(8,128)S(1)}, u32[]{:S(2)}, u32[]{:S(2)}) collective-permute-start(f32[512,512]{1,0:T(8,128)S(1)} %get-tuple-element.77), channel_id=1, source_target_pairs={{0,2},{1,0},{2,6},{3,4},{4,3},{5,1},{6,7},{7,5},{8,10},{9,8},{10,1... | collective-permute-start | bytes 3145736 | tf_op jit(solution)/shard_map/ppermute | solution.py:311
  111.8 55.9 %collective-permute-start.11 = (f32[4,4,32,384]{3,2,1,0:T(8,128)S(1)}, f32[4,4,32,384]{3,2,1,0:T(8,128)S(1)}, u32[]{:S(2)}, u32[]{:S(2)}) collective-permute-start(f32[4,4,32,384]{3,2,1,0:T(8,128)S(1)} %pad_maximum_fusion.16), channel_id=1, source_target_pairs={{0,4},{4,0},{8,12},{12,8},{16,20},{20,16},{24,28},{28,24},{1,5},{5... | collective-permute-start | bytes 2359304 | tf_op jit(solution)/shard_map/ppermute | solution.py:351
  121.8 44.4 %collective-permute-start.19 = (f32[2,4,32,640]{3,2,1,0:T(8,128)S(1)}, f32[2,4,32,640]{3,2,1,0:T(8,128)S(1)}, u32[]{:S(2)}, u32[]{:S(2)}) collective-permute-start(f32[2,4,32,640]{3,2,1,0:T(8,128)S(1)} %pad_maximum_fusion.18), channel_id=1, source_target_pairs={{0,16},{4,20},{8,24},{12,28},{16,0},{20,4},{24,8},{28,12},{1,17},{... | collective-permute-start | bytes 1966088 | tf_op jit(solution)/shard_map/ppermute | solution.py:351
  123.7 79.0 %collective-permute-start.2 = (f32[1024,512]{1,0:T(8,128)S(1)}, f32[1024,512]{1,0:T(8,128)}, u32[]{:S(2)}, u32[]{:S(2)}) collective-permute-start(f32[1024,512]{1,0:T(8,128)S(1)} %maximum_select_fusion.1), channel_id=1, source_target_pairs={{0,4},{4,0},{8,12},{12,8},{16,20},{20,16},{24,28},{28,24},{1,5},{5... | collective-permute-start | bytes 6291464 | tf_op jit(solution)/shard_map/ppermute | solution.py:327
  127.4 46.1 %collective-permute-start.8 = (f32[4,4,32,384]{3,2,1,0:T(8,128)S(1)}, f32[4,4,32,384]{3,2,1,0:T(8,128)S(1)}, u32[]{:S(2)}, u32[]{:S(2)}) collective-permute-start(f32[4,4,32,384]{3,2,1,0:T(8,128)S(1)} %pad_maximum_fusion.15), channel_id=1, source_target_pairs={{0,4},{4,0},{8,12},{12,8},{16,20},{20,16},{24,28},{28,24},{1,5},{5... | collective-permute-start | bytes 2359304 | tf_op jit(solution)/shard_map/ppermute | solution.py:351
  173.5 119.3 %collective-permute-start.26 = (f32[128,512]{1,0:T(8,128)S(1)}, f32[128,512]{1,0:T(8,128)}, u32[]{:S(2)}, u32[]{:S(2)}) collective-permute-start(f32[128,512]{1,0:T(8,128)S(1)} %maximum_select_fusion.11), channel_id=1, source_target_pairs={{0,4},{4,0},{8,12},{12,8},{16,20},{20,16},{24,28},{28,24},{1,5},{5... | collective-permute-start | bytes 786440 | tf_op jit(solution)/shard_map/ppermute | solution.py:327
  192.8 78.9 %collective-permute-start.20 = (f32[4,4,32,640]{3,2,1,0:T(8,128)}, f32[4,4,32,640]{3,2,1,0:T(8,128)S(1)}, u32[]{:S(2)}, u32[]{:S(2)}) collective-permute-start(f32[4,4,32,640]{3,2,1,0:T(8,128)} %pad_maximum_fusion.10), channel_id=1, source_target_pairs={{0,4},{4,0},{8,12},{12,8},{16,20},{20,16},{24,28},{28,24},{1,5},{5... | collective-permute-start | bytes 3932168 | tf_op jit(solution)/shard_map/ppermute | solution.py:351
  196.1 100.8 %collective-permute-start.35 = (f32[4,4,32,1024]{3,2,1,0:T(8,128)}, f32[4,4,32,1024]{3,2,1,0:T(8,128)}, u32[]{:S(2)}, u32[]{:S(2)}) collective-permute-start(f32[4,4,32,1024]{3,2,1,0:T(8,128)} %pad_maximum_fusion.6), channel_id=1, source_target_pairs={{0,4},{4,0},{8,12},{12,8},{16,20},{20,16},{24,28},{28,24},{1,5},{5... | collective-permute-start | bytes 6291464 | tf_op jit(solution)/shard_map/ppermute | solution.py:351
  199.3 102.3 %collective-permute-start.32 = (f32[4,4,32,1024]{3,2,1,0:T(8,128)}, f32[4,4,32,1024]{3,2,1,0:T(8,128)}, u32[]{:S(2)}, u32[]{:S(2)}) collective-permute-start(f32[4,4,32,1024]{3,2,1,0:T(8,128)} %pad_maximum_fusion.5), channel_id=1, source_target_pairs={{0,4},{4,0},{8,12},{12,8},{16,20},{20,16},{24,28},{28,24},{1,5},{5... | collective-permute-start | bytes 6291464 | tf_op jit(solution)/shard_map/ppermute | solution.py:351
  271.5 55.5 %collective-permute-start.14 = (f32[1024,256]{1,0:T(8,128)}, f32[1024,256]{1,0:T(8,128)}, u32[]{:S(2)}, u32[]{:S(2)}) collective-permute-start(f32[1024,256]{1,0:T(8,128)} %get-tuple-element.81), channel_id=1, source_target_pairs={{0,4},{4,0},{8,12},{12,8},{16,20},{20,16},{24,28},{28,24},{1,5},{5... | collective-permute-start | bytes 3145736 | tf_op jit(solution)/shard_map/ppermute | solution.py:327
  479.1 94.7 %collective-permute-start.44 = (f32[128,512]{1,0:T(8,128)}, f32[128,512]{1,0:T(8,128)}, u32[]{:S(2)}, u32[]{:S(2)}) collective-permute-start(f32[128,512]{1,0:T(8,128)} %constant_dynamic-slice_fusion.10), channel_id=1, source_target_pairs={{0,4},{4,0},{8,12},{12,8},{16,20},{20,16},{24,28},{28,24},{1,5},{5... | collective-permute-start | bytes 786440 | tf_op jit(solution)/shard_map/ppermute | solution.py:327
  488.2 86.7 %collective-permute-start.40 = (f32[1024,256]{1,0:T(8,128)}, f32[1024,256]{1,0:T(8,128)}, u32[]{:S(2)}, u32[]{:S(2)}) collective-permute-start(f32[1024,256]{1,0:T(8,128)} %get-tuple-element.75), channel_id=1, source_target_pairs={{0,4},{4,0},{8,12},{12,8},{16,20},{20,16},{24,28},{28,24},{1,5},{5... | collective-permute-start | bytes 3145736 | tf_op jit(solution)/shard_map/ppermute | solution.py:327
  529.1 253.2 %collective-permute-start.55 = (f32[4,4,64,640]{3,2,1,0:T(8,128)}, f32[4,4,64,640]{3,2,1,0:T(8,128)}, u32[]{:S(2)}, u32[]{:S(2)}) collective-permute-start(f32[4,4,64,640]{3,2,1,0:T(8,128)} %bitcast.254), channel_id=1, source_target_pairs={{0,4},{4,0},{8,12},{12,8},{16,20},{20,16},{24,28},{28,24},{1,5},{5... | collective-permute-start | bytes 7864328 | tf_op jit(solution)/shard_map/ppermute | solution.py:327
  529.3 270.5 %collective-permute-start.63 = (f32[4,4,64,1024]{3,2,1,0:T(8,128)}, f32[4,4,64,1024]{3,2,1,0:T(8,128)}, u32[]{:S(2)}, u32[]{:S(2)}) collective-permute-start(f32[4,4,64,1024]{3,2,1,0:T(8,128)} %bitcast.253), channel_id=1, source_target_pairs={{0,4},{4,0},{8,12},{12,8},{16,20},{20,16},{24,28},{28,24},{1,5},{5... | collective-permute-start | bytes 12582920 | tf_op jit(solution)/shard_map/ppermute | solution.py:327
  727.4 49.0 %collective-permute-start.37 = (f32[512,512]{1,0:T(8,128)S(1)}, f32[512,512]{1,0:T(8,128)S(1)}, u32[]{:S(2)}, u32[]{:S(2)}) collective-permute-start(f32[512,512]{1,0:T(8,128)S(1)} %copy-done.76), channel_id=1, source_target_pairs={{2,0},{0,1},{6,2},{4,3},{3,4},{1,5},{7,6},{5,7},{10,8},{8,9},{14,1... | collective-permute-start | bytes 3145736 | tf_op jit(solution)/shard_map/ppermute | solution.py:321
  739.9 49.4 %collective-permute-start.41 = (f32[1024,512]{1,0:T(8,128)S(1)}, f32[1024,512]{1,0:T(8,128)S(1)}, u32[]{:S(2)}, u32[]{:S(2)}) collective-permute-start(f32[1024,512]{1,0:T(8,128)S(1)} %constant_dynamic-slice_fusion.13), channel_id=1, source_target_pairs={{0,4},{4,0},{8,12},{12,8},{16,20},{20,16},{24,28},{28,24},{1,5},{5... | collective-permute-start | bytes 6291464 | tf_op jit(solution)/shard_map/ppermute | solution.py:327
  739.9 36.5 %collective-permute-start.52 = (f32[64,384]{1,0:T(8,128)S(1)}, f32[64,384]{1,0:T(8,128)S(1)}, u32[]{:S(2)}, u32[]{:S(2)}) collective-permute-start(f32[64,384]{1,0:T(8,128)S(1)} %get-tuple-element.98), channel_id=1, source_target_pairs={{0,1},{1,2},{2,3},{3,0},{4,5},{5,6},{6,7},{7,4},{8,9},{9,10},{10,1... | collective-permute-start | bytes 294920 | tf_op jit(solution)/shard_map/ppermute | solution.py:428
  805.1 32.2 %collective-permute-start.66 = (f32[2,4,32,1024]{3,2,1,0:T(8,128)S(1)}, f32[2,4,32,1024]{3,2,1,0:T(8,128)S(1)}, u32[]{:S(2)}, u32[]{:S(2)}) collective-permute-start(f32[2,4,32,1024]{3,2,1,0:T(8,128)S(1)} %dynamic-slice_bitcast_fusion), channel_id=1, source_target_pairs={{0,16},{4,20},{8,24},{12,28},{16,0},{20,4},{24,8},{28,12},{1,17},{... | collective-permute-start | bytes 3145736 | tf_op jit(solution)/shard_map/ppermute | solution.py:421
  808.0 57.9 %collective-permute-start.42 = (f32[512,512]{1,0:T(8,128)S(1)}, f32[512,512]{1,0:T(8,128)S(1)}, u32[]{:S(2)}, u32[]{:S(2)}) collective-permute-start(f32[512,512]{1,0:T(8,128)S(1)} %get-tuple-element.72), channel_id=1, source_target_pairs={{0,0},{2,1},{4,2},{6,3},{1,4},{3,5},{5,6},{7,7},{8,8},{10,9},{12,1... | collective-permute-start | bytes 3145736 | tf_op jit(solution)/shard_map/ppermute | solution.py:320
  841.8 48.5 %collective-permute-start.43 = (f32[512,512]{1,0:T(8,128)S(1)}, f32[512,512]{1,0:T(8,128)S(1)}, u32[]{:S(2)}, u32[]{:S(2)}) collective-permute-start(f32[512,512]{1,0:T(8,128)S(1)} %get-tuple-element.73), channel_id=1, source_target_pairs={{2,0},{0,1},{6,2},{4,3},{3,4},{1,5},{7,6},{5,7},{10,8},{8,9},{14,1... | collective-permute-start | bytes 3145736 | tf_op jit(solution)/shard_map/ppermute | solution.py:321
  859.0 32.9 %collective-permute-start.68 = (f32[64,1024]{1,0:T(8,128)S(1)}, f32[64,1024]{1,0:T(8,128)S(1)}, u32[]{:S(2)}, u32[]{:S(2)}) collective-permute-start(f32[64,1024]{1,0:T(8,128)S(1)} %get-tuple-element.88), channel_id=1, source_target_pairs={{0,1},{1,2},{2,3},{3,0},{4,5},{5,6},{6,7},{7,4},{8,9},{9,10},{10,1... | collective-permute-start | bytes 786440 | tf_op jit(solution)/shard_map/ppermute | solution.py:428
  (146 other events, 2366.4 us)

commit v2 on v1

v2 whole, which is shorter than its diff:
```python
import functools

import jax
import jax.numpy as jnp
from jax import lax
from jax.experimental import pallas as pl
from jax.experimental.pallas import tpu as pltpu
from jax.sharding import PartitionSpec as P

HEAD = 64
LOG2E = 1.4426950408889634
LN2 = 0.6931471805599453
BF = jnp.bfloat16
F32 = jnp.float32
NT = (((1,), (1,)), ((), ()))
NN = (((1,), (0,)), ((), ()))


def dot(a, b, dims=NN):
    return lax.dot_general(a, b, dims, preferred_element_type=F32)


def split(x):
    hi = x.astype(BF).astype(F32)
    return hi, x - hi


def attn_fwd_kernel(q_ref, k_ref, v_ref, qa_ref, ka_ref, *refs, causal, qb, kb, rq, rk):
    o_ref, l_ref, qs, ks, vt = refs[-5:]
    lane = lax.broadcasted_iota(jnp.int32, (256, 128), 1)
    left = lane < HEAD

    def sel(a, b):
        return jnp.where(left, a, b)

    def build_q(i, _):
        r = pl.ds(pl.multiple_of(i * 256, 256), 256)
        x = q_ref[r, :] * (HEAD ** -0.5 * LOG2E)
        hi, lo = split(x)
        hir, lor = pltpu.roll(hi, HEAD, 1), pltpu.roll(lo, HEAD, 1)
        aux = qa_ref[r, :].astype(F32) if causal else jnp.zeros((256, 128), F32)
        qs[0, r, 0:128] = sel(hi, hir).astype(BF)
        qs[0, r, 128:256] = sel(lo, aux).astype(BF)
        qs[1, r, 0:128] = sel(hir, hi).astype(BF)
        qs[1, r, 128:256] = sel(lor, aux).astype(BF)
        return 0

    def build_k(i, _):
        r = pl.ds(pl.multiple_of(i * 256, 256), 256)
        hi, lo = split(k_ref[r, :])
        hir, lor = pltpu.roll(hi, HEAD, 1), pltpu.roll(lo, HEAD, 1)
        aux = ka_ref[r, :].astype(F32) if causal else jnp.zeros((256, 128), F32)
        ks[0, r, 0:128] = sel(hi, lor).astype(BF)
        ks[0, r, 128:256] = sel(hi, aux).astype(BF)
        ks[1, r, 0:128] = sel(hir, lo).astype(BF)
        ks[1, r, 128:256] = sel(hir, aux).astype(BF)
        hi, lo = split(v_ref[r, :])
        hir, lor = pltpu.roll(hi, HEAD, 1), pltpu.roll(lo, HEAD, 1)
        vt[0, :, r] = sel(hi, lor).T.astype(BF)
        vt[1, :, r] = sel(hir, lo).T.astype(BF)
        return 0

    lax.fori_loop(0, rq // 256, build_q, 0)
    lax.fori_loop(0, rk // 256, build_k, 0)

    def one_q(i, _):
        rows = pl.ds(pl.multiple_of(i * qb, qb), qb)

        def update(state, qh, h, keys, mask):
            m, s, acc = state
            st = dot(ks[h, keys, :], qh, NT)
            if mask is not None:
                kk = lax.broadcasted_iota(jnp.int32, st.shape, 0)
                qq = lax.broadcasted_iota(jnp.int32, st.shape, 1)
                st = jnp.where(kk - qq <= mask, st, -1e30)
            mn = jnp.maximum(m, jnp.max(st, axis=0, keepdims=True))
            p = jnp.exp2(st - mn)
            al = jnp.exp2(m - mn)
            s = s * al + jnp.sum(p, axis=0, keepdims=True)
            ph = p.astype(BF)
            plo = (p - ph.astype(F32)).astype(BF)
            return mn, s, acc * al + dot(vt[h, :, keys], ph) + dot(vt[h, :, keys], plo)

        qh = [qs[h, rows, :] for h in range(2)]

        def step(j, carry):
            keys = pl.ds(pl.multiple_of(j * kb, kb), kb)
            return tuple(update(carry[h], qh[h], h, keys, None) for h in range(2))

        init = (jnp.full((1, qb), -1e30, F32), jnp.zeros((1, qb), F32), jnp.zeros((128, qb), F32))
        carry = (init, init)
        if causal:
            carry = lax.fori_loop(0, i * qb // kb, step, carry)
            sub = qb // 2
            for j in range(2):
                keys = pl.ds(pl.multiple_of(i * qb + j * sub, sub), sub)
                new = []
                for h in range(2):
                    part = tuple(t[:, j * sub:] for t in carry[h])
                    part = update(part, qh[h][j * sub:], h, keys, 0)
                    if j:
                        part = tuple(jnp.concatenate([t[:, :sub], u], axis=1) for t, u in zip(carry[h], part))
                    new.append(part)
                carry = tuple(new)
        else:
            for j in range(rk // kb):
                carry = step(j, carry)
        outs = []
        for h in range(2):
            m, s, acc = carry[h]
            outs.append((acc[0:HEAD] + acc[HEAD:]) / s)
            l_ref[0, h:h + 1, rows] = m + jnp.log2(s)
        o_ref[rows, :] = jnp.concatenate(outs, axis=0).T
        return 0

    lax.fori_loop(0, rq // qb, one_q, 0)


def attn_fwd(q, k, v, qaux, kaux, causal, qb=512, kb=512, deps=()):
    rq, w = q.shape
    rk = k.shape[0]
    pairs = w // 128
    ra = qaux.shape[0]
    qspec = pl.BlockSpec((rq, 128), lambda p: (0, p))
    kspec = pl.BlockSpec((rk, 128), lambda p: (0, p))
    return pl.pallas_call(
        functools.partial(attn_fwd_kernel, causal=causal, qb=qb, kb=kb, rq=rq, rk=rk),
        grid=(pairs,),
        in_specs=[qspec, kspec, kspec,
                  pl.BlockSpec((ra, 128), lambda p: (0, 0)), pl.BlockSpec((ra, 128), lambda p: (0, 0))]
        + [pl.BlockSpec(memory_space=pl.ANY)] * len(deps),
        out_specs=[qspec, pl.BlockSpec((1, 2, rq), lambda p: (p, 0, 0))],
        out_shape=[jax.ShapeDtypeStruct((rq, w), F32), jax.ShapeDtypeStruct((pairs, 2, rq), F32)],
        scratch_shapes=[pltpu.VMEM((2, rq, 256), BF), pltpu.VMEM((2, rk, 256), BF), pltpu.VMEM((2, 128, rk), BF)],
        compiler_params=pltpu.CompilerParams(vmem_limit_bytes=32 << 20),
        cost_estimate=pl.CostEstimate(flops=(int(2e10) if causal else int(4e9)) * pairs, bytes_accessed=rq * w * 16, transcendentals=0),
        name="attn_fwd",
    )(q, k, v, qaux, kaux, *deps)


def attn_bwd_kernel(q_ref, k_ref, v_ref, do_ref, l_ref, d_ref, qa_ref, ka_ref, *refs, causal, qb, kb, rq, rk):
    dq_ref, dk_ref, dv_ref, qs, ks, kt, vs, dos, dka, dva = refs[-10:]
    lane = lax.broadcasted_iota(jnp.int32, (256, 128), 1)
    left = lane < HEAD

    def sel(a, b):
        return jnp.where(left, a, b)

    def build_q(i, _):
        r = pl.ds(pl.multiple_of(i * 256, 256), 256)
        hi, lo = split(q_ref[r, :] * (HEAD ** -0.5 * LOG2E))
        hir, lor = pltpu.roll(hi, HEAD, 1), pltpu.roll(lo, HEAD, 1)
        aux = qa_ref[r, :].astype(F32) if causal else jnp.zeros((256, 128), F32)
        qs[0, r, 0:128] = sel(hi, lor).astype(BF)
        qs[0, r, 128:256] = sel(hi, aux).astype(BF)
        qs[1, r, 0:128] = sel(hir, lo).astype(BF)
        qs[1, r, 128:256] = sel(hir, aux).astype(BF)
        hi, lo = split(do_ref[r, :])
        hir, lor = pltpu.roll(hi, HEAD, 1), pltpu.roll(lo, HEAD, 1)
        zero = jnp.zeros((256, 128), F32)
        dos[0, r, 0:128] = sel(hi, lor).astype(BF)
        dos[0, r, 128:256] = sel(hi, zero).astype(BF)
        dos[1, r, 0:128] = sel(hir, lo).astype(BF)
        dos[1, r, 128:256] = sel(hir, zero).astype(BF)
        return 0

    def build_k(i, _):
        r = pl.ds(pl.multiple_of(i * 256, 256), 256)
        hi, lo = split(k_ref[r, :])
        hir, lor = pltpu.roll(hi, HEAD, 1), pltpu.roll(lo, HEAD, 1)
        aux = ka_ref[r, :].astype(F32) if causal else jnp.zeros((256, 128), F32)
        ks[0, r, 0:128] = sel(hi, hir).astype(BF)
        ks[0, r, 128:256] = sel(lo, aux).astype(BF)
        ks[1, r, 0:128] = sel(hir, hi).astype(BF)
        ks[1, r, 128:256] = sel(lor, aux).astype(BF)
        kt[0, :, r] = sel(hi, lor).T.astype(BF)
        kt[1, :, r] = sel(hir, lo).T.astype(BF)
        hi, lo = split(v_ref[r, :])
        hir, lor = pltpu.roll(hi, HEAD, 1), pltpu.roll(lo, HEAD, 1)
        zero = jnp.zeros((256, 128), F32)
        vs[0, r, 0:128] = sel(hi, hir).astype(BF)
        vs[0, r, 128:256] = sel(lo, zero).astype(BF)
        vs[1, r, 0:128] = sel(hir, hi).astype(BF)
        vs[1, r, 128:256] = sel(lor, zero).astype(BF)
        dka[0, r, :] = zero
        dka[1, r, :] = zero
        dva[0, r, :] = zero
        dva[1, r, :] = zero
        return 0

    lax.fori_loop(0, rq // 256, build_q, 0)
    lax.fori_loop(0, rk // 256, build_k, 0)

    def one_q(i, _):
        rows = pl.ds(pl.multiple_of(i * qb, qb), qb)

        def update(acc, h, keys, cols, mask):
            qh = qs[h, cols, :]
            dh = dos[h, cols, :]
            st = dot(ks[h, keys, :], qh, NT)
            if mask is not None:
                kk = lax.broadcasted_iota(jnp.int32, st.shape, 0)
                qq = lax.broadcasted_iota(jnp.int32, st.shape, 1)
                st = jnp.where(kk - qq <= mask, st, -1e30)
            p = jnp.exp2(st - l_ref[0, h:h + 1, cols])
            ph = p.astype(BF)
            plo = (p - ph.astype(F32)).astype(BF)
            dhl = dh[:, 0:128]
            dva[h, keys, :] += dot(ph, dhl) + dot(plo, dhl)
            dp = dot(vs[h, keys, :], dh, NT)
            ds = p * (dp - d_ref[0, h:h + 1, cols])
            dsh = ds.astype(BF)
            dsl = (ds - dsh.astype(F32)).astype(BF)
            qhl = qh[:, 0:128]
            dka[h, keys, :] += dot(dsh, qhl) + dot(dsl, qhl)
            kth = kt[h, :, keys]
            return acc + dot(kth, dsh) + dot(kth, dsl)

        def step(j, carry):
            keys = pl.ds(pl.multiple_of(j * kb, kb), kb)
            return tuple(update(carry[h], h, keys, rows, None) for h in range(2))

        init = jnp.zeros((128, qb), F32)
        carry = (init, init)
        if causal:
            carry = lax.fori_loop(0, i * qb // kb, step, carry)
            sub = qb // 2
            for j in range(2):
                keys = pl.ds(pl.multiple_of(i * qb + j * sub, sub), sub)
                cols = pl.ds(pl.multiple_of(i * qb + j * sub, sub), qb - j * sub)
                new = []
                for h in range(2):
                    part = update(carry[h][:, j * sub:], h, keys, cols, 0)
                    if j:
                        part = jnp.concatenate([carry[h][:, :sub], part], axis=1)
                    new.append(part)
                carry = tuple(new)
        else:
            for j in range(rk // kb):
                carry = step(j, carry)
        outs = [(a[0:HEAD] + a[HEAD:]) * (HEAD ** -0.5) for a in carry]
        dq_ref[rows, :] = jnp.concatenate(outs, axis=0).T
        return 0

    lax.fori_loop(0, rq // qb, one_q, 0)

    def finish(i, _):
        r = pl.ds(pl.multiple_of(i * 256, 256), 256)
        a, b = dka[0, r, :], dka[1, r, :]
        dk_ref[r, :] = sel(a + pltpu.roll(a, HEAD, 1), b + pltpu.roll(b, HEAD, 1)) * LN2
        a, b = dva[0, r, :], dva[1, r, :]
        dv_ref[r, :] = sel(a + pltpu.roll(a, HEAD, 1), b + pltpu.roll(b, HEAD, 1))
        return 0

    lax.fori_loop(0, rk // 256, finish, 0)


def attn_bwd(q, k, v, do, lse, delta, qaux, kaux, causal, qb=512, kb=512, pair=None, deps=()):
    rq, w = q.shape
    rk = k.shape[0]
    pairs = 1 if pair is not None else w // 128
    first = pair or 0
    ra = qaux.shape[0]
    qspec = pl.BlockSpec((rq, 128), lambda p: (0, p + first))
    kspec = pl.BlockSpec((rk, 128), lambda p: (0, p + first))
    lspec = pl.BlockSpec((1, 2, rq), lambda p: (p + first, 0, 0))
    aspec = pl.BlockSpec((ra, 128), lambda p: (0, 0))
    return pl.pallas_call(
        functools.partial(attn_bwd_kernel, causal=causal, qb=qb, kb=kb, rq=rq, rk=rk),
        grid=(pairs,),
        in_specs=[qspec, kspec, kspec, qspec, lspec, lspec, aspec, aspec]
        + [pl.BlockSpec(memory_space=pl.ANY)] * len(deps),
        out_specs=[pl.BlockSpec((n, 128), lambda p: (0, p)) for n in (rq, rk, rk)],
        out_shape=[jax.ShapeDtypeStruct((n, pairs * 128), F32) for n in (rq, rk, rk)],
        scratch_shapes=[pltpu.VMEM((2, rq, 256), BF), pltpu.VMEM((2, rk, 256), BF), pltpu.VMEM((2, 128, rk), BF),
                        pltpu.VMEM((2, rk, 256), BF), pltpu.VMEM((2, rq, 256), BF),
                        pltpu.VMEM((2, rk, 128), F32), pltpu.VMEM((2, rk, 128), F32)],
        compiler_params=pltpu.CompilerParams(vmem_limit_bytes=40 << 20),
        cost_estimate=pl.CostEstimate(flops=(int(3.4e10) if causal else int(5e9)) * pairs, bytes_accessed=rq * w * 32, transcendentals=0),
        name="attn_bwd",
    )(q, k, v, do, lse, delta, qaux, kaux, *deps)


def tree_aux(lengths, parent, n):
    segs = lengths.shape[0]
    ends = jnp.cumsum(lengths)
    places = jnp.arange(n, dtype=jnp.int32)
    seg = jnp.sum((places[:, None] >= ends[None, :-1]).astype(jnp.int32), axis=1)
    labels = jnp.arange(segs, dtype=jnp.int32)
    onehot = seg[:, None] == labels[None, :]
    up1 = jnp.sum(jnp.where(onehot, parent[None, :], 0), axis=1)
    up2 = jnp.sum(jnp.where(up1[:, None] == labels[None, :], parent[None, :], 0), axis=1)
    lab = jnp.arange(128, dtype=jnp.int32)[None, :] - HEAD
    inside = (lab >= 0) & (lab < segs)
    sg = seg[:, None]
    kaux = jnp.where(inside & (lab == sg), 1.0, 0.0).astype(BF)
    ok = (lab == sg) | ((sg > 0) & ((lab == up1[:, None]) | (lab == up2[:, None])))
    qaux = jnp.where(inside & ~ok, -1e30, 0.0).astype(BF)
    return qaux, kaux


HIGH = lax.Precision.HIGH
TN = (((0,), (0,)), ((), ()))
BOTH = ("dp", "tensor")
ANY = pl.BlockSpec(memory_space=pl.ANY)
VMEM = pl.BlockSpec(memory_space=pltpu.VMEM)
SMEM = pl.BlockSpec(memory_space=pltpu.SMEM)


def mm(a, b, dims=NN):
    return lax.dot_general(a, b, dims, precision=HIGH, preferred_element_type=F32)


def nothing(*refs):
    pass


def after(x, *others):
    return pl.pallas_call(
        nothing,
        in_specs=[ANY] * (1 + len(others)),
        out_specs=ANY,
        out_shape=jax.ShapeDtypeStruct(x.shape, x.dtype),
        input_output_aliases={0: 0},
        name="after",
    )(x, *others)


def flip_bit(size, bit):
    return [(i, i ^ (1 << bit)) for i in range(size)]


def turn(size, by):
    return [(i, (i + by) % size) for i in range(size)]


def pick(x, axis, index):
    return lax.dynamic_index_in_dim(x, index, axis, keepdims=False)


def item_routes(dp, tensor):
    routes = []
    for step in range(2):
        pairs = []
        for c in range(dp // 2):
            for t in range(2):
                for z in range(tensor):
                    b = (z + step) % 2
                    pairs.append(((2 * c + t) * tensor + z, (2 * c + z // 2) * tensor + 2 * b + t))
        routes.append(pairs)
    return routes


def send_items(x, routes, z, *others):
    first, second = pick(x, 0, z % 2), pick(x, 0, 1 - z % 2)
    if others:
        first, second = after(first, *others), after(second, *others)
    return lax.ppermute(first, BOTH, routes[0]), lax.ppermute(second, BOTH, routes[1])


def in_order(first, second, z):
    return jnp.where(z // 2 == 0, jnp.concatenate([first, second]), jnp.concatenate([second, first]))


def return_items(rows, routes, z):
    half = rows.shape[0] // 2
    b = z // 2
    back = [[(t, s) for s, t in r] for r in routes]
    first = lax.ppermute(lax.dynamic_slice_in_dim(rows, b * half, half), BOTH, back[0])
    second = lax.ppermute(lax.dynamic_slice_in_dim(rows, (1 - b) * half, half), BOTH, back[1])
    return first, second


def both_batches(first, second, z):
    return jnp.where(z % 2 == 0, jnp.stack([first, second]), jnp.stack([second, first]))


def swap(x, dp):
    return lax.ppermute(x, "dp", flip_bit(dp, 0))


def both_cores(mine, other, k, axis=0):
    return jnp.where(
        k == 0, jnp.concatenate([mine, other], axis), jnp.concatenate([other, mine], axis)
    )


def rows_kernel(who_ref, a_ref, b_ref, c_ref, d_ref, o_ref):
    k, m = who_ref[0], who_ref[1]
    half = a_ref.shape[0]
    for ref, core, which in ((a_ref, k, m), (b_ref, k, 1 - m), (c_ref, 1 - k, m), (d_ref, 1 - k, 1 - m)):
        o_ref[pl.ds(pl.multiple_of((2 * core + which) * half, half), half), :] = ref[...]


def place_rows(first, second, other_first, other_second, k, z):
    half, width = first.shape
    who = jnp.stack([k, z // 2]).astype(jnp.int32)
    return pl.pallas_call(
        rows_kernel,
        in_specs=[SMEM, VMEM, VMEM, VMEM, VMEM],
        out_specs=VMEM,
        out_shape=jax.ShapeDtypeStruct((4 * half, width), F32),
        compiler_params=pltpu.CompilerParams(vmem_limit_bytes=32 << 20),
        cost_estimate=pl.CostEstimate(flops=0, bytes_accessed=32 * half * width, transcendentals=0),
        name="place_rows",
    )(who, first, second, other_first, other_second)


ROOT_HALF = 0.7071067811865476
NORMAL_PEAK = 0.3989422804014327


def parts2(x):
    hi = x.astype(BF)
    return hi, (x - hi.astype(F32)).astype(BF)


def dot3(a, b, dims=NN):
    return dot(a[0], b[0], dims) + (dot(a[0], b[1], dims) + dot(a[1], b[0], dims))


def ffn_kernel(z_ref, h_ref, g_ref, wi_ref, wo_ref, bo_ref, out_ref, dh_ref, gr_ref,
               hh, hl, gh, gl, hth, htl, gth, gtl, ah, al, dh, dl, *, rb, drows):
    j = pl.program_id(0)
    n = h_ref.shape[0]

    @pl.when(j == 0)
    def _():
        for r in range(n // rb):
            rows = slice(r * rb, (r + 1) * rb)
            for ref, h, l, th, tl in ((h_ref, hh, hl, hth, htl), (g_ref, gh, gl, gth, gtl)):
                x = ref[rows, :]
                h[rows, :], l[rows, :] = parts2(x)
                th[:, rows], tl[:, rows] = parts2(x.T)
            out_ref[rows, :] = h_ref[rows, :] + bo_ref[0:1, :]
            dh_ref[rows, :] = g_ref[rows, :]

    dp = wi_ref.shape[0]
    wide = wi_ref.shape[3]
    wi = parts2(wi_ref[:, 0, 0:drows, :].reshape(dp * drows, wide))
    wo = parts2(wo_ref[:, 0, 0:drows, :].reshape(dp * drows, wide))
    bias = wi_ref[0, 0, drows:drows + 1, :]
    total = jnp.zeros((1, wide), F32)
    for r in range(n // rb):
        rows = slice(r * rb, (r + 1) * rb)
        u = dot3((hh[rows, :], hl[rows, :]), wi) + bias
        gz = dot3((gh[rows, :], gl[rows, :]), wo)
        cdf = 0.5 * (1.0 + lax.erf(u * ROOT_HALF))
        act = u * cdf
        du = gz * (cdf + u * (NORMAL_PEAK * jnp.exp(-0.5 * u * u)))
        total = total + jnp.sum(du, axis=0, keepdims=True)
        act, du = parts2(act), parts2(du)
        ah[rows, :], al[rows, :] = act
        dh[rows, :], dl[rows, :] = du
        out_ref[rows, :] += dot3(act, wo, NT)
        dh_ref[rows, :] += dot3(du, wi, NT)
    gr_ref[:, 0:drows, 0:wide] = dot3((hth[...], htl[...]), (dh[...], dl[...])).reshape(dp, drows, wide)
    gr_ref[:, 0:drows, wide:] = dot3((gth[...], gtl[...]), (ah[...], al[...])).reshape(dp, drows, wide)
    gr_ref[:, drows:drows + 8, :] = jnp.zeros((dp, 8, 2 * wide), F32)
    for i in range(dp):
        gr_ref[i, drows:drows + 1, 0:wide] = total

    for half in range(2):
        @pl.when(j % 2 == half)
        def _():
            bout = jnp.sum(g_ref[:, half * wide:(half + 1) * wide], axis=0, keepdims=True)
            for i in range(dp):
                gr_ref[i, drows + 1:drows + 2, 0:wide] = bout


def ffn(h2, g, ff_all, bias_out, z, drows):
    n, width = h2.shape
    dp, tensor, high, both = ff_all.shape
    wide = both // 4
    steps = 2 * tensor
    full = lambda: pl.BlockSpec((n, width), lambda j, z: (0, 0))
    return pl.pallas_call(
        functools.partial(ffn_kernel, rb=512, drows=drows),
        grid_spec=pltpu.PrefetchScalarGridSpec(
            num_scalar_prefetch=1,
            grid=(steps,),
            in_specs=[
                full(), full(),
                pl.BlockSpec((dp, 1, high, wide), lambda j, z: (0, (z[0] + tensor - j // 2) % tensor, 0, j % 2)),
                pl.BlockSpec((dp, 1, high, wide), lambda j, z: (0, (z[0] + tensor - j // 2) % tensor, 0, 2 + j % 2)),
                pl.BlockSpec((1, width), lambda j, z: (0, 0)),
            ],
            out_specs=[full(), full(), pl.BlockSpec((dp, high, 2 * wide), lambda j, z: (0, 0, j))],
            scratch_shapes=[pltpu.VMEM((n, width), BF)] * 4 + [pltpu.VMEM((width, n), BF)] * 4
            + [pltpu.VMEM((n, wide), BF)] * 4,
        ),
        out_shape=[
            jax.ShapeDtypeStruct((n, width), F32),
            jax.ShapeDtypeStruct((n, width), F32),
            jax.ShapeDtypeStruct((dp, high, 2 * wide * steps), F32),
        ],
        compiler_params=pltpu.CompilerParams(vmem_limit_bytes=48 << 20),
        cost_estimate=pl.CostEstimate(flops=int(5e10), bytes_accessed=30 << 20, transcendentals=0),
        name="ffn",
    )(z[None].astype(jnp.int32), h2, g, ff_all, ff_all, bias_out[None])


def around(x, tensor):
    return [x] + [lax.ppermute(x, "tensor", turn(tensor, s)) for s in range(1, tensor)]


def place_kernel(who_ref, g_ref, *outs, widths, own):
    k, z = who_ref[0], who_ref[1]
    tensor = g_ref.shape[1]
    half = tensor // 2
    for s in range(tensor):
        col = (z + tensor - s) % tensor
        start = 0
        for o, w, only in zip(outs, widths, own):
            def copy(c, o=o, w=w, s=s, start=start):
                o[:, pl.ds(pl.multiple_of(c * w, w), w)] = g_ref[0, s, :, start:start + w]

            if only:
                pl.when(col // half == k)(functools.partial(copy, col % half))
            else:
                copy(col)
            start += w


def place_weights(g, widths, own, k, z):
    dp, tensor, rows, wide = g.shape
    who = jnp.stack([k, z]).astype(jnp.int32)
    cols = [w * (tensor // 2 if o else tensor) for o, w in zip(own, widths)]
    return pl.pallas_call(
        functools.partial(place_kernel, widths=widths, own=own),
        grid=(dp,),
        in_specs=[SMEM, pl.BlockSpec((1, tensor, rows, wide), lambda i: (i, 0, 0, 0))],
        out_specs=[pl.BlockSpec((rows, c), lambda i: (i, 0)) for c in cols],
        out_shape=[jax.ShapeDtypeStruct((dp * rows, c), F32) for c in cols],
        cost_estimate=pl.CostEstimate(flops=0, bytes_accessed=8 * dp * tensor * rows * wide, transcendentals=0),
        name="place_weights",
    )(who, g)


def halve(cur, seq, dp, d):
    left = sorted(seq, reverse=True)
    cur = cur.reshape((2,) * len(left) + cur.shape[1:])
    for bit in seq:
        axis = left.index(bit)
        mine = (d >> bit) & 1
        sent = lax.ppermute(pick(cur, axis, 1 - mine), "dp", flip_bit(dp, bit))
        cur = pick(cur, axis, mine) + sent
        left.remove(bit)
    return cur


def along_z(parts, tensor, z):
    total = parts(z)
    for s in range(1, tensor):
        total = total + lax.ppermute(parts((z + s) % tensor), "tensor", turn(tensor, s))
    return total


def column_block(x, i, tensor):
    w = x.shape[-1] // tensor
    return lax.dynamic_slice_in_dim(x, i * w, w, x.ndim - 1)


def reduce_over_dp(mats, dp, tensor, earlier):
    whole = jnp.concatenate([m.reshape(dp, m.shape[0] // dp, m.shape[1]) for m in mats], axis=2)
    mine = lax.psum_scatter(after(whole, earlier), "dp", scatter_dimension=0, tiled=False)
    blocks, start = [], 0
    for i in range(tensor):
        one, start = [], 0
        for m in mats:
            w = m.shape[1] // tensor
            one.append(mine[:, start + i * w:start + (i + 1) * w])
            start += m.shape[1]
        blocks.append(jnp.concatenate(one, axis=1))
    return jnp.stack(blocks)


def reduce_over_tensor(blocks, widths):
    total = lax.psum_scatter(blocks, "tensor", scatter_dimension=0, tiled=False)
    outs, start = [], 0
    for w in widths:
        outs.append(total[:, start:start + w])
        start += w
    return outs


def reduce_head_grads(mats, dp, tensor, d, z):
    bits = dp.bit_length() - 1
    k = d % 2
    half = tensor // 2
    rows = mats[0].shape[0] // dp
    w = mats[0].shape[1] // half
    split = [m.reshape(dp // 2, 2, rows, half, w) for m in mats]

    def side(i, u):
        return jnp.concatenate([pick(m, 1, i)[:, :, u] for m in split], axis=2)

    chains = []
    for u in range(half):
        seq = list(range(1, bits))
        if u % 2:
            seq = seq[::-1]
        both = jnp.stack([side(k, u), swap(side(1 - k, u), dp)], axis=1)
        chains.append(halve(both, seq, dp, d))
    everything = jnp.stack(chains)

    def parts(i):
        return pick(pick(everything, 0, i % half), 0, (i // half + k) % 2)

    total = along_z(parts, tensor, z)
    return [total[:, i * w:(i + 1) * w] for i in range(len(mats))]


def on_device(
    inputs, memory, lengths, parent, self_qkv, self_out, cross_q, cross_kv, cross_out,
    ff_in, ff_bias_in, ff_out, ff_bias_out, cotangent,
):
    dp, tensor = lax.axis_size("dp"), lax.axis_size("tensor")
    d, z = lax.axis_index("dp"), lax.axis_index("tensor")
    k = d % 2
    routes = item_routes(dp, tensor)
    rows = inputs.shape[2] * 2
    width = inputs.shape[3]
    heads_wide = width // 2
    hw = self_qkv.shape[2]
    fw = ff_in.shape[1]
    drows = ff_in.shape[0]

    shard = jnp.concatenate(
        [self_qkv[0], self_qkv[1], self_qkv[2], self_out.T, cross_q, cross_kv[0], cross_kv[1], cross_out.T], axis=1
    )
    parts = around(shard, tensor)
    x1, x2 = send_items(inputs[:, 0], routes, z, *parts[1:])
    weights = lax.all_gather(jnp.stack(parts), "dp", axis=0)
    wq, wk, wv, out_t, cq, ck, cv, cross_out_t = place_weights(
        weights, [hw] * 8, [True] * 3 + [False] * 5, k, z
    )
    own_w = [wq, wk, wv]

    bias_rows = jnp.concatenate([ff_bias_in[None], jnp.zeros((7, fw), F32)])
    ff_shard = jnp.concatenate(
        [jnp.concatenate([ff_in, ff_out.T], axis=1), jnp.concatenate([bias_rows] * 2, axis=1)]
    )
    ff_parts = around(after(ff_shard, x1, x2), tensor)
    ff_z = jnp.stack(ff_parts)
    ff_all = lax.all_gather(ff_z, "dp", axis=0)
    x_all = place_rows(x1, x2, swap(x1, dp), swap(x2, dp), k, z)
    x = lax.dynamic_slice_in_dim(x_all, k * rows, rows)
    g1, g2 = send_items(cotangent[:, 0], routes, z, ff_z)
    m1, m2 = send_items(memory[:, 0], routes, z, ff_z)
    mem = in_order(m1, m2, z)
    mem_all = both_cores(mem, swap(mem, dp), k)

    paths = jnp.concatenate([lengths[:, 0], parent[:, 0]], axis=1)
    other_paths = swap(paths, dp)
    my_path = pick(jnp.where(z % 2 == k, paths, other_paths), 0, z // 2)
    segs = lengths.shape[2]
    qaux, kaux = tree_aux(my_path[:segs], my_path[segs:], 2 * rows)

    q, key, val = (mm(x_all, w) for w in own_w)
    attn, lse = attn_fwd(q, key, val, qaux, kaux, True, 1024, 1024, deps=(ff_z,))
    mine = lax.dynamic_slice_in_dim(attn, k * rows, rows)
    other = swap(lax.dynamic_slice_in_dim(attn, (1 - k) * rows, rows), dp)
    attn_rows = both_cores(mine, other, k, 1)

    h1 = x + mm(attn_rows, out_t, NT)
    q2 = mm(h1, cq)
    k2, v2 = mm(mem_all, ck), mm(mem_all, cv)
    ctx, lse2 = attn_fwd(q2, k2, v2, qaux, kaux, False, 1024, 256)
    h2 = h1 + mm(ctx, cross_out_t, NT)
    g = in_order(g1, g2, z)
    output, dh2, ff_grads = ffn(h2, g, ff_all, ff_bias_out, z, drows)
    ff_mine = lax.psum_scatter(ff_grads, "dp", scatter_dimension=0, tiled=False)
    ff_blocks = ff_mine.reshape(drows + 8, tensor, 2 * fw).transpose(1, 0, 2)
    dctx = mm(dh2, cross_out_t)
    grad_cross_out_t = mm(dh2, ctx, TN)
    heads = width // HEAD
    pick_heads = (jnp.arange(width)[None, :] // HEAD == jnp.arange(heads)[:, None]).astype(F32)

    def deltas(a, b):
        prod = a * b
        n = prod.shape[1] // HEAD
        return lax.dot_general(
            pick_heads[:n, :prod.shape[1]], prod, NT, precision=lax.Precision.HIGHEST
        ).reshape(n // 2, 2, prod.shape[0])

    dq2, dk2, dv2 = attn_bwd(q2, k2, v2, dctx, lse2, deltas(dctx, ctx), qaux, kaux, False, 1024, 256)
    grad_cross_q = mm(h1, dq2, TN)
    grad_ck, grad_cv = mm(mem_all, dk2, TN), mm(mem_all, dv2, TN)
    mem_part = mm(dk2, ck, NT) + mm(dv2, cv, NT)
    mem_rows = mem_part.shape[0] // 2
    grad_mem = lax.dynamic_slice_in_dim(mem_part, k * mem_rows, mem_rows) + swap(
        lax.dynamic_slice_in_dim(mem_part, (1 - k) * mem_rows, mem_rows), dp
    )
    dh1 = dh2 + mm(dq2, cq, NT)
    dattn_rows = mm(dh1, out_t)
    grad_self_out_t = mm(dh1, attn_rows, TN)
    mine = lax.dynamic_slice_in_dim(dattn_rows, k * heads_wide, heads_wide, 1)
    other = swap(lax.dynamic_slice_in_dim(dattn_rows, (1 - k) * heads_wide, heads_wide, 1), dp)
    dattn = both_cores(mine, other, k)
    mid_blocks = reduce_over_dp(
        [grad_cross_q, grad_ck, grad_cv, grad_cross_out_t, grad_self_out_t], dp, tensor, ff_mine
    )
    out_back = return_items(output, routes, z)
    mem_back = return_items(grad_mem, routes, z)
    delta = deltas(dattn, attn)
    back = []
    for p in range(heads_wide // 128):
        deps = [] if p == 0 else list(out_back) + list(mem_back) + [back[0][0], ff_mine]
        back.append(attn_bwd(q, key, val, dattn, lse, delta, qaux, kaux, True, 1024, 512, pair=p, deps=deps))
    dq, dk, dv = (jnp.concatenate([b[i] for b in back], axis=1) for i in range(3))
    part = mm(dq, own_w[0], NT) + mm(dk, own_w[1], NT) + mm(dv, own_w[2], NT)
    dx = (
        dh1
        + lax.dynamic_slice_in_dim(part, k * rows, rows)
        + swap(lax.dynamic_slice_in_dim(part, (1 - k) * rows, rows), dp)
    )
    dq, dk, dv = (after(t, dx) for t in (dq, dk, dv))
    grad_qkv = [mm(x_all, t, TN) for t in (dq, dk, dv)]

    ff_sum = lax.psum_scatter(ff_blocks, "tensor", scatter_dimension=0, tiled=False)
    ff_sum = ff_sum.reshape(drows + 8, 2, 2, fw // 2)
    grad_ff_in = ff_sum[:drows, :, 0].reshape(drows, fw)
    grad_ff_out = ff_sum[:drows, :, 1].reshape(drows, fw)
    grad_bias_in, grad_bias_out = ff_sum[drows, :, 0].reshape(fw), ff_sum[drows + 1, :, 0].reshape(fw)
    mid_sums = reduce_over_tensor(mid_blocks, [hw] * 5)
    mid_a, mid_b = mid_sums[:3], mid_sums[3:]
    x_back = return_items(dx, routes, z)
    att = reduce_head_grads(grad_qkv, dp, tensor, d, z)
    return (
        both_batches(*out_back, z)[:, None],
        both_batches(*x_back, z)[:, None],
        both_batches(*mem_back, z)[:, None],
        jnp.stack(att),
        mid_b[1].T,
        mid_a[0],
        jnp.stack(mid_a[1:]),
        mid_b[0].T,
        grad_ff_in,
        grad_bias_in,
        grad_ff_out.T,
        grad_bias_out,
    )


def solution(mesh):
    rows4 = P(None, "dp", "tensor", None)
    col3, row2, col2 = P(None, "dp", "tensor"), P("tensor", "dp"), P("dp", "tensor")
    idx = P(None, "dp", None)
    return jax.shard_map(
        on_device,
        mesh=mesh,
        in_specs=(rows4, rows4, idx, idx, col3, row2, col2, col3, row2, col2, P("tensor"), row2, P(), rows4),
        out_specs=(rows4, rows4, rows4, col3, row2, col2, col3, row2, col2, P("tensor"), row2, P()),
        check_vma=False,
    )
```

time: 904 us -> 581 us (0.64)
  Pallas kernels: 248 us -> 168 us
  matrix products: 147 us -> 68.8 us
  waiting for transfers between devices: 162 us -> 99.4 us
  blocking collectives: 53.8 us -> 0 us
  starting transfers between devices: 141 us -> 96.6 us
  other arithmetic: 64.5 us -> 32.7 us
  between operations: 2.47 us -> 15.8 us
  local copies, waits for them, and re-layouts: 75.8 us -> 88.5 us
    dot_general x30 -> x24, matrix products: 145 us -> 66.6 us  [mm(): lax.dot_general(a, b, dims, precision=HIGH, preferred_element_type=F32)]
    ppermute x54 -> x19, starting transfers between devices: 132 us -> 71.6 us  [the longest x6 34.2 us: around(): lax.ppermute(x, 'tensor', turn(tensor, s))]
    pallas_call x2 -> x3, Pallas kernels: 123 us -> 70.8 us  [attn_bwd(): pl.pallas_call(functools.partial(attn_bwd_kernel, causal=causal, qb=qb, k...]
    psum x1 -> x0, blocking collectives: 42 us -> none  [on_device(): grad_bias = lax.psum(grad_bias, BOTH)]
    ppermute x54 -> x19, waiting for transfers between devices: 108 us -> 66.5 us  [the longest x6 34.6 us: around(): lax.ppermute(x, 'tensor', turn(tensor, s))]
    unnamed x210 -> x215, local copies, waits for them, and re-layouts: 20.4 us -> 58.4 us
    concatenate x21 -> x4, other arithmetic: 38.2 us -> 2.43 us  [the longest x2 1.62 us: side(): return jnp.concatenate([pick(m, 1, i)[:, :, u] for m in split], axis=2)]
    pallas_call x2, Pallas kernels: 66.9 us -> 36.8 us  [attn_fwd(): pl.pallas_call(functools.partial(attn_fwd_kernel, causal=causal, qb=qb, k...]
  transfers between devices with their start and end apart: 71 -> 41, of which waited for: 20 -> 8; matrix products, arithmetic and copies ran while one was open for 19% -> 24% of each run, Pallas kernels for 23% -> 21%
where the time goes in v2:
time: 581 us; the launch traced here: 570 us
  Pallas kernels  168 us (29%)
  waiting for transfers between devices  99.4 us (17%)
  starting transfers between devices  96.6 us (17%)
  local copies, waits for them, and re-layouts  88.5 us (15%)
  matrix products  68.8 us (12%)
  other arithmetic  32.7 us (6%)
  between operations  15.8 us (3%)
    pallas_call x3, Pallas kernels, attn_bwd(): pl.pallas_call(functools.partial(attn_bwd_kernel, causal=causal, qb=qb, k...  70.8 us
    dot_general x24, matrix products, mm(): lax.dot_general(a, b, dims, precision=HIGH, preferred_element_type=F32)  66.6 us
    unnamed x215, local copies, waits for them, and re-layouts  58.4 us
    pallas_call x1, Pallas kernels, ffn(): pl.pallas_call(functools.partial(ffn_kernel, rb=512, drows=drows), grid_s...  50.5 us
    pallas_call x2, Pallas kernels, attn_fwd(): pl.pallas_call(functools.partial(attn_fwd_kernel, causal=causal, qb=qb, k...  36.8 us
    ppermute x6, waiting for transfers between devices, around(): lax.ppermute(x, 'tensor', turn(tensor, s))  34.6 us
    ppermute x6, starting transfers between devices, around(): lax.ppermute(x, 'tensor', turn(tensor, s))  34.2 us
    ppermute x3, waiting for transfers between devices, return_items(): lax.ppermute(lax.dynamic_slice_in_dim(rows, (1 - b) * half, half), BOTH,...  32.8 us
  transfers between devices with their start and end apart: 41, of which 8 were waited for; matrix products, arithmetic and copies ran while one was open for 24% of the time, Pallas kernels for 21%

profile of v2, /device:TPU:0, one launch (start us, length us, event | category | flops | bytes accessed | tf_op | source)
XLA Modules:
  0.0 570.2 jit_solution(15113888889628378587)
XLA Ops:
  20.3 5.4 collective-permute-done.refs_1_
  25.6 10.4 %collective-permute-done.1.refs_2_ = f32[64,1024]{1,0:T(8,128)S(1)} collective-permute-done((f32[64,1024]{1,0:T(8,128)S(1)}, f32[64,1024]{1,0:T(8,128)S(1)}, u32[]{:S(2)}, u32[]{:S(2)}) %collective-permute-start.1) | collective-permute-done | bytes 262176 | tf_op jit(solution)/shard_map/ppermute | solution.py:504
  40.5 5.0 collective-permute-start.4
  48.2 21.7 %collective-permute-done.4.b_ref.refs_2_ = f32[512,512]{1,0:T(8,128)S(1)} collective-permute-done((f32[512,512]{1,0:T(8,128)}, f32[512,512]{1,0:T(8,128)S(1)}, u32[]{:S(2)}, u32[]{:S(2)}) %collective-permute-start.4) | collective-permute-done | bytes 1048608 | tf_op jit(solution)/shard_map/ppermute | solution.py:358
  71.8 22.5 %collective-permute-start.8 = (f32[72,1024]{1,0:T(8,128)}, f32[72,1024]{1,0:T(8,128)S(1)}, u32[]{:S(2)}, u32[]{:S(2)}) collective-permute-start(f32[72,1024]{1,0:T(8,128)} %after.13), channel_id=1, source_target_pairs={{0,1},{1,2},{2,3},{3,0},{4,5},{5,6},{6,7},{7,4},{8,9},{9,10},{10,1... | collective-permute-start | bytes 884744 | tf_op jit(solution)/shard_map/ppermute | solution.py:504
  99.0 5.3 collective-permute-done.8
  104.2 13.5 %collective-permute-done.9 = f32[72,1024]{1,0:T(8,128)S(1)} collective-permute-done((f32[72,1024]{1,0:T(8,128)}, f32[72,1024]{1,0:T(8,128)S(1)}, u32[]{:S(2)}, u32[]{:S(2)}) %collective-permute-start.9) | collective-permute-done | bytes 294944 | tf_op jit(solution)/shard_map/ppermute | solution.py:504
  128.0 9.5 %collective-permute-start.15 = (f32[512,512]{1,0:T(8,128)}, f32[512,512]{1,0:T(8,128)}, u32[]{:S(2)}, u32[]{:S(2)}) collective-permute-start(f32[512,512]{1,0:T(8,128)} %after.16), channel_id=1, source_target_pairs={{0,0},{1,2},{2,4},{3,6},{4,1},{5,3},{6,5},{7,7},{8,8},{9,10},{10,1... | collective-permute-start | bytes 3145736 | tf_op jit(solution)/shard_map/ppermute | solution.py:358
  141.1 8.7 %place_weights.1 = (f32[512,256]{1,0:T(8,128)}, f32[512,256]{1,0:T(8,128)}, f32[512,256]{1,0:T(8,128)}, f32[512,512]{1,0:T(8,128)}, f32[512,512]{1,0:T(8,128)}, ...) custom-call(s32[2]{0:T(128)} %pad_add_fusion.2.who_ref, f32[8,4,64,1024]{3,2,1,0:T(8,128)} %bitcast.226), custom_call_target="tpu_custom_call" | custom-call | bytes 16777216 | tf_op jit(solution)/shard_map/place_weights/pallas_call | solution.py:529
  158.3 28.1 %attn_fwd.2 = (f32[2048,256]{1,0:T(8,128)S(1)}, f32[2,2,2048]{2,1,0:T(2,128)S(1)}) custom-call(f32[2048,256]{1,0:T(8,128)S(1)} %fusion.37.q_ref, f32[2048,256]{1,0:T(8,128)S(1)} %fusion.38.k_ref, f32[2048,256]{1,0:T(8,128)S(1)} %fusion.39.v_ref, bf16[2048,128]{1,0:T(8,128)(2,1)S(1)} %copy-done.40, bf16[2048,128]{1,0:T(8,128)(2,1)S(1)} %copy-done.35, ...), custom_call_target="tpu_custom_call" | custom-call | flops 40000000000 | bytes 8388608 | tf_op jit(solution)/shard_map/attn_fwd/pallas_call | solution.py:126
  190.7 8.9 %collective-permute-start.13 = (f32[64,512]{1,0:T(8,128)}, f32[64,512]{1,0:T(8,128)S(1)}, u32[]{:S(2)}, u32[]{:S(2)}) collective-permute-start(f32[64,512]{1,0:T(8,128)} %after.15), channel_id=1, source_target_pairs={{0,2},{1,0},{2,6},{3,4},{4,3},{5,1},{6,7},{7,5},{8,10},{9,8},{10,1... | collective-permute-start | bytes 393224 | tf_op jit(solution)/shard_map/ppermute | solution.py:358
  199.6 5.6 collective-permute-done.13
  218.3 8.7 %attn_fwd.3 = (f32[1024,512]{1,0:T(8,128)S(1)}, f32[4,2,1024]{2,1,0:T(2,128)S(1)}) custom-call(f32[1024,512]{1,0:T(8,128)S(1)} %fusion.40.q_ref, f32[256,512]{1,0:T(8,128)S(1)} %fusion.32.k_ref, f32[256,512]{1,0:T(8,128)S(1)} %fusion.31.v_ref, bf16[2048,128]{1,0:T(8,128)(2,1)S(1)} %copy-done.41, bf16[2048,128]{1,0:T(8,128)(2,1)S(1)} %copy-done.36), custom_call_target="tpu_custom_call" | custom-call | flops 16000000000 | bytes 8388608 | tf_op jit(solution)/shard_map/attn_fwd/pallas_call | solution.py:126
  230.1 50.5 %ffn.1 = (f32[1024,512]{1,0:T(8,128)S(1)}, f32[1024,512]{1,0:T(8,128)S(1)}, f32[8,72,4096]{2,1,0:T(8,128)}) custom-call(s32[1]{0:T(128)} %bitcast.z_ref, f32[1024,512]{1,0:T(8,128)} %convolution_add_fusion.1.h_ref, f32[1024,512]{1,0:T(8,128)} %maximum_select_fusion.1.g_ref, f32[8,4,72,1024]{3,2,1,0:T(8,128)} %bitcast.276, f32[8,4,72,1024]{3,2,1,0:T(8,128)} %bitcast.277, ...), custom_call_target="tpu_custom_call" | custom-call | flops 49999998976 | bytes 31457280 | tf_op jit(solution)/shard_map/ffn/pallas_call | solution.py:477
  295.6 14.0 %attn_bwd.3 = (f32[1024,512]{1,0:T(8,128)S(1)}, f32[256,512]{1,0:T(8,128)S(1)}, f32[256,512]{1,0:T(8,128)S(1)}) custom-call(f32[1024,512]{1,0:T(8,128)S(1)} %copy-done.27, f32[256,512]{1,0:T(8,128)S(1)} %fusion.32.k_ref, f32[256,512]{1,0:T(8,128)S(1)} %fusion.31.v_ref, f32[1024,512]{1,0:T(8,128)S(1)} %copy-done.10, ...), custom_call_target="tpu_custom_call" | custom-call | flops 20000000000 | bytes 16777216 | tf_op jit(solution)/shard_map/attn_bwd/pallas_call | solution.py:268
  319.8 9.5 %collective-permute-start.17 = (f32[512,512]{1,0:T(8,128)}, f32[512,512]{1,0:T(8,128)}, u32[]{:S(2)}, u32[]{:S(2)}) collective-permute-start(f32[512,512]{1,0:T(8,128)} %get-tuple-element.66), channel_id=1, source_target_pairs={{0,0},{2,1},{4,2},{6,3},{1,4},{3,5},{5,6},{7,7},{8,8},{10,9},{12,1... | collective-permute-start | bytes 3145736 | tf_op jit(solution)/shard_map/ppermute | solution.py:369
  350.9 27.7 %attn_bwd.4 = (f32[2048,128]{1,0:T(8,128)S(1)}, f32[2048,128]{1,0:T(8,128)S(1)}, f32[2048,128]{1,0:T(8,128)S(1)}) custom-call(f32[2048,256]{1,0:T(8,128)S(1)} %copy-done.24, f32[2048,256]{1,0:T(8,128)S(1)} %copy-done.21, f32[2048,256]{1,0:T(8,128)S(1)} %copy-done.19, f32[2048,256]{1,0:T(8,128)S(1)} %maximum_select_fusion.3.do_ref, ...), custom_call_target="tpu_custom_call" | custom-call | flops 33999998976 | bytes 16777216 | tf_op jit(solution)/shard_map/attn_bwd/pallas_call | solution.py:268
  394.5 29.1 %attn_bwd.5 = (f32[2048,128]{1,0:T(8,128)S(1)}, f32[2048,128]{1,0:T(8,128)S(1)}, f32[2048,128]{1,0:T(8,128)S(1)}) custom-call(f32[2048,256]{1,0:T(8,128)S(1)} %copy-done.25, f32[2048,256]{1,0:T(8,128)S(1)} %copy-done.22, f32[2048,256]{1,0:T(8,128)} %copy-done.18, f32[2048,256]{1,0:T(8,128)} %copy-done.8, f32[2,2,2048]{2,1,0:T(2,128)S(1)} %copy-done.49, ...), custom_call_target="tpu_custom_call" | custom-call | flops 33999998976 | bytes 16777216 | tf_op jit(solution)/shard_map/attn_bwd/pallas_call | solution.py:268
  440.5 6.3 %add_add_fusion = f32[2048,512]{1,0:T(8,128)S(1)} fusion(f32[2048,512]{1,0:T(8,128)} %fusion.44, f32[2048,512]{1,0:T(8,128)} %fusion.45, f32[2048,256]{1,0:T(8,128)S(1)} %constant_dynamic-update-slice_fusion.12.refs_0_, f32[512,256]{1,0:T(8,128)S(1)} %copy-done.87), kind=kOutput, calls=%fused_computation | convolution fusion | flops 1612709888 | bytes 15204352 | tf_op jit(solution)/shard_map/dot_general | solution.py:311
  449.4 7.1 %collective-permute-start.23 = (f32[1024,512]{1,0:T(8,128)}, f32[1024,512]{1,0:T(8,128)S(1)}, u32[]{:S(2)}, u32[]{:S(2)}) collective-permute-start(f32[1024,512]{1,0:T(8,128)} %constant_dynamic-slice_fusion.8), channel_id=1, source_target_pairs={{0,4},{4,0},{8,12},{12,8},{16,20},{20,16},{24,28},{28,24},{1,5},{5... | collective-permute-start | bytes 6291464 | tf_op jit(solution)/shard_map/ppermute | solution.py:379
  466.8 5.8 %fusion.46 = f32[512,256]{1,0:T(8,128)S(1)} fusion(f32[2048,512]{1,0:T(8,128)} %copy-done, f32[2048,256]{1,0:T(8,128)S(1)} %copy-done.55), kind=kOutput, calls=%fused_computation.198 | convolution fusion | flops 1610612736 | bytes 6815744 | tf_op jit(solution)/shard_map/dot_general | solution.py:311
  474.3 5.7 fusion.47
  481.5 5.9 %fusion.48 = f32[512,256]{1,0:T(8,128)S(1)} fusion(f32[2048,512]{1,0:T(8,128)} %copy-done, f32[2048,256]{1,0:T(8,128)S(1)} %copy-done.60), kind=kOutput, calls=%fused_computation.200 | convolution fusion | flops 1610612736 | bytes 6815744 | tf_op jit(solution)/shard_map/dot_general | solution.py:311
  524.2 32.8 %collective-permute-done.25 = f32[512,512]{1,0:T(8,128)} collective-permute-done((f32[512,512]{1,0:T(8,128)S(1)}, f32[512,512]{1,0:T(8,128)}, u32[]{:S(2)}, u32[]{:S(2)}) %collective-permute-start.25) | collective-permute-done | bytes 1048608 | tf_op jit(solution)/shard_map/ppermute | solution.py:370
  (407 shorter events, 206.9 us)
Async XLA Ops:
  7.2 133.9 %all-gather.5.cloned.1.call-start = ((), (), s32[]{:S(2)}) async-start(), calls=%async_computation.8 | async-start | bytes 9437184 | tf_op jit(solution)/shard_map/all_gather | solution.py:634
  37.4 192.8 %all-gather.7.cloned.1.call-start = ((), (), s32[]{:S(2)}) async-start(), calls=%async_computation.9 | async-start | bytes 10616832 | tf_op jit(solution)/shard_map/all_gather | solution.py:646
  40.5 29.3 %collective-permute-start.4 = (f32[512,512]{1,0:T(8,128)}, f32[512,512]{1,0:T(8,128)S(1)}, u32[]{:S(2)}, u32[]{:S(2)}) collective-permute-start(f32[512,512]{1,0:T(8,128)} %after.12), channel_id=1, source_target_pairs={{0,2},{1,0},{2,6},{3,4},{4,3},{5,1},{6,7},{7,5},{8,10},{9,8},{10,1... | collective-permute-start | bytes 3145736 | tf_op jit(solution)/shard_map/ppermute | solution.py:358
  45.5 24.3 %collective-permute-start.3 = (f32[512,512]{1,0:T(8,128)}, f32[512,512]{1,0:T(8,128)S(1)}, u32[]{:S(2)}, u32[]{:S(2)}) collective-permute-start(f32[512,512]{1,0:T(8,128)} %after.11), channel_id=1, source_target_pairs={{0,0},{1,2},{2,4},{3,6},{4,1},{5,3},{6,5},{7,7},{8,8},{9,10},{10,1... | collective-permute-start | bytes 3145736 | tf_op jit(solution)/shard_map/ppermute | solution.py:358
  71.8 32.5 %collective-permute-start.8 = (f32[72,1024]{1,0:T(8,128)}, f32[72,1024]{1,0:T(8,128)S(1)}, u32[]{:S(2)}, u32[]{:S(2)}) collective-permute-start(f32[72,1024]{1,0:T(8,128)} %after.13), channel_id=1, source_target_pairs={{0,1},{1,2},{2,3},{3,0},{4,5},{5,6},{6,7},{7,4},{8,9},{9,10},{10,1... | collective-permute-start | bytes 884744 | tf_op jit(solution)/shard_map/ppermute | solution.py:504
  94.2 23.6 %collective-permute-start.9 = (f32[72,1024]{1,0:T(8,128)}, f32[72,1024]{1,0:T(8,128)S(1)}, u32[]{:S(2)}, u32[]{:S(2)}) collective-permute-start(f32[72,1024]{1,0:T(8,128)} %after.13), channel_id=1, source_target_pairs={{0,2},{1,3},{2,0},{3,1},{4,6},{5,7},{6,4},{7,5},{8,10},{9,11},{10,... | collective-permute-start | bytes 884744 | tf_op jit(solution)/shard_map/ppermute | solution.py:504
  119.9 261.5 %reduce-scatter.5.cloned.1.call-start = ((), (), s32[]{:S(2)}) async-start(), calls=%async_computation.4 | async-start | bytes 10616832 | tf_op jit(solution)/shard_map/reduce_scatter | solution.py:673
  128.0 78.2 %collective-permute-start.15 = (f32[512,512]{1,0:T(8,128)}, f32[512,512]{1,0:T(8,128)}, u32[]{:S(2)}, u32[]{:S(2)}) collective-permute-start(f32[512,512]{1,0:T(8,128)} %after.16), channel_id=1, source_target_pairs={{0,0},{1,2},{2,4},{3,6},{4,1},{5,3},{6,5},{7,7},{8,8},{9,10},{10,1... | collective-permute-start | bytes 3145736 | tf_op jit(solution)/shard_map/ppermute | solution.py:358
  137.5 68.7 %collective-permute-start.16 = (f32[512,512]{1,0:T(8,128)}, f32[512,512]{1,0:T(8,128)}, u32[]{:S(2)}, u32[]{:S(2)}) collective-permute-start(f32[512,512]{1,0:T(8,128)} %after.17), channel_id=1, source_target_pairs={{0,2},{1,0},{2,6},{3,4},{4,3},{5,1},{6,7},{7,5},{8,10},{9,8},{10,1... | collective-permute-start | bytes 3145736 | tf_op jit(solution)/shard_map/ppermute | solution.py:358
  188.4 23.4 %collective-permute-start.11 = (f32[1024,256]{1,0:T(8,128)}, f32[1024,256]{1,0:T(8,128)}, u32[]{:S(2)}, u32[]{:S(2)}) collective-permute-start(f32[1024,256]{1,0:T(8,128)} %get-tuple-element.71), channel_id=1, source_target_pairs={{0,4},{4,0},{8,12},{12,8},{16,20},{20,16},{24,28},{28,24},{1,5},{5... | collective-permute-start | bytes 3145736 | tf_op jit(solution)/shard_map/ppermute | solution.py:379
  283.3 212.3 %reduce-scatter.11.cloned.1.call-start = ((), (), s32[]{:S(2)}) async-start(), calls=%async_computation.7 | async-start | bytes 1474560 | tf_op jit(solution)/shard_map/reduce_scatter | solution.py:721
  311.9 28.0 %collective-permute-start.20 = (f32[128,512]{1,0:T(8,128)S(1)}, f32[128,512]{1,0:T(8,128)S(1)}, u32[]{:S(2)}, u32[]{:S(2)}) collective-permute-start(f32[128,512]{1,0:T(8,128)S(1)} %constant_dynamic-slice_fusion.11), channel_id=1, source_target_pairs={{0,4},{4,0},{8,12},{12,8},{16,20},{20,16},{24,28},{28,24},{1,5},{5... | collective-permute-start | bytes 786440 | tf_op jit(solution)/shard_map/ppermute | solution.py:379
  316.6 25.9 %collective-permute-start.19 = (f32[1024,256]{1,0:T(8,128)S(1)}, f32[1024,256]{1,0:T(8,128)S(1)}, u32[]{:S(2)}, u32[]{:S(2)}) collective-permute-start(f32[1024,256]{1,0:T(8,128)S(1)} %get-tuple-element.65), channel_id=1, source_target_pairs={{0,4},{4,0},{8,12},{12,8},{16,20},{20,16},{24,28},{28,24},{1,5},{5... | collective-permute-start | bytes 3145736 | tf_op jit(solution)/shard_map/ppermute | solution.py:379
  319.8 68.3 %collective-permute-start.17 = (f32[512,512]{1,0:T(8,128)}, f32[512,512]{1,0:T(8,128)}, u32[]{:S(2)}, u32[]{:S(2)}) collective-permute-start(f32[512,512]{1,0:T(8,128)} %get-tuple-element.66), channel_id=1, source_target_pairs={{0,0},{2,1},{4,2},{6,3},{1,4},{3,5},{5,6},{7,7},{8,8},{10,9},{12,1... | collective-permute-start | bytes 3145736 | tf_op jit(solution)/shard_map/ppermute | solution.py:369
  329.2 58.8 %collective-permute-start.18 = (f32[512,512]{1,0:T(8,128)}, f32[512,512]{1,0:T(8,128)}, u32[]{:S(2)}, u32[]{:S(2)}) collective-permute-start(f32[512,512]{1,0:T(8,128)} %get-tuple-element.67), channel_id=1, source_target_pairs={{2,0},{0,1},{6,2},{4,3},{3,4},{1,5},{7,6},{5,7},{10,8},{8,9},{14,1... | collective-permute-start | bytes 3145736 | tf_op jit(solution)/shard_map/ppermute | solution.py:370
  340.8 47.2 %collective-permute-start.21 = (f32[64,512]{1,0:T(8,128)}, f32[64,512]{1,0:T(8,128)S(1)}, u32[]{:S(2)}, u32[]{:S(2)}) collective-permute-start(f32[64,512]{1,0:T(8,128)} %get-tuple-element.118), channel_id=1, source_target_pairs={{0,0},{2,1},{4,2},{6,3},{1,4},{3,5},{5,6},{7,7},{8,8},{10,9},{12,1... | collective-permute-start | bytes 393224 | tf_op jit(solution)/shard_map/ppermute | solution.py:369
  342.5 45.5 %collective-permute-start.22 = (f32[64,512]{1,0:T(8,128)}, f32[64,512]{1,0:T(8,128)S(1)}, u32[]{:S(2)}, u32[]{:S(2)}) collective-permute-start(f32[64,512]{1,0:T(8,128)} %get-tuple-element.117), channel_id=1, source_target_pairs={{2,0},{0,1},{6,2},{4,3},{3,4},{1,5},{7,6},{5,7},{10,8},{8,9},{14,1... | collective-permute-start | bytes 393224 | tf_op jit(solution)/shard_map/ppermute | solution.py:370
  388.0 123.7 %reduce-scatter.7.cloned.1.call-start = ((), (), s32[]{:S(2)}) async-start(), calls=%async_computation.5 | async-start | bytes 5898240 | tf_op jit(solution)/shard_map/reduce_scatter | solution.py:566
  438.5 122.6 %reduce-scatter.9.cloned.1.call-start = ((), (), s32[]{:S(2)}) async-start(), calls=%async_computation.6 | async-start | bytes 819200 | tf_op jit(solution)/shard_map/reduce_scatter | solution.py:579
  491.9 32.3 %collective-permute-start.24 = (f32[512,512]{1,0:T(8,128)}, f32[512,512]{1,0:T(8,128)S(1)}, u32[]{:S(2)}, u32[]{:S(2)}) collective-permute-start(f32[512,512]{1,0:T(8,128)} %get-tuple-element.62), channel_id=1, source_target_pairs={{0,0},{2,1},{4,2},{6,3},{1,4},{3,5},{5,6},{7,7},{8,8},{10,9},{12,1... | collective-permute-start | bytes 3145736 | tf_op jit(solution)/shard_map/ppermute | solution.py:369
  493.7 63.2 %collective-permute-start.25 = (f32[512,512]{1,0:T(8,128)S(1)}, f32[512,512]{1,0:T(8,128)}, u32[]{:S(2)}, u32[]{:S(2)}) collective-permute-start(f32[512,512]{1,0:T(8,128)S(1)} %get-tuple-element.63), channel_id=1, source_target_pairs={{2,0},{0,1},{6,2},{4,3},{3,4},{1,5},{7,6},{5,7},{10,8},{8,9},{14,1... | collective-permute-start | bytes 3145736 | tf_op jit(solution)/shard_map/ppermute | solution.py:370
  518.8 41.5 %collective-permute-start.32 = (f32[64,384]{1,0:T(8,128)S(1)}, f32[64,384]{1,0:T(8,128)S(1)}, u32[]{:S(2)}, u32[]{:S(2)}) collective-permute-start(f32[64,384]{1,0:T(8,128)S(1)} %get-tuple-element.100), channel_id=1, source_target_pairs={{0,1},{1,2},{2,3},{3,0},{4,5},{5,6},{6,7},{7,4},{8,9},{9,10},{10,1... | collective-permute-start | bytes 294920 | tf_op jit(solution)/shard_map/ppermute | solution.py:555
  520.3 40.0 %collective-permute-start.33 = (f32[64,384]{1,0:T(8,128)S(1)}, f32[64,384]{1,0:T(8,128)S(1)}, u32[]{:S(2)}, u32[]{:S(2)}) collective-permute-start(f32[64,384]{1,0:T(8,128)S(1)} %get-tuple-element.101), channel_id=1, source_target_pairs={{0,2},{1,3},{2,0},{3,1},{4,6},{5,7},{6,4},{7,5},{8,10},{9,11},{10,... | collective-permute-start | bytes 294920 | tf_op jit(solution)/shard_map/ppermute | solution.py:555
  522.7 37.6 %collective-permute-start.34 = (f32[64,384]{1,0:T(8,128)S(1)}, f32[64,384]{1,0:T(8,128)S(1)}, u32[]{:S(2)}, u32[]{:S(2)}) collective-permute-start(f32[64,384]{1,0:T(8,128)S(1)} %get-tuple-element.102), channel_id=1, source_target_pairs={{0,3},{1,0},{2,1},{3,2},{4,7},{5,4},{6,5},{7,6},{8,11},{9,8},{10,9... | collective-permute-start | bytes 294920 | tf_op jit(solution)/shard_map/ppermute | solution.py:555
  (112 other events, 804.0 us)
Sparse Core Ops, SparseCore 0:
  37.5 59.1 all-gather.4
  120.0 63.4 all-gather.6
  283.4 77.4 reduce-scatter.4
  388.1 33.6 reduce-scatter.10
  438.6 64.2 reduce-scatter.6
  516.9 32.8 reduce-scatter.8

commit v3 on v2

--- a/solution.py
+++ b/solution.py
@@ -132,7 +132,7 @@
         out_specs=[qspec, pl.BlockSpec((1, 2, rq), lambda p: (p, 0, 0))],
         out_shape=[jax.ShapeDtypeStruct((rq, w), F32), jax.ShapeDtypeStruct((pairs, 2, rq), F32)],
         scratch_shapes=[pltpu.VMEM((2, rq, 256), BF), pltpu.VMEM((2, rk, 256), BF), pltpu.VMEM((2, 128, rk), BF)],
-        compiler_params=pltpu.CompilerParams(vmem_limit_bytes=32 << 20),
+        compiler_params=pltpu.CompilerParams(vmem_limit_bytes=28 << 20),
         cost_estimate=pl.CostEstimate(flops=(int(2e10) if causal else int(4e9)) * pairs, bytes_accessed=rq * w * 16, transcendentals=0),
         name="attn_fwd",
     )(q, k, v, qaux, kaux, *deps)
@@ -255,11 +255,12 @@
     lax.fori_loop(0, rk // 256, finish, 0)
 
 
-def attn_bwd(q, k, v, do, lse, delta, qaux, kaux, causal, qb=512, kb=512, pair=None, deps=()):
+def attn_bwd(q, k, v, do, lse, delta, qaux, kaux, causal, qb=512, kb=512, pair=None, deps=(), prev=()):
     rq, w = q.shape
     rk = k.shape[0]
     pairs = 1 if pair is not None else w // 128
     first = pair or 0
+    deps = list(prev) + list(deps)
     ra = qaux.shape[0]
     qspec = pl.BlockSpec((rq, 128), lambda p: (0, p + first))
     kspec = pl.BlockSpec((rk, 128), lambda p: (0, p + first))
@@ -270,8 +271,9 @@
         grid=(pairs,),
         in_specs=[qspec, kspec, kspec, qspec, lspec, lspec, aspec, aspec]
         + [pl.BlockSpec(memory_space=pl.ANY)] * len(deps),
-        out_specs=[pl.BlockSpec((n, 128), lambda p: (0, p)) for n in (rq, rk, rk)],
-        out_shape=[jax.ShapeDtypeStruct((n, pairs * 128), F32) for n in (rq, rk, rk)],
+        out_specs=[qspec, kspec, kspec],
+        out_shape=[jax.ShapeDtypeStruct((n, w), F32) for n in (rq, rk, rk)],
+        input_output_aliases={8 + i: i for i in range(len(prev))},
         scratch_shapes=[pltpu.VMEM((2, rq, 256), BF), pltpu.VMEM((2, rk, 256), BF), pltpu.VMEM((2, 128, rk), BF),
                         pltpu.VMEM((2, rk, 256), BF), pltpu.VMEM((2, rq, 256), BF),
                         pltpu.VMEM((2, rk, 128), F32), pltpu.VMEM((2, rk, 128), F32)],
@@ -279,6 +281,56 @@
         cost_estimate=pl.CostEstimate(flops=(int(3.4e10) if causal else int(5e9)) * pairs, bytes_accessed=rq * w * 32, transcendentals=0),
         name="attn_bwd",
     )(q, k, v, do, lse, delta, qaux, kaux, *deps)
+
+
+def attn_bwd_inputs_kernel(q_ref, k_ref, v_ref, do_ref, l_ref, d_ref, qa_ref, ka_ref, x_ref, wq_ref, wk_ref, wv_ref,
+                           *refs, qb, kb, rq, rk, more):
+    part_ref, g_ref, dq, dk, dv = refs[-12:-7]
+    scratch = refs[-7:]
+    attn_bwd_kernel(
+        q_ref, k_ref, v_ref, do_ref, l_ref, d_ref, qa_ref, ka_ref, dq, dk, dv, *scratch,
+        causal=True, qb=qb, kb=kb, rq=rq, rk=rk,
+    )
+    weights = parts2(jnp.concatenate([wq_ref[...], wk_ref[...], wv_ref[...]], axis=1))
+    step = 512
+    g_ref[...] = jnp.zeros(g_ref.shape, F32)
+
+    def body(i, _):
+        r = pl.ds(pl.multiple_of(i * step, step), step)
+        grads = parts2(jnp.concatenate([dq[r, :], dk[r, :], dv[r, :]], axis=1))
+        new = dot3(grads, weights, NT)
+        part_ref[r, :] = new + refs[0][r, :] if more else new
+        g_ref[...] += dot3(parts2(x_ref[r, :].T), grads)
+        return 0
+
+    lax.fori_loop(0, rq // step, body, 0)
+
+
+def attn_bwd_inputs(q, k, v, do, lse, delta, qaux, kaux, x, weights, qb, kb, pair, prev=None, deps=()):
+    rows, w = q.shape
+    width = x.shape[1]
+    one = pl.Buffered(1)
+    qspec = pl.BlockSpec((rows, 128), lambda p: (0, pair), pipeline_mode=one)
+    lspec = pl.BlockSpec((1, 2, rows), lambda p: (pair, 0, 0))
+    aspec = pl.BlockSpec((rows, 128), lambda p: (0, 0), pipeline_mode=one)
+    wspec = pl.BlockSpec((width, 128), lambda p: (0, pair), pipeline_mode=one)
+    xspec = pl.BlockSpec((rows, width), lambda p: (0, 0), pipeline_mode=one)
+    first = () if prev is None else (prev,)
+    return pl.pallas_call(
+        functools.partial(attn_bwd_inputs_kernel, qb=qb, kb=kb, rq=rows, rk=rows, more=bool(first)),
+        grid=(1,),
+        in_specs=[qspec] * 4 + [lspec, lspec, aspec, aspec, xspec, wspec, wspec, wspec] + [xspec] * len(first)
+        + [pl.BlockSpec(memory_space=pl.ANY)] * len(deps),
+        out_specs=[xspec, pl.BlockSpec((width, 384), lambda p: (0, 0), pipeline_mode=one)],
+        out_shape=[jax.ShapeDtypeStruct((rows, width), F32), jax.ShapeDtypeStruct((width, 384), F32)],
+        scratch_shapes=[pltpu.VMEM((rows, 128), F32)] * 3
+        + [pltpu.VMEM((2, rows, 256), BF), pltpu.VMEM((2, rows, 256), BF), pltpu.VMEM((2, 128, rows), BF),
+           pltpu.VMEM((2, rows, 256), BF), pltpu.VMEM((2, rows, 256), BF),
+           pltpu.VMEM((2, rows, 128), F32), pltpu.VMEM((2, rows, 128), F32)],
+        compiler_params=pltpu.CompilerParams(vmem_limit_bytes=48 << 20),
+        cost_estimate=pl.CostEstimate(flops=int(4e10), bytes_accessed=rows * w * 32, transcendentals=0),
+        name="attn_bwd_inputs",
+    )(q, k, v, do, lse, delta, qaux, kaux, x, *weights, *first, *deps)
 
 
 def tree_aux(lengths, parent, n):
@@ -315,6 +367,10 @@
     pass
 
 
+def corner(x):
+    return x if x.ndim < 2 else x.reshape((-1,) + x.shape[-1:])[:8, :128]
+
+
 def after(x, *others):
     return pl.pallas_call(
         nothing,
@@ -362,13 +418,15 @@
     return jnp.where(z // 2 == 0, jnp.concatenate([first, second]), jnp.concatenate([second, first]))
 
 
-def return_items(rows, routes, z):
+def return_items(rows, routes, z, between=None):
     half = rows.shape[0] // 2
     b = z // 2
     back = [[(t, s) for s, t in r] for r in routes]
     first = lax.ppermute(lax.dynamic_slice_in_dim(rows, b * half, half), BOTH, back[0])
-    second = lax.ppermute(lax.dynamic_slice_in_dim(rows, (1 - b) * half, half), BOTH, back[1])
-    return first, second
+    second = lax.dynamic_slice_in_dim(rows, (1 - b) * half, half)
+    if between is not None:
+        second = after(second, first, between)
+    return first, lax.ppermute(second, BOTH, back[1])
 
 
 def both_batches(first, second, z):
@@ -419,7 +477,7 @@
     return dot(a[0], b[0], dims) + (dot(a[0], b[1], dims) + dot(a[1], b[0], dims))
 
 
-def ffn_kernel(z_ref, h_ref, g_ref, wi_ref, wo_ref, bo_ref, out_ref, dh_ref, gr_ref,
+def ffn_kernel(z_ref, h_ref, g_ref, wi_ref, wo_ref, bo_ref, out_ref, dh_ref, gr_ref, bi_ref, go_ref,
                hh, hl, gh, gl, hth, htl, gth, gtl, ah, al, dh, dl, *, rb, drows):
     j = pl.program_id(0)
     n = h_ref.shape[0]
@@ -454,18 +512,13 @@
         dh[rows, :], dl[rows, :] = du
         out_ref[rows, :] += dot3(act, wo, NT)
         dh_ref[rows, :] += dot3(du, wi, NT)
-    gr_ref[:, 0:drows, 0:wide] = dot3((hth[...], htl[...]), (dh[...], dl[...])).reshape(dp, drows, wide)
-    gr_ref[:, 0:drows, wide:] = dot3((gth[...], gtl[...]), (ah[...], al[...])).reshape(dp, drows, wide)
-    gr_ref[:, drows:drows + 8, :] = jnp.zeros((dp, 8, 2 * wide), F32)
-    for i in range(dp):
-        gr_ref[i, drows:drows + 1, 0:wide] = total
-
-    for half in range(2):
-        @pl.when(j % 2 == half)
-        def _():
-            bout = jnp.sum(g_ref[:, half * wide:(half + 1) * wide], axis=0, keepdims=True)
-            for i in range(dp):
-                gr_ref[i, drows + 1:drows + 2, 0:wide] = bout
+    gr_ref[:, :, 0:wide] = dot3((hth[...], htl[...]), (dh[...], dl[...])).reshape(dp, drows, wide)
+    gr_ref[:, :, wide:] = dot3((gth[...], gtl[...]), (ah[...], al[...])).reshape(dp, drows, wide)
+    bi_ref[0:1, :] = total
+
+    @pl.when(j == 0)
+    def _():
+        go_ref[0:1, :] = jnp.sum(g_ref[...], axis=0, keepdims=True)
 
 
 def ffn(h2, g, ff_all, bias_out, z, drows):
@@ -485,14 +538,19 @@
                 pl.BlockSpec((dp, 1, high, wide), lambda j, z: (0, (z[0] + tensor - j // 2) % tensor, 0, 2 + j % 2)),
                 pl.BlockSpec((1, width), lambda j, z: (0, 0)),
             ],
-            out_specs=[full(), full(), pl.BlockSpec((dp, high, 2 * wide), lambda j, z: (0, 0, j))],
+            out_specs=[
+                full(), full(), pl.BlockSpec((dp, drows, 2 * wide), lambda j, z: (0, 0, j)),
+                pl.BlockSpec((1, wide), lambda j, z: (0, j)), pl.BlockSpec((1, width), lambda j, z: (0, 0)),
+            ],
             scratch_shapes=[pltpu.VMEM((n, width), BF)] * 4 + [pltpu.VMEM((width, n), BF)] * 4
             + [pltpu.VMEM((n, wide), BF)] * 4,
         ),
         out_shape=[
             jax.ShapeDtypeStruct((n, width), F32),
             jax.ShapeDtypeStruct((n, width), F32),
-            jax.ShapeDtypeStruct((dp, high, 2 * wide * steps), F32),
+            jax.ShapeDtypeStruct((dp, drows, 2 * wide * steps), F32),
+            jax.ShapeDtypeStruct((1, wide * steps), F32),
+            jax.ShapeDtypeStruct((1, width), F32),
         ],
         compiler_params=pltpu.CompilerParams(vmem_limit_bytes=48 << 20),
         cost_estimate=pl.CostEstimate(flops=int(5e10), bytes_accessed=30 << 20, transcendentals=0),
@@ -549,10 +607,13 @@
     return cur
 
 
-def along_z(parts, tensor, z):
+def along_z(parts, tensor, z, *others):
     total = parts(z)
     for s in range(1, tensor):
-        total = total + lax.ppermute(parts((z + s) % tensor), "tensor", turn(tensor, s))
+        part = parts((z + s) % tensor)
+        if others:
+            part = after(part, *others)
+        total = total + lax.ppermute(part, "tensor", turn(tensor, s))
     return total
 
 
@@ -561,54 +622,24 @@
     return lax.dynamic_slice_in_dim(x, i * w, w, x.ndim - 1)
 
 
-def reduce_over_dp(mats, dp, tensor, earlier):
+def reduce_over_dp(mats, extra, dp, *others):
     whole = jnp.concatenate([m.reshape(dp, m.shape[0] // dp, m.shape[1]) for m in mats], axis=2)
-    mine = lax.psum_scatter(after(whole, earlier), "dp", scatter_dimension=0, tiled=False)
-    blocks, start = [], 0
-    for i in range(tensor):
-        one, start = [], 0
-        for m in mats:
-            w = m.shape[1] // tensor
-            one.append(mine[:, start + i * w:start + (i + 1) * w])
-            start += m.shape[1]
-        blocks.append(jnp.concatenate(one, axis=1))
-    return jnp.stack(blocks)
-
-
-def reduce_over_tensor(blocks, widths):
-    total = lax.psum_scatter(blocks, "tensor", scatter_dimension=0, tiled=False)
-    outs, start = [], 0
-    for w in widths:
-        outs.append(total[:, start:start + w])
-        start += w
-    return outs
+    whole = jnp.concatenate([whole, jnp.broadcast_to(extra[None], (dp,) + extra.shape)], axis=1)
+    return lax.psum_scatter(after(whole, *others), "dp", scatter_dimension=0, tiled=False)
 
 
 def reduce_head_grads(mats, dp, tensor, d, z):
     bits = dp.bit_length() - 1
     k = d % 2
-    half = tensor // 2
-    rows = mats[0].shape[0] // dp
-    w = mats[0].shape[1] // half
-    split = [m.reshape(dp // 2, 2, rows, half, w) for m in mats]
-
-    def side(i, u):
-        return jnp.concatenate([pick(m, 1, i)[:, :, u] for m in split], axis=2)
-
     chains = []
-    for u in range(half):
+    for u, m in enumerate(mats):
         seq = list(range(1, bits))
         if u % 2:
             seq = seq[::-1]
-        both = jnp.stack([side(k, u), swap(side(1 - k, u), dp)], axis=1)
+        m = m.reshape(dp // 2, 2, m.shape[0] // dp, m.shape[1])
+        both = jnp.stack([pick(m, 1, k), swap(pick(m, 1, 1 - k), dp)], axis=1)
         chains.append(halve(both, seq, dp, d))
-    everything = jnp.stack(chains)
-
-    def parts(i):
-        return pick(pick(everything, 0, i % half), 0, (i // half + k) % 2)
-
-    total = along_z(parts, tensor, z)
-    return [total[:, i * w:(i + 1) * w] for i in range(len(mats))]
+    return jnp.stack(chains)
 
 
 def on_device(
@@ -629,35 +660,39 @@
     shard = jnp.concatenate(
         [self_qkv[0], self_qkv[1], self_qkv[2], self_out.T, cross_q, cross_kv[0], cross_kv[1], cross_out.T], axis=1
     )
-    parts = around(shard, tensor)
-    x1, x2 = send_items(inputs[:, 0], routes, z, *parts[1:])
-    weights = lax.all_gather(jnp.stack(parts), "dp", axis=0)
-    wq, wk, wv, out_t, cq, ck, cv, cross_out_t = place_weights(
-        weights, [hw] * 8, [True] * 3 + [False] * 5, k, z
-    )
-    own_w = [wq, wk, wv]
+    x_first, x_second = pick(inputs[:, 0], 0, z % 2), pick(inputs[:, 0], 0, 1 - z % 2)
+    g_first, g_second = pick(cotangent[:, 0], 0, z % 2), pick(cotangent[:, 0], 0, 1 - z % 2)
+    paths = jnp.concatenate([lengths[:, 0], parent[:, 0]], axis=1)
+    other_paths = swap(paths, dp)
+    m1, m2 = send_items(memory[:, 0], routes, z)
+    parts = around(after(shard, x_first, x_second), tensor)
+    weights = lax.all_gather(after(jnp.stack(parts), m1, m2, other_paths), "dp", axis=0)
+    x1 = lax.ppermute(after(x_first, *parts[1:]), BOTH, routes[0])
+    x2 = lax.ppermute(after(x_second, *parts[1:]), BOTH, routes[1])
+    mem = in_order(m1, m2, z)
+    mem_all = both_cores(mem, swap(mem, dp), k)
+
+    my_path = pick(jnp.where(z % 2 == k, paths, other_paths), 0, z // 2)
+    segs = lengths.shape[2]
+    qaux, kaux = tree_aux(my_path[:segs], my_path[segs:], 2 * rows)
 
     bias_rows = jnp.concatenate([ff_bias_in[None], jnp.zeros((7, fw), F32)])
     ff_shard = jnp.concatenate(
         [jnp.concatenate([ff_in, ff_out.T], axis=1), jnp.concatenate([bias_rows] * 2, axis=1)]
     )
-    ff_parts = around(after(ff_shard, x1, x2), tensor)
-    ff_z = jnp.stack(ff_parts)
-    ff_all = lax.all_gather(ff_z, "dp", axis=0)
+    ff_parts = around(after(ff_shard, x1, x2, mem_all, qaux, kaux, corner(g_first), corner(g_second)), tensor)
+    wq, wk, wv, out_t, cq, ck, cv, cross_out_t = place_weights(
+        weights, [hw] * 8, [True] * 3 + [False] * 5, k, z
+    )
+    own_w = [wq, wk, wv]
     x_all = place_rows(x1, x2, swap(x1, dp), swap(x2, dp), k, z)
     x = lax.dynamic_slice_in_dim(x_all, k * rows, rows)
-    g1, g2 = send_items(cotangent[:, 0], routes, z, ff_z)
-    m1, m2 = send_items(memory[:, 0], routes, z, ff_z)
-    mem = in_order(m1, m2, z)
-    mem_all = both_cores(mem, swap(mem, dp), k)
-
-    paths = jnp.concatenate([lengths[:, 0], parent[:, 0]], axis=1)
-    other_paths = swap(paths, dp)
-    my_path = pick(jnp.where(z % 2 == k, paths, other_paths), 0, z // 2)
-    segs = lengths.shape[2]
-    qaux, kaux = tree_aux(my_path[:segs], my_path[segs:], 2 * rows)
-
     q, key, val = (mm(x_all, w) for w in own_w)
+    ff_z = jnp.stack([ff_parts[0]] + [after(t, corner(q), corner(key), corner(val)) for t in ff_parts[1:]])
+    ff_all = lax.all_gather(ff_z, "dp", axis=0)
+    g1 = lax.ppermute(after(g_first, ff_z), BOTH, routes[0])
+    g2 = lax.ppermute(after(g_second, ff_z), BOTH, routes[1])
+
     attn, lse = attn_fwd(q, key, val, qaux, kaux, True, 1024, 1024, deps=(ff_z,))
     mine = lax.dynamic_slice_in_dim(attn, k * rows, rows)
     other = swap(lax.dynamic_slice_in_dim(attn, (1 - k) * rows, rows), dp)
@@ -669,9 +704,15 @@
     ctx, lse2 = attn_fwd(q2, k2, v2, qaux, kaux, False, 1024, 256)
     h2 = h1 + mm(ctx, cross_out_t, NT)
     g = in_order(g1, g2, z)
-    output, dh2, ff_grads = ffn(h2, g, ff_all, ff_bias_out, z, drows)
+    output, dh2, ff_grads, du_sum, g_sum = ffn(h2, g, ff_all, ff_bias_out, z, drows)
     ff_mine = lax.psum_scatter(ff_grads, "dp", scatter_dimension=0, tiled=False)
-    ff_blocks = ff_mine.reshape(drows + 8, tensor, 2 * fw).transpose(1, 0, 2)
+    cut = fw // hw
+    spare = jnp.zeros((1, (5 - cut) * tensor * hw), F32)
+    bias_rows = jnp.concatenate([
+        jnp.concatenate([du_sum.reshape(tensor, cut, hw).transpose(1, 0, 2).reshape(1, -1), spare], axis=1),
+        jnp.concatenate([jnp.repeat(g_sum.reshape(cut, 1, hw), tensor, axis=1).reshape(1, -1), spare], axis=1),
+        jnp.zeros((6, 5 * tensor * hw), F32),
+    ])
     dctx = mm(dh2, cross_out_t)
     grad_cross_out_t = mm(dh2, ctx, TN)
     heads = width // HEAD
@@ -698,44 +739,57 @@
     mine = lax.dynamic_slice_in_dim(dattn_rows, k * heads_wide, heads_wide, 1)
     other = swap(lax.dynamic_slice_in_dim(dattn_rows, (1 - k) * heads_wide, heads_wide, 1), dp)
     dattn = both_cores(mine, other, k)
-    mid_blocks = reduce_over_dp(
-        [grad_cross_q, grad_ck, grad_cv, grad_cross_out_t, grad_self_out_t], dp, tensor, ff_mine
-    )
+    mid_mine = reduce_over_dp(
+        [grad_cross_q, grad_ck, grad_cv, grad_cross_out_t, grad_self_out_t], bias_rows, dp, ff_mine
+    )
+    ff_sum = along_z(lambda i: column_block(ff_mine, i, tensor), tensor, z)
     out_back = return_items(output, routes, z)
-    mem_back = return_items(grad_mem, routes, z)
     delta = deltas(dattn, attn)
-    back = []
+    part, head_grads = None, []
     for p in range(heads_wide // 128):
-        deps = [] if p == 0 else list(out_back) + list(mem_back) + [back[0][0], ff_mine]
-        back.append(attn_bwd(q, key, val, dattn, lse, delta, qaux, kaux, True, 1024, 512, pair=p, deps=deps))
-    dq, dk, dv = (jnp.concatenate([b[i] for b in back], axis=1) for i in range(3))
-    part = mm(dq, own_w[0], NT) + mm(dk, own_w[1], NT) + mm(dv, own_w[2], NT)
+        deps = [ff_mine]
+        if p:
+            ff_sum, *out_back = (after(t, corner(part)) for t in [ff_sum, *out_back])
+            deps = [corner(t) for t in [ff_sum, *out_back]]
+        part, got = attn_bwd_inputs(
+            q, key, val, dattn, lse, delta, qaux, kaux, x_all, own_w, 1024, 512, p, prev=part, deps=deps
+        )
+        head_grads.append(got)
     dx = (
         dh1
         + lax.dynamic_slice_in_dim(part, k * rows, rows)
         + swap(lax.dynamic_slice_in_dim(part, (1 - k) * rows, rows), dp)
     )
-    dq, dk, dv = (after(t, dx) for t in (dq, dk, dv))
-    grad_qkv = [mm(x_all, t, TN) for t in (dq, dk, dv)]
-
-    ff_sum = lax.psum_scatter(ff_blocks, "tensor", scatter_dimension=0, tiled=False)
-    ff_sum = ff_sum.reshape(drows + 8, 2, 2, fw // 2)
-    grad_ff_in = ff_sum[:drows, :, 0].reshape(drows, fw)
-    grad_ff_out = ff_sum[:drows, :, 1].reshape(drows, fw)
-    grad_bias_in, grad_bias_out = ff_sum[drows, :, 0].reshape(fw), ff_sum[drows + 1, :, 0].reshape(fw)
-    mid_sums = reduce_over_tensor(mid_blocks, [hw] * 5)
-    mid_a, mid_b = mid_sums[:3], mid_sums[3:]
-    x_back = return_items(dx, routes, z)
-    att = reduce_head_grads(grad_qkv, dp, tensor, d, z)
+    def mid_parts(i):
+        return jnp.concatenate(
+            [column_block(mid_mine[:, n * width:(n + 1) * width], i, tensor) for n in range(5)], axis=1
+        )
+
+    mid_sum = along_z(mid_parts, tensor, z)
+    x_back = return_items(dx, routes, z, between=corner(mid_sum))
+    head_grads = [after(t, corner(mid_sum)) for t in head_grads]
+    mem_back = return_items(after(grad_mem, corner(mid_sum)), routes, z)
+    ff_sum = ff_sum.reshape(drows, 2, 2, fw // 2)
+    grad_ff_in = ff_sum[:, :, 0].reshape(drows, fw)
+    grad_ff_out = ff_sum[:, :, 1].reshape(drows, fw)
+
+    mid = [mid_sum[:drows, n * hw:(n + 1) * hw] for n in range(5)]
+    grad_bias_in, grad_bias_out = mid_sum[drows, :fw], mid_sum[drows + 1, :fw]
+    head_sums = reduce_head_grads(head_grads, dp, tensor, d, z)
+    half = tensor // 2
+    att = along_z(
+        lambda i: pick(pick(head_sums, 0, i % half), 0, (i // half + k) % 2), tensor, z,
+    )
+    att = [att[:, n * hw:(n + 1) * hw] for n in range(3)]
     return (
         both_batches(*out_back, z)[:, None],
         both_batches(*x_back, z)[:, None],
         both_batches(*mem_back, z)[:, None],
         jnp.stack(att),
-        mid_b[1].T,
-        mid_a[0],
-        jnp.stack(mid_a[1:]),
-        mid_b[0].T,
+        mid[4].T,
+        mid[0],
+        jnp.stack(mid[1:3]),
+        mid[3].T,
         grad_ff_in,
         grad_bias_in,
         grad_ff_out.T,

time: 581 us -> 550 us (0.947)
  matrix products: 68.8 us -> 33.8 us
  Pallas kernels: 168 us -> 192 us
  waiting for transfers between devices: 99.4 us -> 86.4 us
  local copies, waits for them, and re-layouts: 88.5 us -> 79.5 us
    pallas_call x0 -> x2, Pallas kernels: none -> 80.9 us  [attn_bwd_inputs(): pl.pallas_call(functools.partial(attn_bwd_inputs_kernel, qb=qb, kb=kb, rq...]
    pallas_call x3 -> x1, Pallas kernels: 70.8 us -> 13.9 us  [attn_bwd(): pl.pallas_call(functools.partial(attn_bwd_kernel, causal=causal, qb=qb, k...]
    dot_general x24 -> x18, matrix products: 66.6 us -> 31.5 us  [mm(): lax.dot_general(a, b, dims, precision=HIGH, preferred_element_type=F32)]
    ppermute x6 -> x16, starting transfers between devices: 7.25 us -> 37.6 us  [the longest x9 17 us: along_z(): total = total + lax.ppermute(part, 'tensor', turn(tensor, s))]
    ppermute x3 -> x1, waiting for transfers between devices: 27.3 us -> 0.01 us  [send_items(): lax.ppermute(second, BOTH, routes[1])]
    ppermute x6, starting transfers between devices: 34.2 us -> 12.3 us  [around(): lax.ppermute(x, 'tensor', turn(tensor, s))]
    ppermute x6, waiting for transfers between devices: 34.6 us -> 13.3 us  [around(): lax.ppermute(x, 'tensor', turn(tensor, s))]
    ppermute x10, starting transfers between devices: 9.87 us -> 31.1 us  [swap(): return lax.ppermute(x, 'dp', flip_bit(dp, 0))]
  transfers between devices with their start and end apart: 41 -> 45, of which waited for: 8 -> 12; matrix products, arithmetic and copies ran while one was open for 24% -> 17% of each run, Pallas kernels for 21% -> 26%
where the time goes in v3:
time: 550 us; the launch traced here: 540 us
  Pallas kernels  192 us (35%)
  starting transfers between devices  99.8 us (18%)
  waiting for transfers between devices  86.4 us (16%)
  local copies, waits for them, and re-layouts  79.5 us (14%)
  matrix products  33.8 us (6%)
  other arithmetic  32.7 us (6%)
  between operations  15.8 us (3%)
    pallas_call x2, Pallas kernels, attn_bwd_inputs(): pl.pallas_call(functools.partial(attn_bwd_inputs_kernel, qb=qb, kb=kb, rq...  80.9 us
    pallas_call x1, Pallas kernels, ffn(): pl.pallas_call(functools.partial(ffn_kernel, rb=512, drows=drows), grid_s...  49.6 us
    unnamed x203, local copies, waits for them, and re-layouts  49 us
    pallas_call x2, Pallas kernels, attn_fwd(): pl.pallas_call(functools.partial(attn_fwd_kernel, causal=causal, qb=qb, k...  36.9 us
    dot_general x18, matrix products, mm(): lax.dot_general(a, b, dims, precision=HIGH, preferred_element_type=F32)  31.5 us
    ppermute x10, starting transfers between devices, swap(): return lax.ppermute(x, 'dp', flip_bit(dp, 0))  31.1 us
    ppermute x9, waiting for transfers between devices, along_z(): total = total + lax.ppermute(part, 'tensor', turn(tensor, s))  19.1 us
    ppermute x1, waiting for transfers between devices, on_device(): x2 = lax.ppermute(after(x_second, *parts[1:]), BOTH, routes[1])  18.4 us
  transfers between devices with their start and end apart: 45, of which 12 were waited for; matrix products, arithmetic and copies ran while one was open for 17% of the time, Pallas kernels for 26%

profile of v3, /device:TPU:0, one launch (start us, length us, event | category | flops | bytes accessed | tf_op | source)
XLA Modules:
  0.0 539.6 jit_solution(9910787800546562308)
XLA Ops:
  29.1 11.4 %collective-permute-done.1.refs_2_ = f32[64,1024]{1,0:T(8,128)S(1)} collective-permute-done((f32[64,1024]{1,0:T(8,128)}, f32[64,1024]{1,0:T(8,128)S(1)}, u32[]{:S(2)}, u32[]{:S(2)}) %collective-permute-start.1) | collective-permute-done | bytes 262176 | tf_op jit(solution)/shard_map/ppermute | solution.py:562
  48.3 8.6 %collective-permute-start.4 = (f32[512,512]{1,0:T(8,128)}, f32[512,512]{1,0:T(8,128)S(1)}, u32[]{:S(2)}, u32[]{:S(2)}) collective-permute-start(f32[512,512]{1,0:T(8,128)} %after.20), channel_id=1, source_target_pairs={{0,2},{1,0},{2,6},{3,4},{4,3},{5,1},{6,7},{7,5},{8,10},{9,8},{10,1... | collective-permute-start | bytes 3145736 | tf_op jit(solution)/shard_map/ppermute | solution.py:671
  61.4 18.4 %collective-permute-done.4.b_ref.refs_2_ = f32[512,512]{1,0:T(8,128)S(1)} collective-permute-done((f32[512,512]{1,0:T(8,128)}, f32[512,512]{1,0:T(8,128)S(1)}, u32[]{:S(2)}, u32[]{:S(2)}) %collective-permute-start.4) | collective-permute-done | bytes 1048608 | tf_op jit(solution)/shard_map/ppermute | solution.py:671
  82.1 22.4 %collective-permute-start.5 = (f32[512,512]{1,0:T(8,128)S(1)}, f32[512,512]{1,0:T(8,128)}, u32[]{:S(2)}, u32[]{:S(2)}) collective-permute-start(f32[512,512]{1,0:T(8,128)S(1)} %collective-permute-done.3.a_ref.refs_1_), channel_id=1, source_target_pairs={{0,4},{4,0},{8,12},{12,8},{16,20},{20,16},{24,28},{28,24},{1,5},{5... | collective-permute-start | bytes 3145736 | tf_op jit(solution)/shard_map/ppermute | solution.py:437
  119.6 8.7 %place_weights.1 = (f32[512,256]{1,0:T(8,128)}, f32[512,256]{1,0:T(8,128)}, f32[512,256]{1,0:T(8,128)}, f32[512,512]{1,0:T(8,128)}, f32[512,512]{1,0:T(8,128)}, ...) custom-call(s32[2]{0:T(128)} %pad_add_fusion.2.who_ref, f32[8,4,64,1024]{3,2,1,0:T(8,128)} %bitcast.194), custom_call_target="tpu_custom_call" | custom-call | bytes 16777216 | tf_op jit(solution)/shard_map/place_weights/pallas_call | solution.py:587
  128.4 4.3 fusion.41.v_ref
  152.7 28.5 %attn_fwd.2 = (f32[2048,256]{1,0:T(8,128)S(1)}, f32[2,2,2048]{2,1,0:T(2,128)S(1)}) custom-call(f32[2048,256]{1,0:T(8,128)S(1)} %copy-done.21, f32[2048,256]{1,0:T(8,128)S(1)} %copy-done.19, f32[2048,256]{1,0:T(8,128)S(1)} %fusion.41.v_ref, bf16[2048,128]{1,0:T(8,128)(2,1)S(1)} %copy-done.34, bf16[2048,128]{1,0:T(8,128)(2,1)S(1)} %copy-done.31, ...), custom_call_target="tpu_custom_call" | custom-call | flops 40000000000 | bytes 8388608 | tf_op jit(solution)/shard_map/attn_fwd/pallas_call | solution.py:126
  192.3 8.5 %attn_fwd.3 = (f32[1024,512]{1,0:T(8,128)S(1)}, f32[4,2,1024]{2,1,0:T(2,128)S(1)}) custom-call(f32[1024,512]{1,0:T(8,128)S(1)} %fusion.42.q_ref, f32[256,512]{1,0:T(8,128)S(1)} %fusion.43.k_ref, f32[256,512]{1,0:T(8,128)S(1)} %fusion.44.v_ref, bf16[2048,128]{1,0:T(8,128)(2,1)S(1)} %copy-done.34, bf16[2048,128]{1,0:T(8,128)(2,1)S(1)} %copy-done.31), custom_call_target="tpu_custom_call" | custom-call | flops 16000000000 | bytes 8388608 | tf_op jit(solution)/shard_map/attn_fwd/pallas_call | solution.py:126
  204.0 49.6 %ffn.1 = (f32[1024,512]{1,0:T(8,128)S(1)}, f32[1024,512]{1,0:T(8,128)S(1)}, f32[8,64,4096]{2,1,0:T(8,128)}, f32[1,2048]{1,0:T(1,128)S(1)}, f32[1,512]{1,0:T(1,128)S(1)}) custom-call(s32[1]{0:T(128)} %bitcast.z_ref, f32[1024,512]{1,0:T(8,128)} %convolution_add_fusion.1.h_ref, f32[1024,512]{1,0:T(8,128)} %maximum_select_fusion.1.g_ref, ...), custom_call_target="tpu_custom_call" | custom-call | flops 49999998976 | bytes 31457280 | tf_op jit(solution)/shard_map/ffn/pallas_call | solution.py:530
  256.5 3.4 fusion.45.do_ref
  267.8 13.9 %attn_bwd.1 = (f32[1024,512]{1,0:T(8,128)S(1)}, f32[256,512]{1,0:T(8,128)S(1)}, f32[256,512]{1,0:T(8,128)S(1)}) custom-call(f32[1024,512]{1,0:T(8,128)S(1)} %copy-done.26, f32[256,512]{1,0:T(8,128)S(1)} %copy-done.38, f32[256,512]{1,0:T(8,128)S(1)} %copy-done.40, f32[1024,512]{1,0:T(8,128)S(1)} %copy-done.9, f32[4,2,1024]{2,1,0:T(2,128)S(1)} %get-tuple-element.48.l_ref, ...), custom_call_target="tpu_custom_call" | custom-call | flops 20000000000 | bytes 16777216 | tf_op jit(solution)/shard_map/attn_bwd/pallas_call | solution.py:269
  285.8 5.8 %collective-permute-start.18 = (f32[1024,256]{1,0:T(8,128)S(1)}, f32[1024,256]{1,0:T(8,128)S(1)}, u32[]{:S(2)}, u32[]{:S(2)}) collective-permute-start(f32[1024,256]{1,0:T(8,128)S(1)} %get-tuple-element.67), channel_id=1, source_target_pairs={{0,4},{4,0},{8,12},{12,8},{16,20},{20,16},{24,28},{28,24},{1,5},{5... | collective-permute-start | bytes 3145736 | tf_op jit(solution)/shard_map/ppermute | solution.py:437
  293.1 9.4 %collective-permute-start.17 = (f32[512,512]{1,0:T(8,128)}, f32[512,512]{1,0:T(8,128)}, u32[]{:S(2)}, u32[]{:S(2)}) collective-permute-start(f32[512,512]{1,0:T(8,128)} %get-tuple-element.64), channel_id=1, source_target_pairs={{0,0},{2,1},{4,2},{6,3},{1,4},{3,5},{5,6},{7,7},{8,8},{10,9},{12,1... | collective-permute-start | bytes 3145736 | tf_op jit(solution)/shard_map/ppermute | solution.py:425
  319.6 12.2 %reduce-scatter.3.cloned.1.call-done = f32[1,64,4096]{2,1,0:T(8,128)} async-done(((f32[8,64,4096]{2,1,0:T(8,128)}), f32[1,64,4096]{2,1,0:T(8,128)}) %reduce-scatter.3.cloned.1.call-update) | async-done | bytes 1048592 | tf_op jit(solution)/shard_map/reduce_scatter | solution.py:708
  340.4 40.2 %attn_bwd_inputs.2 = (f32[2048,512]{1,0:T(8,128)}, f32[512,384]{1,0:T(8,128)S(1)}) custom-call(f32[2048,256]{1,0:T(8,128)} %copy-done.20, f32[2048,256]{1,0:T(8,128)} %copy-done.18, f32[2048,256]{1,0:T(8,128)} %copy-done.17, f32[2048,256]{1,0:T(8,128)} %copy-done.56, f32[2,2,2048]{2,1,0:T(2,128)S(1)} %get-tuple-element.50.l_ref, ...), custom_call_target="tpu_custom_call" | custom-call | flops 40000000000 | bytes 16777216 | tf_op jit(solution)/shard_map/attn_bwd_inputs/pallas_call | solution.py:319
  392.4 40.7 %attn_bwd_inputs.3 = (f32[2048,512]{1,0:T(8,128)}, f32[512,384]{1,0:T(8,128)S(1)}) custom-call(f32[2048,256]{1,0:T(8,128)S(1)} %copy-done.22, f32[2048,256]{1,0:T(8,128)} %copy-done.18, f32[2048,256]{1,0:T(8,128)} %copy-done.17, f32[2048,256]{1,0:T(8,128)} %copy-done.56, f32[2,2,2048]{2,1,0:T(2,128)S(1)} %get-tuple-element.50.l_ref, ...), custom_call_target="tpu_custom_call" | custom-call | flops 40000000000 | bytes 16777216 | tf_op jit(solution)/shard_map/attn_bwd_inputs/pallas_call | solution.py:319
  433.0 3.4 constant_dynamic-slice_fusion.7
  441.7 4.1 maximum_select_fusion.3
  450.0 3.5 collective-permute-start.27
  459.1 18.4 %collective-permute-done.26 = f32[72,640]{1,0:T(8,128)S(1)} collective-permute-done((f32[72,640]{1,0:T(8,128)S(1)}, f32[72,640]{1,0:T(8,128)S(1)}, u32[]{:S(2)}, u32[]{:S(2)}) %collective-permute-start.26) | collective-permute-done | bytes 184352 | tf_op jit(solution)/shard_map/ppermute | solution.py:616
  487.3 5.5 %collective-permute-start.31 = (f32[64,512]{1,0:T(8,128)}, f32[64,512]{1,0:T(8,128)S(1)}, u32[]{:S(2)}, u32[]{:S(2)}) collective-permute-start(f32[64,512]{1,0:T(8,128)} %get-tuple-element.94), channel_id=1, source_target_pairs={{2,0},{0,1},{6,2},{4,3},{3,4},{1,5},{7,6},{5,7},{10,8},{8,9},{14,1... | collective-permute-start | bytes 393224 | tf_op jit(solution)/shard_map/ppermute | solution.py:429
  497.4 3.9 collective-permute-done.31
  514.5 4.7 collective-permute-start.39
  520.2 10.1 %collective-permute-done.28 = f32[512,512]{1,0:T(8,128)S(1)} collective-permute-done((f32[512,512]{1,0:T(8,128)}, f32[512,512]{1,0:T(8,128)S(1)}, u32[]{:S(2)}, u32[]{:S(2)}) %collective-permute-start.28) | collective-permute-done | bytes 1048608 | tf_op jit(solution)/shard_map/ppermute | solution.py:429
  (406 shorter events, 184.3 us)
Async XLA Ops:
  7.2 112.5 %all-gather.5.cloned.1.call-start = ((), (), s32[]{:S(2)}) async-start(), calls=%async_computation.4 | async-start | bytes 9437184 | tf_op jit(solution)/shard_map/all_gather | solution.py:669
  19.6 20.9 %collective-permute-start.1 = (f32[64,1024]{1,0:T(8,128)}, f32[64,1024]{1,0:T(8,128)S(1)}, u32[]{:S(2)}, u32[]{:S(2)}) collective-permute-start(f32[64,1024]{1,0:T(8,128)} %after.18), channel_id=1, source_target_pairs={{0,2},{1,3},{2,0},{3,1},{4,6},{5,7},{6,4},{7,5},{8,10},{9,11},{10,... | collective-permute-start | bytes 786440 | tf_op jit(solution)/shard_map/ppermute | solution.py:562
  44.1 159.8 %all-gather.7.cloned.1.call-start = ((), (), s32[]{:S(2)}) async-start(), calls=%async_computation.5 | async-start | bytes 10616832 | tf_op jit(solution)/shard_map/all_gather | solution.py:692
  48.3 31.5 %collective-permute-start.4 = (f32[512,512]{1,0:T(8,128)}, f32[512,512]{1,0:T(8,128)S(1)}, u32[]{:S(2)}, u32[]{:S(2)}) collective-permute-start(f32[512,512]{1,0:T(8,128)} %after.20), channel_id=1, source_target_pairs={{0,2},{1,0},{2,6},{3,4},{4,3},{5,1},{6,7},{7,5},{8,10},{9,8},{10,1... | collective-permute-start | bytes 3145736 | tf_op jit(solution)/shard_map/ppermute | solution.py:671
  56.9 25.2 %collective-permute-start.3 = (f32[512,512]{1,0:T(8,128)}, f32[512,512]{1,0:T(8,128)S(1)}, u32[]{:S(2)}, u32[]{:S(2)}) collective-permute-start(f32[512,512]{1,0:T(8,128)} %after.19), channel_id=1, source_target_pairs={{0,0},{1,2},{2,4},{3,6},{4,1},{5,3},{6,5},{7,7},{8,8},{9,10},{10,1... | collective-permute-start | bytes 3145736 | tf_op jit(solution)/shard_map/ppermute | solution.py:670
  79.8 33.9 %collective-permute-start.6 = (f32[512,512]{1,0:T(8,128)S(1)}, f32[512,512]{1,0:T(8,128)S(1)}, u32[]{:S(2)}, u32[]{:S(2)}) collective-permute-start(f32[512,512]{1,0:T(8,128)S(1)} %collective-permute-done.4.b_ref.refs_2_), channel_id=1, source_target_pairs={{0,4},{4,0},{8,12},{12,8},{16,20},{20,16},{24,28},{28,24},{1,5},{5... | collective-permute-start | bytes 3145736 | tf_op jit(solution)/shard_map/ppermute | solution.py:437
  82.1 31.6 %collective-permute-start.5 = (f32[512,512]{1,0:T(8,128)S(1)}, f32[512,512]{1,0:T(8,128)}, u32[]{:S(2)}, u32[]{:S(2)}) collective-permute-start(f32[512,512]{1,0:T(8,128)S(1)} %collective-permute-done.3.a_ref.refs_1_), channel_id=1, source_target_pairs={{0,4},{4,0},{8,12},{12,8},{16,20},{20,16},{24,28},{28,24},{1,5},{5... | collective-permute-start | bytes 3145736 | tf_op jit(solution)/shard_map/ppermute | solution.py:437
  108.4 31.2 %collective-permute-start.11 = (f32[72,1024]{1,0:T(8,128)}, f32[72,1024]{1,0:T(8,128)}, u32[]{:S(2)}, u32[]{:S(2)}) collective-permute-start(f32[72,1024]{1,0:T(8,128)} %after.22), channel_id=1, source_target_pairs={{0,1},{1,2},{2,3},{3,0},{4,5},{5,6},{6,7},{7,4},{8,9},{9,10},{10,1... | collective-permute-start | bytes 884744 | tf_op jit(solution)/shard_map/ppermute | solution.py:562
  109.2 30.4 %collective-permute-start.12 = (f32[72,1024]{1,0:T(8,128)}, f32[72,1024]{1,0:T(8,128)}, u32[]{:S(2)}, u32[]{:S(2)}) collective-permute-start(f32[72,1024]{1,0:T(8,128)} %after.22), channel_id=1, source_target_pairs={{0,2},{1,3},{2,0},{3,1},{4,6},{5,7},{6,4},{7,5},{8,10},{9,11},{10,... | collective-permute-start | bytes 884744 | tf_op jit(solution)/shard_map/ppermute | solution.py:562
  112.3 27.3 %collective-permute-start.13 = (f32[72,1024]{1,0:T(8,128)}, f32[72,1024]{1,0:T(8,128)S(1)}, u32[]{:S(2)}, u32[]{:S(2)}) collective-permute-start(f32[72,1024]{1,0:T(8,128)} %after.22), channel_id=1, source_target_pairs={{0,3},{1,0},{2,1},{3,2},{4,7},{5,4},{6,5},{7,6},{8,11},{9,8},{10,9... | collective-permute-start | bytes 884744 | tf_op jit(solution)/shard_map/ppermute | solution.py:562
  142.7 189.1 %reduce-scatter.3.cloned.1.call-start = ((), (), s32[]{:S(2)}) async-start(), calls=%async_computation.2 | async-start | bytes 9437184 | tf_op jit(solution)/shard_map/reduce_scatter | solution.py:708
  142.8 42.2 %collective-permute-start.15 = (f32[512,512]{1,0:T(8,128)}, f32[512,512]{1,0:T(8,128)S(1)}, u32[]{:S(2)}, u32[]{:S(2)}) collective-permute-start(f32[512,512]{1,0:T(8,128)} %after.26), channel_id=1, source_target_pairs={{0,0},{1,2},{2,4},{3,6},{4,1},{5,3},{6,5},{7,7},{8,8},{9,10},{10,1... | collective-permute-start | bytes 3145736 | tf_op jit(solution)/shard_map/ppermute | solution.py:693
  144.8 40.1 %collective-permute-start.16 = (f32[512,512]{1,0:T(8,128)}, f32[512,512]{1,0:T(8,128)S(1)}, u32[]{:S(2)}, u32[]{:S(2)}) collective-permute-start(f32[512,512]{1,0:T(8,128)} %after.27), channel_id=1, source_target_pairs={{0,2},{1,0},{2,6},{3,4},{4,3},{5,1},{6,7},{7,5},{8,10},{9,8},{10,1... | collective-permute-start | bytes 3145736 | tf_op jit(solution)/shard_map/ppermute | solution.py:694
  256.3 191.9 %reduce-scatter.5.cloned.1.call-start = ((), (), s32[]{:S(2)}) async-start(), calls=%async_computation.3 | async-start | bytes 6635520 | tf_op jit(solution)/shard_map/reduce_scatter | solution.py:628
  285.8 30.1 %collective-permute-start.18 = (f32[1024,256]{1,0:T(8,128)S(1)}, f32[1024,256]{1,0:T(8,128)S(1)}, u32[]{:S(2)}, u32[]{:S(2)}) collective-permute-start(f32[1024,256]{1,0:T(8,128)S(1)} %get-tuple-element.67), channel_id=1, source_target_pairs={{0,4},{4,0},{8,12},{12,8},{16,20},{20,16},{24,28},{28,24},{1,5},{5... | collective-permute-start | bytes 3145736 | tf_op jit(solution)/shard_map/ppermute | solution.py:437
  293.1 89.7 %collective-permute-start.17 = (f32[512,512]{1,0:T(8,128)}, f32[512,512]{1,0:T(8,128)}, u32[]{:S(2)}, u32[]{:S(2)}) collective-permute-start(f32[512,512]{1,0:T(8,128)} %get-tuple-element.64), channel_id=1, source_target_pairs={{0,0},{2,1},{4,2},{6,3},{1,4},{3,5},{5,6},{7,7},{8,8},{10,9},{12,1... | collective-permute-start | bytes 3145736 | tf_op jit(solution)/shard_map/ppermute | solution.py:425
  302.5 81.1 %collective-permute-start.19 = (f32[512,512]{1,0:T(8,128)}, f32[512,512]{1,0:T(8,128)}, u32[]{:S(2)}, u32[]{:S(2)}) collective-permute-start(f32[512,512]{1,0:T(8,128)} %get-tuple-element.65), channel_id=1, source_target_pairs={{2,0},{0,1},{6,2},{4,3},{3,4},{1,5},{7,6},{5,7},{10,8},{8,9},{14,1... | collective-permute-start | bytes 3145736 | tf_op jit(solution)/shard_map/ppermute | solution.py:429
  333.9 50.7 %collective-permute-start.20 = (f32[64,1024]{1,0:T(8,128)}, f32[64,1024]{1,0:T(8,128)}, u32[]{:S(2)}, u32[]{:S(2)}) collective-permute-start(f32[64,1024]{1,0:T(8,128)} %get-tuple-element.74), channel_id=1, source_target_pairs={{0,1},{1,2},{2,3},{3,0},{4,5},{5,6},{6,7},{7,4},{8,9},{9,10},{10,1... | collective-permute-start | bytes 786440 | tf_op jit(solution)/shard_map/ppermute | solution.py:616
  335.4 49.2 %collective-permute-start.21 = (f32[64,1024]{1,0:T(8,128)}, f32[64,1024]{1,0:T(8,128)}, u32[]{:S(2)}, u32[]{:S(2)}) collective-permute-start(f32[64,1024]{1,0:T(8,128)} %get-tuple-element.76), channel_id=1, source_target_pairs={{0,2},{1,3},{2,0},{3,1},{4,6},{5,7},{6,4},{7,5},{8,10},{9,11},{10,... | collective-permute-start | bytes 786440 | tf_op jit(solution)/shard_map/ppermute | solution.py:616
  337.8 46.8 %collective-permute-start.22 = (f32[64,1024]{1,0:T(8,128)S(1)}, f32[64,1024]{1,0:T(8,128)}, u32[]{:S(2)}, u32[]{:S(2)}) collective-permute-start(f32[64,1024]{1,0:T(8,128)S(1)} %get-tuple-element.75), channel_id=1, source_target_pairs={{0,3},{1,0},{2,1},{3,2},{4,7},{5,4},{6,5},{7,6},{8,11},{9,8},{10,9... | collective-permute-start | bytes 786440 | tf_op jit(solution)/shard_map/ppermute | solution.py:616
  450.0 27.4 %collective-permute-start.26 = (f32[72,640]{1,0:T(8,128)S(1)}, f32[72,640]{1,0:T(8,128)S(1)}, u32[]{:S(2)}, u32[]{:S(2)}) collective-permute-start(f32[72,640]{1,0:T(8,128)S(1)} %get-tuple-element.106), channel_id=1, source_target_pairs={{0,2},{1,3},{2,0},{3,1},{4,6},{5,7},{6,4},{7,5},{8,10},{9,11},{10,... | collective-permute-start | bytes 552968 | tf_op jit(solution)/shard_map/ppermute | solution.py:616
  450.0 27.4 %collective-permute-start.27 = (f32[72,640]{1,0:T(8,128)S(1)}, f32[72,640]{1,0:T(8,128)S(1)}, u32[]{:S(2)}, u32[]{:S(2)}) collective-permute-start(f32[72,640]{1,0:T(8,128)S(1)} %get-tuple-element.105), channel_id=1, source_target_pairs={{0,3},{1,0},{2,1},{3,2},{4,7},{5,4},{6,5},{7,6},{8,11},{9,8},{10,9... | collective-permute-start | bytes 552968 | tf_op jit(solution)/shard_map/ppermute | solution.py:616
  457.6 35.1 %collective-permute-start.24 = (f32[512,512]{1,0:T(8,128)S(1)}, f32[512,512]{1,0:T(8,128)S(1)}, u32[]{:S(2)}, u32[]{:S(2)}) collective-permute-start(f32[512,512]{1,0:T(8,128)S(1)} %get-tuple-element.62), channel_id=1, source_target_pairs={{0,0},{2,1},{4,2},{6,3},{1,4},{3,5},{5,6},{7,7},{8,8},{10,9},{12,1... | collective-permute-start | bytes 3145736 | tf_op jit(solution)/shard_map/ppermute | solution.py:425
  493.7 36.6 %collective-permute-start.28 = (f32[512,512]{1,0:T(8,128)}, f32[512,512]{1,0:T(8,128)S(1)}, u32[]{:S(2)}, u32[]{:S(2)}) collective-permute-start(f32[512,512]{1,0:T(8,128)} %after.32), channel_id=1, source_target_pairs={{2,0},{0,1},{6,2},{4,3},{3,4},{1,5},{7,6},{5,7},{10,8},{8,9},{14,1... | collective-permute-start | bytes 3145736 | tf_op jit(solution)/shard_map/ppermute | solution.py:429
  (114 other events, 847.8 us)
Sparse Core Ops, SparseCore 0:
  44.2 63.6 all-gather.4
  142.8 57.1 all-gather.6
  256.4 75.3 reduce-scatter.2
  335.5 59.6 reduce-scatter.4

commit v4 on v3

--- a/solution.py
+++ b/solution.py
@@ -765,7 +765,7 @@
             [column_block(mid_mine[:, n * width:(n + 1) * width], i, tensor) for n in range(5)], axis=1
         )
 
-    mid_sum = along_z(mid_parts, tensor, z)
+    mid_sum = along_z(mid_parts, tensor, z, corner(dx))
     x_back = return_items(dx, routes, z, between=corner(mid_sum))
     head_grads = [after(t, corner(mid_sum)) for t in head_grads]
     mem_back = return_items(after(grad_mem, corner(mid_sum)), routes, z)

time: 550 us -> 555 us (level)
    unnamed x203 -> x213, local copies, waits for them, and re-layouts: 49 us -> 51 us
where the time goes in v4:
time: 555 us; the launch traced here: 544 us
  Pallas kernels  192 us (35%)
  starting transfers between devices  98 us (18%)
  waiting for transfers between devices  89.3 us (16%)
  local copies, waits for them, and re-layouts  82.2 us (15%)
  other arithmetic  33.8 us (6%)
  matrix products  33.7 us (6%)
  between operations  15.9 us (3%)
    pallas_call x2, Pallas kernels, attn_bwd_inputs(): pl.pallas_call(functools.partial(attn_bwd_inputs_kernel, qb=qb, kb=kb, rq...  80.9 us
    unnamed x213, local copies, waits for them, and re-layouts  51 us
    pallas_call x1, Pallas kernels, ffn(): pl.pallas_call(functools.partial(ffn_kernel, rb=512, drows=drows), grid_s...  49.6 us
    pallas_call x2, Pallas kernels, attn_fwd(): pl.pallas_call(functools.partial(attn_fwd_kernel, causal=causal, qb=qb, k...  36.9 us
    dot_general x18, matrix products, mm(): lax.dot_general(a, b, dims, precision=HIGH, preferred_element_type=F32)  31.5 us
    ppermute x10, starting transfers between devices, swap(): return lax.ppermute(x, 'dp', flip_bit(dp, 0))  31.1 us
    ppermute x9, waiting for transfers between devices, along_z(): total = total + lax.ppermute(part, 'tensor', turn(tensor, s))  20.2 us
    ppermute x1, waiting for transfers between devices, on_device(): x2 = lax.ppermute(after(x_second, *parts[1:]), BOTH, routes[1])  18.5 us
  transfers between devices with their start and end apart: 45, of which 12 were waited for; matrix products, arithmetic and copies ran while one was open for 17% of the time, Pallas kernels for 26%

profile of v4, /device:TPU:0, one launch (start us, length us, event | category | flops | bytes accessed | tf_op | source)
XLA Modules:
  0.0 544.4 jit_solution(13119741393667263017)
XLA Ops:
  29.1 11.4 %collective-permute-done.1.refs_2_ = f32[64,1024]{1,0:T(8,128)S(1)} collective-permute-done((f32[64,1024]{1,0:T(8,128)}, f32[64,1024]{1,0:T(8,128)S(1)}, u32[]{:S(2)}, u32[]{:S(2)}) %collective-permute-start.1) | collective-permute-done | bytes 262176 | tf_op jit(solution)/shard_map/ppermute | solution.py:562
  48.3 8.6 %collective-permute-start.4 = (f32[512,512]{1,0:T(8,128)}, f32[512,512]{1,0:T(8,128)S(1)}, u32[]{:S(2)}, u32[]{:S(2)}) collective-permute-start(f32[512,512]{1,0:T(8,128)} %after.23), channel_id=1, source_target_pairs={{0,2},{1,0},{2,6},{3,4},{4,3},{5,1},{6,7},{7,5},{8,10},{9,8},{10,1... | collective-permute-start | bytes 3145736 | tf_op jit(solution)/shard_map/ppermute | solution.py:671
  61.4 18.5 %collective-permute-done.4.b_ref.refs_2_ = f32[512,512]{1,0:T(8,128)S(1)} collective-permute-done((f32[512,512]{1,0:T(8,128)}, f32[512,512]{1,0:T(8,128)S(1)}, u32[]{:S(2)}, u32[]{:S(2)}) %collective-permute-start.4) | collective-permute-done | bytes 1048608 | tf_op jit(solution)/shard_map/ppermute | solution.py:671
  82.1 22.4 %collective-permute-start.5 = (f32[512,512]{1,0:T(8,128)S(1)}, f32[512,512]{1,0:T(8,128)}, u32[]{:S(2)}, u32[]{:S(2)}) collective-permute-start(f32[512,512]{1,0:T(8,128)S(1)} %collective-permute-done.3.a_ref.refs_1_), channel_id=1, source_target_pairs={{0,4},{4,0},{8,12},{12,8},{16,20},{20,16},{24,28},{28,24},{1,5},{5... | collective-permute-start | bytes 3145736 | tf_op jit(solution)/shard_map/ppermute | solution.py:437
  119.7 8.7 %place_weights.1 = (f32[512,256]{1,0:T(8,128)}, f32[512,256]{1,0:T(8,128)}, f32[512,256]{1,0:T(8,128)}, f32[512,512]{1,0:T(8,128)}, f32[512,512]{1,0:T(8,128)}, ...) custom-call(s32[2]{0:T(128)} %pad_add_fusion.2.who_ref, f32[8,4,64,1024]{3,2,1,0:T(8,128)} %bitcast.194), custom_call_target="tpu_custom_call" | custom-call | bytes 16777216 | tf_op jit(solution)/shard_map/place_weights/pallas_call | solution.py:587
  128.4 4.3 fusion.41.v_ref
  152.7 28.5 %attn_fwd.2 = (f32[2048,256]{1,0:T(8,128)S(1)}, f32[2,2,2048]{2,1,0:T(2,128)S(1)}) custom-call(f32[2048,256]{1,0:T(8,128)S(1)} %copy-done.21, f32[2048,256]{1,0:T(8,128)S(1)} %copy-done.19, f32[2048,256]{1,0:T(8,128)S(1)} %fusion.41.v_ref, bf16[2048,128]{1,0:T(8,128)(2,1)S(1)} %copy-done.34, bf16[2048,128]{1,0:T(8,128)(2,1)S(1)} %copy-done.31, ...), custom_call_target="tpu_custom_call" | custom-call | flops 40000000000 | bytes 8388608 | tf_op jit(solution)/shard_map/attn_fwd/pallas_call | solution.py:126
  192.3 8.5 %attn_fwd.3 = (f32[1024,512]{1,0:T(8,128)S(1)}, f32[4,2,1024]{2,1,0:T(2,128)S(1)}) custom-call(f32[1024,512]{1,0:T(8,128)S(1)} %fusion.42.q_ref, f32[256,512]{1,0:T(8,128)S(1)} %fusion.43.k_ref, f32[256,512]{1,0:T(8,128)S(1)} %fusion.44.v_ref, bf16[2048,128]{1,0:T(8,128)(2,1)S(1)} %copy-done.34, bf16[2048,128]{1,0:T(8,128)(2,1)S(1)} %copy-done.31), custom_call_target="tpu_custom_call" | custom-call | flops 16000000000 | bytes 8388608 | tf_op jit(solution)/shard_map/attn_fwd/pallas_call | solution.py:126
  204.0 49.6 %ffn.1 = (f32[1024,512]{1,0:T(8,128)S(1)}, f32[1024,512]{1,0:T(8,128)S(1)}, f32[8,64,4096]{2,1,0:T(8,128)}, f32[1,2048]{1,0:T(1,128)S(1)}, f32[1,512]{1,0:T(1,128)S(1)}) custom-call(s32[1]{0:T(128)} %bitcast.z_ref, f32[1024,512]{1,0:T(8,128)} %convolution_add_fusion.1.h_ref, f32[1024,512]{1,0:T(8,128)} %maximum_select_fusion.1.g_ref, ...), custom_call_target="tpu_custom_call" | custom-call | flops 49999998976 | bytes 31457280 | tf_op jit(solution)/shard_map/ffn/pallas_call | solution.py:530
  256.5 3.4 fusion.45.do_ref
  267.9 13.9 %attn_bwd.1 = (f32[1024,512]{1,0:T(8,128)S(1)}, f32[256,512]{1,0:T(8,128)S(1)}, f32[256,512]{1,0:T(8,128)S(1)}) custom-call(f32[1024,512]{1,0:T(8,128)S(1)} %copy-done.26, f32[256,512]{1,0:T(8,128)S(1)} %copy-done.38, f32[256,512]{1,0:T(8,128)S(1)} %copy-done.40, f32[1024,512]{1,0:T(8,128)S(1)} %copy-done.9, f32[4,2,1024]{2,1,0:T(2,128)S(1)} %get-tuple-element.48.l_ref, ...), custom_call_target="tpu_custom_call" | custom-call | flops 20000000000 | bytes 16777216 | tf_op jit(solution)/shard_map/attn_bwd/pallas_call | solution.py:269
  285.9 5.8 %collective-permute-start.18 = (f32[1024,256]{1,0:T(8,128)S(1)}, f32[1024,256]{1,0:T(8,128)S(1)}, u32[]{:S(2)}, u32[]{:S(2)}) collective-permute-start(f32[1024,256]{1,0:T(8,128)S(1)} %get-tuple-element.67), channel_id=1, source_target_pairs={{0,4},{4,0},{8,12},{12,8},{16,20},{20,16},{24,28},{28,24},{1,5},{5... | collective-permute-start | bytes 3145736 | tf_op jit(solution)/shard_map/ppermute | solution.py:437
  293.1 9.5 %collective-permute-start.17 = (f32[512,512]{1,0:T(8,128)}, f32[512,512]{1,0:T(8,128)}, u32[]{:S(2)}, u32[]{:S(2)}) collective-permute-start(f32[512,512]{1,0:T(8,128)} %get-tuple-element.64), channel_id=1, source_target_pairs={{0,0},{2,1},{4,2},{6,3},{1,4},{3,5},{5,6},{7,7},{8,8},{10,9},{12,1... | collective-permute-start | bytes 3145736 | tf_op jit(solution)/shard_map/ppermute | solution.py:425
  319.7 12.2 %reduce-scatter.3.cloned.1.call-done = f32[1,64,4096]{2,1,0:T(8,128)} async-done(((f32[8,64,4096]{2,1,0:T(8,128)}), f32[1,64,4096]{2,1,0:T(8,128)}) %reduce-scatter.3.cloned.1.call-update) | async-done | bytes 1048592 | tf_op jit(solution)/shard_map/reduce_scatter | solution.py:708
  340.5 40.2 %attn_bwd_inputs.2 = (f32[2048,512]{1,0:T(8,128)}, f32[512,384]{1,0:T(8,128)S(1)}) custom-call(f32[2048,256]{1,0:T(8,128)} %copy-done.20, f32[2048,256]{1,0:T(8,128)} %copy-done.18, f32[2048,256]{1,0:T(8,128)} %copy-done.17, f32[2048,256]{1,0:T(8,128)} %copy-done.58, f32[2,2,2048]{2,1,0:T(2,128)S(1)} %get-tuple-element.50.l_ref, ...), custom_call_target="tpu_custom_call" | custom-call | flops 40000000000 | bytes 16777216 | tf_op jit(solution)/shard_map/attn_bwd_inputs/pallas_call | solution.py:319
  392.4 40.6 %attn_bwd_inputs.3 = (f32[2048,512]{1,0:T(8,128)}, f32[512,384]{1,0:T(8,128)S(1)}) custom-call(f32[2048,256]{1,0:T(8,128)S(1)} %copy-done.22, f32[2048,256]{1,0:T(8,128)} %copy-done.18, f32[2048,256]{1,0:T(8,128)} %copy-done.17, f32[2048,256]{1,0:T(8,128)} %copy-done.58, f32[2,2,2048]{2,1,0:T(2,128)S(1)} %get-tuple-element.50.l_ref, ...), custom_call_target="tpu_custom_call" | custom-call | flops 40000000000 | bytes 16777216 | tf_op jit(solution)/shard_map/attn_bwd_inputs/pallas_call | solution.py:319
  441.8 4.1 maximum_select_fusion.3
  453.7 3.4 collective-permute-start.27
  463.0 18.4 %collective-permute-done.26 = f32[72,640]{1,0:T(8,128)} collective-permute-done((f32[72,640]{1,0:T(8,128)}, f32[72,640]{1,0:T(8,128)}, u32[]{:S(2)}, u32[]{:S(2)}) %collective-permute-start.26) | collective-permute-done | bytes 184352 | tf_op jit(solution)/shard_map/ppermute | solution.py:616
  492.1 5.4 collective-permute-start.31
  501.5 4.6 collective-permute-done.31
  512.0 3.8 collective-permute-done.37
  518.5 5.5 %collective-permute-start.39 = (f32[64,384]{1,0:T(8,128)S(1)}, f32[64,384]{1,0:T(8,128)S(1)}, u32[]{:S(2)}, u32[]{:S(2)}) collective-permute-start(f32[64,384]{1,0:T(8,128)S(1)} %get-tuple-element.91), channel_id=1, source_target_pairs={{0,2},{1,3},{2,0},{3,1},{4,6},{5,7},{6,4},{7,5},{8,10},{9,11},{10,... | collective-permute-start | bytes 294920 | tf_op jit(solution)/shard_map/ppermute | solution.py:616
  525.0 10.1 %collective-permute-done.28 = f32[512,512]{1,0:T(8,128)S(1)} collective-permute-done((f32[512,512]{1,0:T(8,128)}, f32[512,512]{1,0:T(8,128)S(1)}, u32[]{:S(2)}, u32[]{:S(2)}) %collective-permute-start.28) | collective-permute-done | bytes 1048608 | tf_op jit(solution)/shard_map/ppermute | solution.py:429
  (420 shorter events, 187.1 us)
Async XLA Ops:
  7.2 112.5 %all-gather.5.cloned.1.call-start = ((), (), s32[]{:S(2)}) async-start(), calls=%async_computation.4 | async-start | bytes 9437184 | tf_op jit(solution)/shard_map/all_gather | solution.py:669
  19.6 20.9 %collective-permute-start.1 = (f32[64,1024]{1,0:T(8,128)}, f32[64,1024]{1,0:T(8,128)S(1)}, u32[]{:S(2)}, u32[]{:S(2)}) collective-permute-start(f32[64,1024]{1,0:T(8,128)} %after.21), channel_id=1, source_target_pairs={{0,2},{1,3},{2,0},{3,1},{4,6},{5,7},{6,4},{7,5},{8,10},{9,11},{10,... | collective-permute-start | bytes 786440 | tf_op jit(solution)/shard_map/ppermute | solution.py:562
  44.1 159.9 %all-gather.7.cloned.1.call-start = ((), (), s32[]{:S(2)}) async-start(), calls=%async_computation.5 | async-start | bytes 10616832 | tf_op jit(solution)/shard_map/all_gather | solution.py:692
  48.3 31.6 %collective-permute-start.4 = (f32[512,512]{1,0:T(8,128)}, f32[512,512]{1,0:T(8,128)S(1)}, u32[]{:S(2)}, u32[]{:S(2)}) collective-permute-start(f32[512,512]{1,0:T(8,128)} %after.23), channel_id=1, source_target_pairs={{0,2},{1,0},{2,6},{3,4},{4,3},{5,1},{6,7},{7,5},{8,10},{9,8},{10,1... | collective-permute-start | bytes 3145736 | tf_op jit(solution)/shard_map/ppermute | solution.py:671
  56.9 25.2 %collective-permute-start.3 = (f32[512,512]{1,0:T(8,128)}, f32[512,512]{1,0:T(8,128)S(1)}, u32[]{:S(2)}, u32[]{:S(2)}) collective-permute-start(f32[512,512]{1,0:T(8,128)} %after.22), channel_id=1, source_target_pairs={{0,0},{1,2},{2,4},{3,6},{4,1},{5,3},{6,5},{7,7},{8,8},{9,10},{10,1... | collective-permute-start | bytes 3145736 | tf_op jit(solution)/shard_map/ppermute | solution.py:670
  79.8 33.9 %collective-permute-start.6 = (f32[512,512]{1,0:T(8,128)S(1)}, f32[512,512]{1,0:T(8,128)S(1)}, u32[]{:S(2)}, u32[]{:S(2)}) collective-permute-start(f32[512,512]{1,0:T(8,128)S(1)} %collective-permute-done.4.b_ref.refs_2_), channel_id=1, source_target_pairs={{0,4},{4,0},{8,12},{12,8},{16,20},{20,16},{24,28},{28,24},{1,5},{5... | collective-permute-start | bytes 3145736 | tf_op jit(solution)/shard_map/ppermute | solution.py:437
  82.1 31.7 %collective-permute-start.5 = (f32[512,512]{1,0:T(8,128)S(1)}, f32[512,512]{1,0:T(8,128)}, u32[]{:S(2)}, u32[]{:S(2)}) collective-permute-start(f32[512,512]{1,0:T(8,128)S(1)} %collective-permute-done.3.a_ref.refs_1_), channel_id=1, source_target_pairs={{0,4},{4,0},{8,12},{12,8},{16,20},{20,16},{24,28},{28,24},{1,5},{5... | collective-permute-start | bytes 3145736 | tf_op jit(solution)/shard_map/ppermute | solution.py:437
  108.4 31.2 %collective-permute-start.11 = (f32[72,1024]{1,0:T(8,128)}, f32[72,1024]{1,0:T(8,128)}, u32[]{:S(2)}, u32[]{:S(2)}) collective-permute-start(f32[72,1024]{1,0:T(8,128)} %after.25), channel_id=1, source_target_pairs={{0,1},{1,2},{2,3},{3,0},{4,5},{5,6},{6,7},{7,4},{8,9},{9,10},{10,1... | collective-permute-start | bytes 884744 | tf_op jit(solution)/shard_map/ppermute | solution.py:562
  109.2 30.4 %collective-permute-start.12 = (f32[72,1024]{1,0:T(8,128)}, f32[72,1024]{1,0:T(8,128)}, u32[]{:S(2)}, u32[]{:S(2)}) collective-permute-start(f32[72,1024]{1,0:T(8,128)} %after.25), channel_id=1, source_target_pairs={{0,2},{1,3},{2,0},{3,1},{4,6},{5,7},{6,4},{7,5},{8,10},{9,11},{10,... | collective-permute-start | bytes 884744 | tf_op jit(solution)/shard_map/ppermute | solution.py:562
  112.4 27.3 %collective-permute-start.13 = (f32[72,1024]{1,0:T(8,128)}, f32[72,1024]{1,0:T(8,128)S(1)}, u32[]{:S(2)}, u32[]{:S(2)}) collective-permute-start(f32[72,1024]{1,0:T(8,128)} %after.25), channel_id=1, source_target_pairs={{0,3},{1,0},{2,1},{3,2},{4,7},{5,4},{6,5},{7,6},{8,11},{9,8},{10,9... | collective-permute-start | bytes 884744 | tf_op jit(solution)/shard_map/ppermute | solution.py:562
  142.7 189.2 %reduce-scatter.3.cloned.1.call-start = ((), (), s32[]{:S(2)}) async-start(), calls=%async_computation.2 | async-start | bytes 9437184 | tf_op jit(solution)/shard_map/reduce_scatter | solution.py:708
  142.8 42.1 %collective-permute-start.15 = (f32[512,512]{1,0:T(8,128)}, f32[512,512]{1,0:T(8,128)S(1)}, u32[]{:S(2)}, u32[]{:S(2)}) collective-permute-start(f32[512,512]{1,0:T(8,128)} %after.29), channel_id=1, source_target_pairs={{0,0},{1,2},{2,4},{3,6},{4,1},{5,3},{6,5},{7,7},{8,8},{9,10},{10,1... | collective-permute-start | bytes 3145736 | tf_op jit(solution)/shard_map/ppermute | solution.py:693
  144.8 40.1 %collective-permute-start.16 = (f32[512,512]{1,0:T(8,128)}, f32[512,512]{1,0:T(8,128)S(1)}, u32[]{:S(2)}, u32[]{:S(2)}) collective-permute-start(f32[512,512]{1,0:T(8,128)} %after.30), channel_id=1, source_target_pairs={{0,2},{1,0},{2,6},{3,4},{4,3},{5,1},{6,7},{7,5},{8,10},{9,8},{10,1... | collective-permute-start | bytes 3145736 | tf_op jit(solution)/shard_map/ppermute | solution.py:694
  256.3 194.8 %reduce-scatter.5.cloned.1.call-start = ((), (), s32[]{:S(2)}) async-start(), calls=%async_computation.3 | async-start | bytes 6635520 | tf_op jit(solution)/shard_map/reduce_scatter | solution.py:628
  285.9 30.1 %collective-permute-start.18 = (f32[1024,256]{1,0:T(8,128)S(1)}, f32[1024,256]{1,0:T(8,128)S(1)}, u32[]{:S(2)}, u32[]{:S(2)}) collective-permute-start(f32[1024,256]{1,0:T(8,128)S(1)} %get-tuple-element.67), channel_id=1, source_target_pairs={{0,4},{4,0},{8,12},{12,8},{16,20},{20,16},{24,28},{28,24},{1,5},{5... | collective-permute-start | bytes 3145736 | tf_op jit(solution)/shard_map/ppermute | solution.py:437
  293.1 89.8 %collective-permute-start.17 = (f32[512,512]{1,0:T(8,128)}, f32[512,512]{1,0:T(8,128)}, u32[]{:S(2)}, u32[]{:S(2)}) collective-permute-start(f32[512,512]{1,0:T(8,128)} %get-tuple-element.64), channel_id=1, source_target_pairs={{0,0},{2,1},{4,2},{6,3},{1,4},{3,5},{5,6},{7,7},{8,8},{10,9},{12,1... | collective-permute-start | bytes 3145736 | tf_op jit(solution)/shard_map/ppermute | solution.py:425
  302.6 81.1 %collective-permute-start.19 = (f32[512,512]{1,0:T(8,128)}, f32[512,512]{1,0:T(8,128)}, u32[]{:S(2)}, u32[]{:S(2)}) collective-permute-start(f32[512,512]{1,0:T(8,128)} %get-tuple-element.65), channel_id=1, source_target_pairs={{2,0},{0,1},{6,2},{4,3},{3,4},{1,5},{7,6},{5,7},{10,8},{8,9},{14,1... | collective-permute-start | bytes 3145736 | tf_op jit(solution)/shard_map/ppermute | solution.py:429
  334.0 50.7 %collective-permute-start.20 = (f32[64,1024]{1,0:T(8,128)}, f32[64,1024]{1,0:T(8,128)}, u32[]{:S(2)}, u32[]{:S(2)}) collective-permute-start(f32[64,1024]{1,0:T(8,128)} %get-tuple-element.74), channel_id=1, source_target_pairs={{0,1},{1,2},{2,3},{3,0},{4,5},{5,6},{6,7},{7,4},{8,9},{9,10},{10,1... | collective-permute-start | bytes 786440 | tf_op jit(solution)/shard_map/ppermute | solution.py:616
  335.5 49.2 %collective-permute-start.21 = (f32[64,1024]{1,0:T(8,128)}, f32[64,1024]{1,0:T(8,128)}, u32[]{:S(2)}, u32[]{:S(2)}) collective-permute-start(f32[64,1024]{1,0:T(8,128)} %get-tuple-element.76), channel_id=1, source_target_pairs={{0,2},{1,3},{2,0},{3,1},{4,6},{5,7},{6,4},{7,5},{8,10},{9,11},{10,... | collective-permute-start | bytes 786440 | tf_op jit(solution)/shard_map/ppermute | solution.py:616
  337.9 46.7 %collective-permute-start.22 = (f32[64,1024]{1,0:T(8,128)S(1)}, f32[64,1024]{1,0:T(8,128)}, u32[]{:S(2)}, u32[]{:S(2)}) collective-permute-start(f32[64,1024]{1,0:T(8,128)S(1)} %get-tuple-element.75), channel_id=1, source_target_pairs={{0,3},{1,0},{2,1},{3,2},{4,7},{5,4},{6,5},{7,6},{8,11},{9,8},{10,9... | collective-permute-start | bytes 786440 | tf_op jit(solution)/shard_map/ppermute | solution.py:616
  453.7 27.7 %collective-permute-start.26 = (f32[72,640]{1,0:T(8,128)}, f32[72,640]{1,0:T(8,128)}, u32[]{:S(2)}, u32[]{:S(2)}) collective-permute-start(f32[72,640]{1,0:T(8,128)} %after.36), channel_id=1, source_target_pairs={{0,2},{1,3},{2,0},{3,1},{4,6},{5,7},{6,4},{7,5},{8,10},{9,11},{10,... | collective-permute-start | bytes 552968 | tf_op jit(solution)/shard_map/ppermute | solution.py:616
  453.7 27.7 %collective-permute-start.27 = (f32[72,640]{1,0:T(8,128)}, f32[72,640]{1,0:T(8,128)S(1)}, u32[]{:S(2)}, u32[]{:S(2)}) collective-permute-start(f32[72,640]{1,0:T(8,128)} %after.37), channel_id=1, source_target_pairs={{0,3},{1,0},{2,1},{3,2},{4,7},{5,4},{6,5},{7,6},{8,11},{9,8},{10,9... | collective-permute-start | bytes 552968 | tf_op jit(solution)/shard_map/ppermute | solution.py:616
  460.4 37.1 %collective-permute-start.24 = (f32[512,512]{1,0:T(8,128)S(1)}, f32[512,512]{1,0:T(8,128)S(1)}, u32[]{:S(2)}, u32[]{:S(2)}) collective-permute-start(f32[512,512]{1,0:T(8,128)S(1)} %get-tuple-element.62), channel_id=1, source_target_pairs={{0,0},{2,1},{4,2},{6,3},{1,4},{3,5},{5,6},{7,7},{8,8},{10,9},{12,1... | collective-permute-start | bytes 3145736 | tf_op jit(solution)/shard_map/ppermute | solution.py:425
  498.5 36.6 %collective-permute-start.28 = (f32[512,512]{1,0:T(8,128)}, f32[512,512]{1,0:T(8,128)S(1)}, u32[]{:S(2)}, u32[]{:S(2)}) collective-permute-start(f32[512,512]{1,0:T(8,128)} %after.38), channel_id=1, source_target_pairs={{2,0},{0,1},{6,2},{4,3},{3,4},{1,5},{7,6},{5,7},{10,8},{8,9},{14,1... | collective-permute-start | bytes 3145736 | tf_op jit(solution)/shard_map/ppermute | solution.py:429
  (119 other events, 848.7 us)
Sparse Core Ops, SparseCore 0:
  44.2 63.6 all-gather.4
  142.9 57.1 all-gather.6
  256.4 75.4 reduce-scatter.2
  335.6 59.6 reduce-scatter.4
